TPU v7x, 512 devices: a whole 4x8x8 slice. The times are simulated.
512 devices in a mesh: inner: 16 (over z_lo, y), blk: 32 (over x, z_hi, core).
Axes of the slice: x: 4, y: 8, z: 8 (z_hi: 4, z_lo: 2; z = z_hi * 2 + z_lo), core: 2. Of those that a mesh axis runs over, the one named last changes fastest.
Arguments:
- image_emb: float32 [12288, 768], P(('inner', 'blk')), may hold values from -150 to 150
- text_emb: float32 [12288, 768], P(('inner', 'blk')), may hold values from -150 to 150
- logit_scale: float32 [1], replicated, may hold values from 30 to 100
Outputs:
- mean_loss: float32 [1], replicated
- image_grad: float32 [12288, 768], P(('inner', 'blk'))
- text_grad: float32 [12288, 768], P(('inner', 'blk'))
All inputs are finite; a program needn't handle non-finite values.
Results may differ from a plain program's by a relative error of at most 0.006.
Values may be sent and summed in bfloat16 or wider, within the bound.
No kernel may reach another device: no remote copies, remote signals or barrier semaphores. Data moves between devices by JAX's collectives and lax.ppermute only.
A program may use at most 64 MiB of HBM per device.

v0:
```python
import jax
import jax.numpy as jnp
from jax import lax
from jax.sharding import Mesh
from jax.sharding import PartitionSpec as P

BLK = ("blk_0", "blk_1", "blk_2")
INNER = ("inner_0", "inner_1")
INNER_BLK = ("inner_0", "inner_1", "blk_0", "blk_1", "blk_2")


EPSILON = 1e-06


def sent_to_all(x, axis):
    copies = jnp.broadcast_to(x, (lax.axis_size(axis), *x.shape))
    return lax.all_to_all(copies, axis, split_axis=0, concat_axis=0, tiled=True)


def in_order(blocks, dim):
    dims = list(blocks.shape[1:])
    dims[dim] *= blocks.shape[0]
    return jnp.moveaxis(blocks, 0, dim).reshape(dims)


def gather_directly(x, axis, dim):
    blocks = sent_to_all(x, axis)
    return in_order(blocks, dim)


def all_in_one(x, axis):
    leaves = jax.tree.leaves(x)
    turns = sorted(range(len(leaves)), key=lambda k: -leaves[k].size)
    width = (1, *leaves[turns[0]].shape)[-1]
    lines = [
        jnp.pad(leaves[k].reshape(-1), (0, -leaves[k].size % width)).reshape(-1, width)
        for k in turns
    ]
    both, at, found = (sent_to_all(jnp.concatenate(lines), axis), 0, {})
    for k, line in zip(turns, lines):
        slab = both[:, at : at + len(line)].reshape(len(both), -1)
        found[k] = slab[:, : leaves[k].size].reshape(-1, *leaves[k].shape)
        at += len(line)
    numbers = iter(range(len(leaves)))
    return jax.tree.map(lambda _: found[next(numbers)], x)


def joined_by_halves(pieces, combine):
    while len(jax.tree.leaves(pieces)[0]) > 1:
        pieces = jax.vmap(combine)(
            *(jax.tree.map(lambda part: part[side::2], pieces) for side in (0, 1))
        )
    return jax.tree.map(lambda part: part[0], pieces)


def combined_all(x, axis, combine):
    pieces = all_in_one(x, axis)
    return joined_by_halves(pieces, combine)


def split_up(x, dim, length):
    before, after = (x.shape[:dim], x.shape[dim + 1 :])
    return jnp.moveaxis(x.reshape(*before, length, -1, *after), dim, 0)


def summed_on_arrival(x, axis, dim):
    length = lax.axis_size(axis)
    blocks = lax.all_to_all(split_up(x, dim, length), axis, 0, 0, tiled=True)
    return jnp.sum(blocks.astype(jnp.float32), axis=0)


def by_axis(x, axes):
    for axis in axes:
        x = lax.psum(x, axis)
    return x


def unit_rows(values):
    inverse = lax.rsqrt(jnp.sum(values * values, axis=1, keepdims=True) + EPSILON)
    return (values * inverse, inverse)


def project(gradient, direction, inverse):
    return (gradient - direction * jnp.sum(gradient * direction, axis=1, keepdims=True)) * inverse


def gather_rows(values, wide_axis):
    if wide_axis:
        return gather_directly(values, BLK, 0)
    return gather_directly(values, INNER, 0)


def combine_stats(former, latter):
    highest = jnp.maximum(former[0], latter[0])
    summed = former[1] * jnp.exp(former[0] - highest) + latter[1] * jnp.exp(latter[0] - highest)
    return (highest, summed)


def merge_stats(peaks, totals, wide_axis):
    if wide_axis:
        peaks, totals = combined_all((peaks, totals), BLK, combine_stats)
    else:
        peaks, totals = combined_all((peaks, totals), INNER, combine_stats)
    return peaks + jnp.log(totals)


def reduce_rows(partial_value, wide_axis):
    if wide_axis:
        return summed_on_arrival(partial_value.astype(jnp.bfloat16), BLK, 0)
    return summed_on_arrival(partial_value.astype(jnp.bfloat16), INNER, 0)


def own_index(wide_axis):
    if wide_axis:
        return lax.axis_index(BLK)
    return lax.axis_index(INNER)


def on_device(image_emb, text_emb, logit_scale):
    own_rows, embed_width = image_emb.shape
    factor = logit_scale[0]
    image_unit, image_inverse = unit_rows(image_emb)
    text_unit, text_inverse = unit_rows(text_emb)
    image_half = image_unit.astype(jnp.bfloat16)
    text_half = text_unit.astype(jnp.bfloat16)
    image_group = gather_rows(image_half, False)
    text_group = gather_rows(text_half, True)
    image_count = image_group.shape[0]
    text_count = text_group.shape[0]
    pieces = max(1, text_count // 128)
    text_blocks = text_group.reshape(pieces, text_count // pieces, embed_width)
    contract_last = (((1,), (1,)), ((), ()))
    contract_first = (((0,), (0,)), ((), ()))

    def scores(text_block):
        return factor * lax.dot_general(
            image_group, text_block, contract_last, preferred_element_type=jnp.float32
        )

    def first_pass(state, text_block):
        row_peak, row_total = state
        logits = scores(text_block)
        new_peak = jnp.maximum(row_peak, jnp.max(logits, axis=1))
        row_total = row_total * jnp.exp(row_peak - new_peak) + jnp.sum(
            jnp.exp(logits - new_peak[:, None]), axis=1
        )
        col_peak = jnp.max(logits, axis=0)
        col_total = jnp.sum(jnp.exp(logits - col_peak[None, :]), axis=0)
        return ((new_peak, row_total), (col_peak, col_total))

    initial = (jnp.full((image_count,), -1e30, jnp.float32), jnp.zeros((image_count,), jnp.float32))
    (row_peak, row_total), (col_peak, col_total) = lax.scan(first_pass, initial, text_blocks)
    row_lse = merge_stats(row_peak, row_total, False)
    col_lse = merge_stats(col_peak.reshape(text_count), col_total.reshape(text_count), True)
    half_factor = 0.5 * factor

    def make_weights(text_block, col_block):
        logits = scores(text_block)
        return (
            half_factor
            * (jnp.exp(logits - row_lse[:, None]) + jnp.exp(logits - col_block[None, :]))
        ).astype(jnp.bfloat16)

    col_blocks = col_lse.reshape(pieces, text_count // pieces)
    empty = jnp.zeros((image_count, embed_width), jnp.float32)

    def second_pass(image_acc, inputs):
        text_block, col_block = inputs
        weights = make_weights(text_block, col_block)
        image_acc = image_acc + jnp.dot(weights, text_block, preferred_element_type=jnp.float32)
        text_part = lax.dot_general(
            weights, image_group, contract_first, preferred_element_type=jnp.float32
        )
        return (image_acc, text_part)

    image_partial, text_parts = lax.scan(second_pass, empty, (text_blocks, col_blocks))
    text_sum = reduce_rows(text_parts.reshape(text_count, embed_width), True)
    image_sum = reduce_rows(image_partial, False)
    diagonal = factor * jnp.sum(
        image_half.astype(jnp.float32) * text_half.astype(jnp.float32), axis=1
    )
    row_own = lax.dynamic_slice_in_dim(row_lse, own_index(False) * own_rows, own_rows)
    col_own = lax.dynamic_slice_in_dim(col_lse, own_index(True) * own_rows, own_rows)
    share = jnp.sum(row_own - diagonal) + jnp.sum(col_own - diagonal)
    whole_count = own_rows * lax.axis_size(INNER) * lax.axis_size(BLK)
    mean_loss = (by_axis(share, INNER_BLK) / (2.0 * whole_count)).reshape(1)
    image_pull = image_sum - factor * text_half.astype(jnp.float32)
    text_pull = text_sum - factor * image_half.astype(jnp.float32)
    image_grad = project(image_pull, image_unit, image_inverse)
    text_grad = project(text_pull, text_unit, text_inverse)
    return (mean_loss, image_grad, text_grad)


def solution(mesh):
    split = Mesh(
        mesh.devices.reshape(2, 8, 4, 4, 2), ("inner_0", "inner_1", "blk_0", "blk_1", "blk_2")
    )
    in_specs = (P(INNER_BLK, None), P(INNER_BLK, None), P())
    out_specs = (P(), P(INNER_BLK, None), P(INNER_BLK, None))
    return jax.shard_map(
        on_device, mesh=split, in_specs=in_specs, out_specs=out_specs, check_vma=False
    )
```

profile of v0, /device:TPU:1, one launch (start us, length us, event | category | flops | bytes accessed | tf_op | source)
XLA Modules:
  0.0 240.1 jit_solution(7228179052295470135)
XLA Ops:
  0.6 1.0 multiply_reduce_fusion.2
  1.7 1.0 multiply_convert_fusion.1
  2.6 0.8 broadcast_in_dim.46
  3.5 9.6 %all-to-all-start.1 = ((bf16[16,24,768]{2,1,0:T(8,128)(2,1)}), bf16[16,24,768]{2,1,0:T(8,128)(2,1)S(1)}, u32[]{:S(2)}, u32[]{:S(2)}) async-start(bf16[16,24,768]{2,1,0:T(8,128)(2,1)} %broadcast_in_dim.46), calls=%async_computation.1 | async-start | bytes 1179648 | tf_op jit(solution)/shard_map/all_to_all | solution.py:17
  13.1 0.1 multiply_reduce_fusion.3
  13.2 0.1 multiply_convert_fusion.2
  13.3 14.8 %all-to-all-done.1 = bf16[16,24,768]{2,1,0:T(8,128)(2,1)S(1)} async-done(((bf16[16,24,768]{2,1,0:T(8,128)(2,1)}), bf16[16,24,768]{2,1,0:T(8,128)(2,1)S(1)}, u32[]{:S(2)}, u32[]{:S(2)}) %all-to-all-start.1) | async-done | bytes 589856 | tf_op jit(solution)/shard_map/all_to_all | solution.py:17
  28.1 1.1 broadcast_in_dim.45
  29.3 14.8 %all-to-all-start = ((bf16[32,24,768]{2,1,0:T(8,128)(2,1)}), bf16[32,24,768]{2,1,0:T(8,128)(2,1)S(1)}, u32[]{:S(2)}, u32[]{:S(2)}) async-start(bf16[32,24,768]{2,1,0:T(8,128)(2,1)} %broadcast_in_dim.45), calls=%async_computation | async-start | bytes 2359296 | tf_op jit(solution)/shard_map/all_to_all | solution.py:17
  44.8 30.6 %all-to-all-done = bf16[32,24,768]{2,1,0:T(8,128)(2,1)S(1)} async-done(((bf16[32,24,768]{2,1,0:T(8,128)(2,1)}), bf16[32,24,768]{2,1,0:T(8,128)(2,1)S(1)}, u32[]{:S(2)}, u32[]{:S(2)}) %all-to-all-start) | async-done | bytes 1179680 | tf_op jit(solution)/shard_map/all_to_all | solution.py:17
  75.3 8.2 %while.30 = (s32[]{:T(128)}, f32[384]{0:T(512)S(1)}, f32[384]{0:T(512)S(1)}, f32[6,128]{1,0:T(8,128)S(1)}, f32[6,128]{1,0:T(8,128)S(1)}, /*index=5*/f32[]{:T(128...) while((s32[]{:T(128)}, f32[384]{0:T(512)S(1)}, ...), condition=%wide.region_7.8_spmd.clone, body=%wide.region_2.7_spmd.clone.sunk | while | flops 75843200 | bytes 1203328 | solution.py:152
  75.3 1.1 fusion.45
  76.4 0.2 exponential_reduce_fusion.3
  76.7 1.1 fusion.45
  77.8 0.2 exponential_reduce_fusion.3
  78.1 1.1 fusion.45
  79.2 0.2 exponential_reduce_fusion.3
  79.5 1.1 fusion.45
  80.5 0.2 exponential_reduce_fusion.3
  80.8 1.1 fusion.45
  81.9 0.2 exponential_reduce_fusion.3
  82.2 1.1 fusion.45
  83.3 0.2 exponential_reduce_fusion.3
  83.6 0.6 broadcast_in_dim.47
  84.3 5.6 %all-to-all-start.2 = ((f32[16,2,384]{2,1,0:T(2,128)}), f32[16,2,384]{2,1,0:T(2,128)S(1)}, u32[]{:S(2)}, u32[]{:S(2)}) async-start(f32[16,2,384]{2,1,0:T(2,128)} %broadcast_in_dim.47), calls=%async_computation.2 | async-start | bytes 98304 | tf_op jit(solution)/shard_map/all_to_all | solution.py:17
  89.9 7.3 %all-to-all-done.2 = f32[16,2,384]{2,1,0:T(2,128)S(1)} async-done(((f32[16,2,384]{2,1,0:T(2,128)}), f32[16,2,384]{2,1,0:T(2,128)S(1)}, u32[]{:S(2)}, u32[]{:S(2)}) %all-to-all-start.2) | async-done | bytes 49184 | tf_op jit(solution)/shard_map/all_to_all | solution.py:17
  97.2 0.7 broadcast_in_dim.48
  98.0 6.0 %all-to-all-start.3 = ((f32[32,2,768]{2,1,0:T(2,128)}), f32[32,2,768]{2,1,0:T(2,128)S(1)}, u32[]{:S(2)}, u32[]{:S(2)}) async-start(f32[32,2,768]{2,1,0:T(2,128)} %broadcast_in_dim.48), calls=%async_computation.3 | async-start | bytes 393216 | tf_op jit(solution)/shard_map/all_to_all | solution.py:17
  104.4 11.3 %all-to-all-done.3 = f32[32,2,768]{2,1,0:T(2,128)S(1)} async-done(((f32[32,2,768]{2,1,0:T(2,128)}), f32[32,2,768]{2,1,0:T(2,128)S(1)}, u32[]{:S(2)}, u32[]{:S(2)}) %all-to-all-start.3) | async-done | bytes 196640 | tf_op jit(solution)/shard_map/all_to_all | solution.py:17
  115.8 0.2 fusion.26
  116.5 14.9 %while.31 = (s32[]{:T(128)}, f32[384,768]{1,0:T(8,128)S(1)}, bf16[6,128,768]{2,1,0:T(8,128)(2,1)}, f32[]{:T(128)}, f32[]{:T(128)}, /*index=5*/bf16[6,128,768]{2,...) while((s32[]{:T(128)}, f32[384,768]{1,0:T(8,128)S(1)}, ...), condition=%wide.region_17.18_spmd.clone, body=%wide.region_16.17_spmd.clone.sunk | while | flops 227377152 | bytes 4624523 | solution.py:176
  116.5 1.0 multiply_convert_fusion.4
  117.5 0.5 convolution_add_fusion.2
  118.0 0.9 fusion.54
  119.0 1.0 multiply_convert_fusion.4
  120.0 0.5 convolution_add_fusion.2
  120.5 0.9 fusion.54
  121.5 1.0 multiply_convert_fusion.4
  122.5 0.5 convolution_add_fusion.2
  123.0 0.9 fusion.54
  123.9 1.0 multiply_convert_fusion.4
  124.9 0.5 convolution_add_fusion.2
  125.5 0.9 fusion.54
  126.4 1.0 multiply_convert_fusion.4
  127.4 0.5 convolution_add_fusion.2
  127.9 0.9 fusion.54
  128.9 1.0 multiply_convert_fusion.4
  129.9 0.5 convolution_add_fusion.2
  130.4 0.9 fusion.54
  131.4 0.1 convert_element_type.37
  131.4 20.4 %all_to_all.30 = bf16[16,24,768]{2,1,0:T(8,128)(2,1)S(1)} all-to-all(bf16[16,24,768]{2,1,0:T(8,128)(2,1)S(1)} %bitcast.92), channel_id=1, replica_groups=mesh['inner_0'=2,'inner_1'=8,'blk_0'=4,'blk_1'=4,'blk_2'=2] {'inner_0','..., dimensions={0} | all-to-all | bytes 1179648 | tf_op jit(solution)/shard_map/all_to_all | solution.py:68
  151.8 5.9 %all-to-all-start.5 = ((bf16[32,24,768]{2,1,0:T(8,128)(2,1)}), bf16[32,24,768]{2,1,0:T(8,128)(2,1)S(1)}, u32[]{:S(2)}, u32[]{:S(2)}) async-start(bf16[32,24,768]{2,1,0:T(8,128)(2,1)} %bitcast.9), calls=%async_computation.5 | async-start | bytes 2359296 | tf_op jit(solution)/shard_map/all_to_all | solution.py:68
  157.7 0.0 copy-start.1
  157.8 0.1 convert_reduce_fusion.1
  157.9 31.1 %all-to-all-done.5 = bf16[32,24,768]{2,1,0:T(8,128)(2,1)S(1)} async-done(((bf16[32,24,768]{2,1,0:T(8,128)(2,1)}), bf16[32,24,768]{2,1,0:T(8,128)(2,1)S(1)}, u32[]{:S(2)}, u32[]{:S(2)}) %all-to-all-start.5) | async-done | bytes 1179680 | tf_op jit(solution)/shard_map/all_to_all | solution.py:68
  189.0 0.2 convert_reduce_fusion
  189.1 0.2 multiply_reduce_fusion
  189.4 0.7 fusion.21
  191.4 4.3 %psum.35 = f32[]{:T(128)} all-reduce(f32[]{:T(128)S(6)} %add.121), channel_id=1, replica_groups=mesh['inner_0'=2,'inner_1'=8,'blk_0'=4,'blk_1'=4,'blk_2'=2] {'inner_0'}, use_global_device_ids=true, to_apply=%region_11.12 | all-reduce | flops 1 | bytes 8 | tf_op jit(solution)/shard_map/psum | solution.py:74
  195.7 12.1 %psum.36 = f32[]{:T(128)} all-reduce(f32[]{:T(128)} %psum.35), channel_id=1, replica_groups=mesh['inner_0'=2,'inner_1'=8,'blk_0'=4,'blk_1'=4,'blk_2'=2] {'inner_1'}, use_global_device_ids=true, to_apply=%region_12.13 | all-reduce | flops 1 | bytes 8 | tf_op jit(solution)/shard_map/psum | solution.py:74
  207.8 7.9 %psum.37 = f32[]{:T(128)} all-reduce(f32[]{:T(128)} %psum.36), channel_id=1, replica_groups=mesh['inner_0'=2,'inner_1'=8,'blk_0'=4,'blk_1'=4,'blk_2'=2] {'blk_0'}, use_global_device_ids=true, to_apply=%region_13.14 | all-reduce | flops 1 | bytes 8 | tf_op jit(solution)/shard_map/psum | solution.py:74
  215.7 9.7 %psum.38 = f32[]{:T(128)} all-reduce(f32[]{:T(128)} %psum.37), channel_id=1, replica_groups=mesh['inner_0'=2,'inner_1'=8,'blk_0'=4,'blk_1'=4,'blk_2'=2] {'blk_1'}, use_global_device_ids=true, to_apply=%region_14.15 | all-reduce | flops 1 | bytes 8 | tf_op jit(solution)/shard_map/psum | solution.py:74
  225.4 12.2 %psum.39 = f32[]{:T(128)} all-reduce(f32[]{:T(128)} %psum.38), channel_id=1, replica_groups=mesh['inner_0'=2,'inner_1'=8,'blk_0'=4,'blk_1'=4,'blk_2'=2] {'blk_2'}, use_global_device_ids=true, to_apply=%region_15.16 | all-reduce | flops 1 | bytes 8 | tf_op jit(solution)/shard_map/psum | solution.py:74
  238.2 0.8 subtract_multiply_fusion
  (95 shorter events, 1.5 us)
Async XLA Ops:
  0.6 12.4 %copy-start = (f32[24,768]{1,0:T(8,128)S(1)}, f32[24,768]{1,0:T(8,128)}, u32[]{:S(2)}) copy-start(f32[24,768]{1,0:T(8,128)} %param.8) | copy-start | bytes 221188
  3.5 24.6 %all-to-all-start.1 = ((bf16[16,24,768]{2,1,0:T(8,128)(2,1)}), bf16[16,24,768]{2,1,0:T(8,128)(2,1)S(1)}, u32[]{:S(2)}, u32[]{:S(2)}) async-start(bf16[16,24,768]{2,1,0:T(8,128)(2,1)} %broadcast_in_dim.46), calls=%async_computation.1 | async-start | bytes 1179648 | tf_op jit(solution)/shard_map/all_to_all | solution.py:17
  29.3 46.1 %all-to-all-start = ((bf16[32,24,768]{2,1,0:T(8,128)(2,1)}), bf16[32,24,768]{2,1,0:T(8,128)(2,1)S(1)}, u32[]{:S(2)}, u32[]{:S(2)}) async-start(bf16[32,24,768]{2,1,0:T(8,128)(2,1)} %broadcast_in_dim.45), calls=%async_computation | async-start | bytes 2359296 | tf_op jit(solution)/shard_map/all_to_all | solution.py:17
  84.3 13.0 %all-to-all-start.2 = ((f32[16,2,384]{2,1,0:T(2,128)}), f32[16,2,384]{2,1,0:T(2,128)S(1)}, u32[]{:S(2)}, u32[]{:S(2)}) async-start(f32[16,2,384]{2,1,0:T(2,128)} %broadcast_in_dim.47), calls=%async_computation.2 | async-start | bytes 98304 | tf_op jit(solution)/shard_map/all_to_all | solution.py:17
  98.0 17.8 %all-to-all-start.3 = ((f32[32,2,768]{2,1,0:T(2,128)}), f32[32,2,768]{2,1,0:T(2,128)S(1)}, u32[]{:S(2)}, u32[]{:S(2)}) async-start(f32[32,2,768]{2,1,0:T(2,128)} %broadcast_in_dim.48), calls=%async_computation.3 | async-start | bytes 393216 | tf_op jit(solution)/shard_map/all_to_all | solution.py:17
  151.8 37.2 %all-to-all-start.5 = ((bf16[32,24,768]{2,1,0:T(8,128)(2,1)}), bf16[32,24,768]{2,1,0:T(8,128)(2,1)S(1)}, u32[]{:S(2)}, u32[]{:S(2)}) async-start(bf16[32,24,768]{2,1,0:T(8,128)(2,1)} %bitcast.9), calls=%async_computation.5 | async-start | bytes 2359296 | tf_op jit(solution)/shard_map/all_to_all | solution.py:68
  157.7 31.4 %copy-start.1 = (f32[24,768]{1,0:T(8,128)S(1)}, f32[24,768]{1,0:T(8,128)}, u32[]{:S(2)}) copy-start(f32[24,768]{1,0:T(8,128)} %param.7) | copy-start | bytes 221188
where the time goes:
time: 241 us; the launch traced here: 240 us
  waiting for transfers between devices  95.2 us (40%)
  blocking collectives  66.6 us (28%)
  starting transfers between devices  41.9 us (17%)
  matrix products  21 us (9%)
  other arithmetic  5.69 us (2%)
  between operations  4.68 us (2%)
  local copies, waits for them, and re-layouts  4.64 us (2%)
    all_to_all x4, waiting for transfers between devices, sent_to_all(): return lax.all_to_all(copies, axis, split_axis=0, concat_axis=0, tiled=True)  64.1 us
    psum x5, blocking collectives, by_axis(): x = lax.psum(x, axis)  46.2 us
    all_to_all x4, starting transfers between devices, sent_to_all(): return lax.all_to_all(copies, axis, split_axis=0, concat_axis=0, tiled=True)  36 us
    all_to_all x1, waiting for transfers between devices, summed_on_arrival(): blocks = lax.all_to_all(split_up(x, dim, length), axis, 0, 0, tiled=True)  31.1 us
    all_to_all x1, blocking collectives, summed_on_arrival(): blocks = lax.all_to_all(split_up(x, dim, length), axis, 0, 0, tiled=True)  20.4 us
    dot_general x12, matrix products, scores(): lax.dot_general(image_group, text_block, contract_last, preferred_element...  12.3 us
    all_to_all x1, starting transfers between devices, summed_on_arrival(): blocks = lax.all_to_all(split_up(x, dim, length), axis, 0, 0, tiled=True)  5.93 us
    dot_general x6, matrix products, second_pass(): lax.dot_general(weights, image_group, contract_first, preferred_element_t...  5.64 us
  transfers between devices with their start and end apart: 5, of which 5 were waited for; matrix products, arithmetic and copies ran while one was open for 0% of the time, Pallas kernels for 0%

commit v1 on v0

v1 whole, which is shorter than its diff:
```python
import functools

import jax
import jax.numpy as jnp
from jax import lax
from jax.experimental import pallas as pl
from jax.experimental.pallas import tpu as pltpu
from jax.sharding import Mesh
from jax.sharding import PartitionSpec as P

INNER = ("z0", "y2", "y1", "y0")
CHIPS = ("x", "zh")
CORE = "c"
BLK = ("x", "zh", "c")
ALL = ("z0", "y2", "y1", "y0", "x", "zh", "c")

EPSILON = 1e-06
LAST = (((1,), (1,)), ((), ()))
FIRST = (((0,), (0,)), ((), ()))
VMEM_LIMIT = 48 * 1024 * 1024


def f32_dot(a, b, dims):
    return lax.dot_general(a, b, dims, preferred_element_type=jnp.float32)


def unit_rows(values):
    inverse = lax.rsqrt(jnp.sum(values * values, axis=1, keepdims=True) + EPSILON)
    return values * inverse, inverse


def kernel_call(body, out_shape, *args, flops=0):
    in_specs = [
        pl.BlockSpec(memory_space=pltpu.SMEM if a.size == 1 else pltpu.VMEM) for a in args
    ]
    outs = jax.tree.leaves(out_shape)
    moved = sum(a.size * a.dtype.itemsize for a in (*args, *outs))
    return pl.pallas_call(
        body,
        out_shape=out_shape,
        in_specs=in_specs,
        compiler_params=pltpu.CompilerParams(vmem_limit_bytes=VMEM_LIMIT),
        cost_estimate=pl.CostEstimate(flops=flops, bytes_accessed=moved, transcendentals=0),
    )(*args)


def units_kernel(values_ref, copies_ref):
    unit, _ = unit_rows(values_ref[...])
    half = jnp.concatenate([unit, unit], axis=0).astype(jnp.bfloat16)
    rows = half.shape[0]
    for k in range(copies_ref.shape[0] // rows):
        copies_ref[k * rows : (k + 1) * rows, :] = half


def units_and_diagonal_kernel(values_ref, other_ref, copies_ref, diagonal_ref):
    units_kernel(values_ref, copies_ref)
    first = unit_rows(values_ref[...])[0].astype(jnp.bfloat16).astype(jnp.float32)
    second = unit_rows(other_ref[...])[0].astype(jnp.bfloat16).astype(jnp.float32)
    diagonal_ref[...] = jnp.broadcast_to(jnp.sum(first * second), diagonal_ref.shape)


def lines(row):
    return [row[:, k * 128 : (k + 1) * 128] for k in range(row.shape[1] // 128)]


def lse_of(parts):
    peak = functools.reduce(jnp.maximum, [jnp.max(p, axis=0, keepdims=True) for p in parts])
    total = sum(jnp.sum(jnp.exp(p - peak), axis=0, keepdims=True) for p in parts)
    return peak + jnp.log(total)


def stats_kernel(factor_ref, core_ref, image_ref, own_ref, other_ref, diagonal_ref, row_ref, col_ref):
    factor = factor_ref[0]
    image, own, other = image_ref[...], own_ref[...], other_ref[...]
    own_lse = lse_of([factor * f32_dot(image, own, LAST)])
    other_lse = lse_of([factor * f32_dot(image, other, LAST)])
    row_lse = lse_of([factor * f32_dot(own, image, LAST), factor * f32_dot(other, image, LAST)])
    zero = jnp.zeros((1, 128), jnp.float32)
    rows = lines(row_lse)
    diagonal = factor * diagonal_ref[0:1, :]
    message = jnp.concatenate([*rows, diagonal, *[zero] * (7 - len(rows))], axis=0)
    row_ref[...] = jnp.broadcast_to(message[None], row_ref.shape)
    first_core = core_ref[0] == 0
    cols = lines(jnp.where(first_core, own_lse, other_lse)) + lines(
        jnp.where(first_core, other_lse, own_lse)
    )
    col_ref[...] = jnp.concatenate([*cols, *[zero] * (8 - len(cols))], axis=0)


def pieces_lse(pieces):
    peak = jnp.max(pieces, axis=0)
    return peak + jnp.log(jnp.sum(jnp.exp(pieces - peak[None]), axis=0))


def middle_kernel(pieces_ref, col_ref, row_ref, message_ref):
    pieces = pieces_ref[...]
    lse = pieces_lse(pieces)
    diagonal = jnp.sum(pieces[:, 3:4, 0:1])
    share = jnp.sum(lse[0:3, :]) - 2.0 * diagonal
    row_ref[...] = lse
    place = lax.broadcasted_iota(jnp.int32, (8, 128), 0)
    message = jnp.where(place == 6, share, col_ref[...])
    message_ref[...] = jnp.broadcast_to(message[None], message_ref.shape)


def weights_kernel(
    factor_ref, core_ref, image_ref, own_ref, other_ref, row_ref, pieces_ref,
    image_out, own_out, other_out, share_ref,
):
    factor = factor_ref[0]
    pieces = pieces_ref[...]
    cols = pieces_lse(pieces)
    share_ref[0:8, :] = jnp.broadcast_to(jnp.sum(cols[0:6, :]), (8, 128))
    share_ref[8:16, :] = jnp.broadcast_to(jnp.sum(pieces[:, 6:7, 0:1]), (8, 128))
    core0 = jnp.concatenate([cols[k : k + 1, :] for k in range(3)], axis=1)
    core1 = jnp.concatenate([cols[k : k + 1, :] for k in range(3, 6)], axis=1)
    first_core = core_ref[0] == 0
    row_lse = jnp.concatenate(
        [jnp.transpose(jnp.broadcast_to(row_ref[k : k + 1, :], (128, 128))) for k in range(3)],
        axis=0,
    )[:, 0:1]
    image = image_ref[...]
    image_sum = None
    for mine, text_ref in ((True, own_ref), (False, other_ref)):
        text = text_ref[...]
        col_lse = jnp.where(first_core == mine, core0, core1)
        logits = factor * f32_dot(image, text, LAST)
        weights = (
            (0.5 * factor) * (jnp.exp(logits - row_lse) + jnp.exp(logits - col_lse))
        ).astype(jnp.bfloat16)
        part = jnp.dot(weights, text, preferred_element_type=jnp.float32)
        image_sum = part if image_sum is None else image_sum + part
        text_sum = f32_dot(weights, image, FIRST)
        if mine:
            own_out[...] = text_sum
        else:
            other_out[...] = text_sum.astype(jnp.bfloat16)
    image_out[...] = image_sum.astype(jnp.bfloat16)


def gradient_kernel(factor_ref, values_ref, paired_ref, pieces_ref, gradient_ref):
    unit, inverse = unit_rows(values_ref[...])
    paired = unit_rows(paired_ref[...])[0].astype(jnp.bfloat16).astype(jnp.float32)
    rows = unit.shape[0]
    total = None
    for k in range(pieces_ref.shape[0] // (2 * rows)):
        both = pieces_ref[2 * rows * k : 2 * rows * (k + 1), :].astype(jnp.float32)
        both = both[:rows] + both[rows:]
        total = both if total is None else total + both
    pull = total - factor_ref[0] * paired
    gradient_ref[...] = (pull - unit * jnp.sum(pull * unit, axis=1, keepdims=True)) * inverse


def exchanged(blocks, axis):
    count = lax.axis_size(axis)
    split = blocks.reshape(count, -1, *blocks.shape[1:])
    return lax.all_to_all(split, axis, split_axis=0, concat_axis=0, tiled=True).reshape(blocks.shape)


def swapped(x, axis):
    return lax.ppermute(x, axis, [(0, 1), (1, 0)])


def shape(dims, dtype):
    return jax.ShapeDtypeStruct(dims, dtype)


def on_device(image_emb, text_emb, factor):
    own_rows, width = image_emb.shape
    inner, chips, blk = (lax.axis_size(a) for a in (INNER, CHIPS, BLK))
    core = lax.axis_index(CORE).astype(jnp.int32).reshape(1)
    bf16, f32 = jnp.bfloat16, jnp.float32
    image_rows, text_rows = own_rows * inner, own_rows * chips
    work = 2 * image_rows * text_rows * width

    text_copies = kernel_call(units_kernel, shape((text_rows, width), bf16), text_emb)
    text_own = exchanged(text_copies, CHIPS)
    text_other = swapped(text_own, CORE)
    image_copies, diagonal = kernel_call(
        units_and_diagonal_kernel,
        (shape((image_rows, width), bf16), shape((8, 128), f32)),
        image_emb,
        text_emb,
    )
    image_copies, _ = lax.optimization_barrier((image_copies, text_own))
    image_group = exchanged(image_copies, INNER)

    row_message, col_part = kernel_call(
        stats_kernel,
        (shape((inner, 8, 128), f32), shape((8, 128), f32)),
        factor, core, image_group, text_own, text_other, diagonal,
        flops=4 * work,
    )
    row_pieces = exchanged(row_message, INNER)
    row_lse, col_message = kernel_call(
        middle_kernel, (shape((8, 128), f32), shape((blk, 8, 128), f32)), row_pieces, col_part
    )
    col_pieces = exchanged(col_message, BLK)

    image_part, own_part, other_part, shares = kernel_call(
        weights_kernel,
        (
            shape((image_rows, width), bf16),
            shape((text_rows, width), f32),
            shape((text_rows, width), bf16),
            shape((16, 128), f32),
        ),
        factor, core, image_group, text_own, text_other, row_lse, col_pieces,
        flops=6 * work,
    )
    swapped_part = swapped(other_part, CORE)
    image_pieces = exchanged(image_part, INNER)
    text_part = (own_part + swapped_part.astype(f32)).astype(bf16)
    text_part, _ = lax.optimization_barrier((text_part, image_pieces))
    text_pieces = exchanged(text_part, CHIPS)

    col_share = shares[0:8]
    for axis in INNER:
        col_share = col_share + swapped(col_share, axis)
    whole = 2.0 * own_rows * inner * blk
    mean_loss = ((col_share[0, 0] + shares[8, 0]) / whole).reshape(1)

    out = shape((own_rows, width), f32)
    image_grad = kernel_call(gradient_kernel, out, factor, image_emb, text_emb, image_pieces)
    text_grad = kernel_call(gradient_kernel, out, factor, text_emb, image_emb, text_pieces)
    return (mean_loss, image_grad, text_grad)


def solution(mesh):
    split = Mesh(mesh.devices.reshape(2, 2, 2, 2, 4, 4, 2), ALL)
    in_specs = (P(ALL, None), P(ALL, None), P())
    out_specs = (P(), P(ALL, None), P(ALL, None))
    return jax.shard_map(
        on_device, mesh=split, in_specs=in_specs, out_specs=out_specs, check_vma=False
    )
```

time: 241 us -> 159 us (0.66)
  the two profiles are of different devices: /device:TPU:1 before, /device:TPU:10 now
where the time goes in v1:
time: 159 us; the launch traced here: 158 us
  waiting for transfers between devices  65 us (41%)
  starting transfers between devices  48.5 us (31%)
  blocking collectives  28.9 us (18%)
  Pallas kernels  8.5 us (5%)
  between operations  3.82 us (2%)
  local copies, waits for them, and re-layouts  2.75 us (2%)
    all_to_all x4, waiting for transfers between devices, exchanged(): lax.all_to_all(split, axis, split_axis=0, concat_axis=0, tiled=True)  42 us
    all_to_all x4, starting transfers between devices, exchanged(): lax.all_to_all(split, axis, split_axis=0, concat_axis=0, tiled=True)  30.5 us
    all_to_all x2, blocking collectives, exchanged(): lax.all_to_all(split, axis, split_axis=0, concat_axis=0, tiled=True)  28.9 us
    ppermute x6, waiting for transfers between devices, swapped(): return lax.ppermute(x, axis, [(0, 1), (1, 0)])  23 us
    ppermute x6, starting transfers between devices, swapped(): return lax.ppermute(x, axis, [(0, 1), (1, 0)])  18.1 us
    pallas_call x7, Pallas kernels, kernel_call(): pl.pallas_call(body, out_shape=out_shape, in_specs=in_specs, compiler_par...  8.5 us
  transfers between devices with their start and end apart: 10, of which 9 were waited for; matrix products, arithmetic and copies ran while one was open for 1% of the time, Pallas kernels for 1%

profile of v1, /device:TPU:10, one launch (start us, length us, event | category | flops | bytes accessed | tf_op | source)
XLA Modules:
  0.0 158.5 jit_solution(2889994049994650783)
XLA Ops:
  0.6 0.0 copy-start
  0.6 0.9 copy-done
  1.5 0.0 copy-start.1
  1.5 0.0 copy-start.2
  1.5 1.0 shard_map.59
  2.5 13.3 %all-to-all-start = ((bf16[16,24,768]{2,1,0:T(8,128)(2,1)}), bf16[16,24,768]{2,1,0:T(8,128)(2,1)S(1)}, u32[]{:S(2)}, u32[]{:S(2)}) async-start(bf16[16,24,768]{2,1,0:T(8,128)(2,1)} %bitcast.1), calls=%async_computation | async-start | bytes 1179648 | tf_op jit(solution)/shard_map/all_to_all | solution.py:157
  15.8 0.0 copy-done.1
  15.8 0.0 copy-done.2
  15.8 1.0 shard_map.58
  16.8 17.3 %all-to-all-done = bf16[16,24,768]{2,1,0:T(8,128)(2,1)S(1)} async-done(((bf16[16,24,768]{2,1,0:T(8,128)(2,1)}), bf16[16,24,768]{2,1,0:T(8,128)(2,1)S(1)}, u32[]{:S(2)}, u32[]{:S(2)}) %all-to-all-start) | async-done | bytes 589856 | tf_op jit(solution)/shard_map/all_to_all | solution.py:157
  34.1 7.7 %all-to-all-start.1 = ((bf16[16,24,768]{2,1,0:T(8,128)(2,1)}), bf16[16,24,768]{2,1,0:T(8,128)(2,1)S(1)}, u32[]{:S(2)}, u32[]{:S(2)}) async-start(bf16[16,24,768]{2,1,0:T(8,128)(2,1)} %bitcast.3), calls=%async_computation.1 | async-start | bytes 1179648 | tf_op jit(solution)/shard_map/all_to_all | solution.py:157
  41.9 1.9 %collective-permute-start = (bf16[384,768]{1,0:T(8,128)(2,1)S(1)}, bf16[384,768]{1,0:T(8,128)(2,1)S(1)}, u32[]{:S(2)}, u32[]{:S(2)}) collective-permute-start(bf16[384,768]{1,0:T(8,128)(2,1)S(1)} %bitcast.20), channel_id=1, source_target_pairs={{0,1},{1,0},{2,3},{3,2},{4,5},{5,4},{6,7},{7,6},{8,9},{9,8},{10,11... | collective-permute-start | bytes 1769480 | tf_op jit(solution)/shard_map/ppermute | solution.py:161
  44.4 1.3 collective-permute-done.other_ref
  45.8 11.8 %all-to-all-done.1 = bf16[16,24,768]{2,1,0:T(8,128)(2,1)S(1)} async-done(((bf16[16,24,768]{2,1,0:T(8,128)(2,1)}), bf16[16,24,768]{2,1,0:T(8,128)(2,1)S(1)}, u32[]{:S(2)}, u32[]{:S(2)}) %all-to-all-start.1) | async-done | bytes 589856 | tf_op jit(solution)/shard_map/all_to_all | solution.py:157
  57.5 1.6 %shard_map.60 = (f32[16,8,128]{2,1,0:T(8,128)S(1)}, f32[8,128]{1,0:T(8,128)S(1)}) custom-call(f32[1]{0:T(128)S(6)} %copy.8.factor_ref, s32[1]{0:T(128)} %bitcast.core_ref, bf16[384,768]{1,0:T(8,128)(2,1)S(1)} %bitcast.23, bf16[384,768]{1,0:T(8,128)(2,1)S(1)} %bitcast.21, bf16[384,768]{1,0:T(8,128)(2,1)S(1)} %collective-permute-done.other_ref, ...), custom_call_target="tpu_custom_call" | custom-call | flops 905969664 | bytes 1843208 | tf_op jit(solution)/shard_map/pallas_call | solution.py:38
  59.1 12.6 %all_to_all.30 = f32[16,1,8,128]{3,2,1,0:T(8,128)S(1)} all-to-all(f32[16,1,8,128]{3,2,1,0:T(8,128)S(1)} %bitcast.28), channel_id=1, replica_groups=mesh['z0'=2,'y2'=2,'y1'=2,'y0'=2,'x'=4,'zh'=4,'c'=2] {'z0','y2','y1','y0'}, dimensions={0} | all-to-all | bytes 131072 | tf_op jit(solution)/shard_map/all_to_all | solution.py:157
  71.8 0.2 shard_map.61
  71.9 16.3 %all_to_all.31 = f32[32,1,8,128]{3,2,1,0:T(8,128)S(1)} all-to-all(f32[32,1,8,128]{3,2,1,0:T(8,128)S(1)} %bitcast.27), channel_id=1, replica_groups=mesh['z0'=2,'y2'=2,'y1'=2,'y0'=2,'x'=4,'zh'=4,'c'=2] {'x','zh','c'}, dimensions={0} | all-to-all | bytes 262144 | tf_op jit(solution)/shard_map/all_to_all | solution.py:157
  88.2 3.1 %shard_map.62 = (bf16[384,768]{1,0:T(8,128)(2,1)}, f32[384,768]{1,0:T(8,128)S(1)}, bf16[384,768]{1,0:T(8,128)(2,1)S(1)}, f32[16,128]{1,0:T(8,128)S(1)}) custom-call(f32[1]{0:T(128)S(6)} %copy.8.factor_ref, s32[1]{0:T(128)} %bitcast.core_ref, bf16[384,768]{1,0:T(8,128)(2,1)S(1)} %bitcast.24, bf16[384,768]{1,0:T(8,128)(2,1)S(1)} %bitcast.22, ...), custom_call_target="tpu_custom_call" | custom-call | flops 1358954496 | bytes 4272136 | tf_op jit(solution)/shard_map/pallas_call | solution.py:38
  91.3 0.0 copy-start.3
  91.3 0.8 copy-done.3
  92.1 0.0 copy-start.4
  92.1 4.5 %all-to-all-start.4 = ((bf16[16,24,768]{2,1,0:T(8,128)(2,1)}), bf16[16,24,768]{2,1,0:T(8,128)(2,1)S(1)}, u32[]{:S(2)}, u32[]{:S(2)}) async-start(bf16[16,24,768]{2,1,0:T(8,128)(2,1)} %bitcast.12), calls=%async_computation.4 | async-start | bytes 1179648 | tf_op jit(solution)/shard_map/all_to_all | solution.py:157
  96.7 0.0 copy-done.4
  96.7 2.2 %collective-permute-start.5 = (bf16[384,768]{1,0:T(8,128)(2,1)S(1)}, bf16[384,768]{1,0:T(8,128)(2,1)S(1)}, u32[]{:S(2)}, u32[]{:S(2)}) collective-permute-start(bf16[384,768]{1,0:T(8,128)(2,1)S(1)} %copy-done.4), channel_id=1, source_target_pairs={{0,1},{1,0},{2,3},{3,2},{4,5},{5,4},{6,7},{7,6},{8,9},{9,8},{10,11... | collective-permute-start | bytes 1769480 | tf_op jit(solution)/shard_map/ppermute | solution.py:161
  98.9 1.7 %collective-permute-done.5 = bf16[384,768]{1,0:T(8,128)(2,1)S(1)} collective-permute-done((bf16[384,768]{1,0:T(8,128)(2,1)S(1)}, bf16[384,768]{1,0:T(8,128)(2,1)S(1)}, u32[]{:S(2)}, u32[]{:S(2)}) %collective-permute-start.5) | collective-permute-done | bytes 589856 | tf_op jit(solution)/shard_map/ppermute | solution.py:161
  100.6 0.9 add_convert_fusion
  101.5 12.9 %all-to-all-done.4 = bf16[16,24,768]{2,1,0:T(8,128)(2,1)S(1)} async-done(((bf16[16,24,768]{2,1,0:T(8,128)(2,1)}), bf16[16,24,768]{2,1,0:T(8,128)(2,1)S(1)}, u32[]{:S(2)}, u32[]{:S(2)}) %all-to-all-start.4) | async-done | bytes 589856 | tf_op jit(solution)/shard_map/all_to_all | solution.py:157
  114.4 4.9 %all-to-all-start.5 = ((bf16[16,24,768]{2,1,0:T(8,128)(2,1)}), bf16[16,24,768]{2,1,0:T(8,128)(2,1)S(1)}, u32[]{:S(2)}, u32[]{:S(2)}) async-start(bf16[16,24,768]{2,1,0:T(8,128)(2,1)} %bitcast.14), calls=%async_computation.5 | async-start | bytes 1179648 | tf_op jit(solution)/shard_map/all_to_all | solution.py:157
  119.3 3.4 %collective-permute-start.1 = (f32[8,128]{1,0:T(8,128)S(1)}, f32[8,128]{1,0:T(8,128)S(1)}, u32[]{:S(2)}, u32[]{:S(2)}) collective-permute-start(f32[8,128]{1,0:T(8,128)S(1)} %slice.9), channel_id=1, source_target_pairs={{0,256},{256,0},{1,257},{257,1},{2,258},{258,2},{3,259},{259,3},{4... | collective-permute-start | bytes 12296 | tf_op jit(solution)/shard_map/ppermute | solution.py:161
  122.8 9.8 %collective-permute-done.1 = f32[8,128]{1,0:T(8,128)S(1)} collective-permute-done((f32[8,128]{1,0:T(8,128)S(1)}, f32[8,128]{1,0:T(8,128)S(1)}, u32[]{:S(2)}, u32[]{:S(2)}) %collective-permute-start.1) | collective-permute-done | bytes 4128 | tf_op jit(solution)/shard_map/ppermute | solution.py:161
  132.6 4.7 %collective-permute-start.2 = (f32[8,128]{1,0:T(8,128)S(1)}, f32[8,128]{1,0:T(8,128)S(1)}, u32[]{:S(2)}, u32[]{:S(2)}) collective-permute-start(f32[8,128]{1,0:T(8,128)S(1)} %slice_add_fusion), channel_id=1, source_target_pairs={{0,128},{128,0},{1,129},{129,1},{2,130},{130,2},{3,131},{131,3},{4... | collective-permute-start | bytes 12296 | tf_op jit(solution)/shard_map/ppermute | solution.py:161
  137.3 4.7 %collective-permute-done.2 = f32[8,128]{1,0:T(8,128)S(1)} collective-permute-done((f32[8,128]{1,0:T(8,128)S(1)}, f32[8,128]{1,0:T(8,128)S(1)}, u32[]{:S(2)}, u32[]{:S(2)}) %collective-permute-start.2) | collective-permute-done | bytes 4128 | tf_op jit(solution)/shard_map/ppermute | solution.py:161
  142.0 3.9 %collective-permute-start.3 = (f32[8,128]{1,0:T(8,128)S(1)}, f32[8,128]{1,0:T(8,128)S(1)}, u32[]{:S(2)}, u32[]{:S(2)}) collective-permute-start(f32[8,128]{1,0:T(8,128)S(1)} %add.20), channel_id=1, source_target_pairs={{0,64},{64,0},{1,65},{65,1},{2,66},{66,2},{3,67},{67,3},{4,68},{68... | collective-permute-start | bytes 12296 | tf_op jit(solution)/shard_map/ppermute | solution.py:161
  145.9 2.5 %collective-permute-done.3 = f32[8,128]{1,0:T(8,128)S(1)} collective-permute-done((f32[8,128]{1,0:T(8,128)S(1)}, f32[8,128]{1,0:T(8,128)S(1)}, u32[]{:S(2)}, u32[]{:S(2)}) %collective-permute-start.3) | collective-permute-done | bytes 4128 | tf_op jit(solution)/shard_map/ppermute | solution.py:161
  148.4 1.9 %collective-permute-start.4 = (f32[8,128]{1,0:T(8,128)S(1)}, f32[8,128]{1,0:T(8,128)S(1)}, u32[]{:S(2)}, u32[]{:S(2)}) collective-permute-start(f32[8,128]{1,0:T(8,128)S(1)} %add.21), channel_id=1, source_target_pairs={{0,32},{32,0},{1,33},{33,1},{2,34},{34,2},{3,35},{35,3},{4,36},{36... | collective-permute-start | bytes 12296 | tf_op jit(solution)/shard_map/ppermute | solution.py:161
  150.3 0.5 slice.11
  150.8 3.1 %collective-permute-done.4 = f32[8,128]{1,0:T(8,128)S(1)} collective-permute-done((f32[8,128]{1,0:T(8,128)S(1)}, f32[8,128]{1,0:T(8,128)S(1)}, u32[]{:S(2)}, u32[]{:S(2)}) %collective-permute-start.4) | collective-permute-done | bytes 4128 | tf_op jit(solution)/shard_map/ppermute | solution.py:161
  153.9 0.5 slice.10
  155.7 0.8 shard_map.63
  156.5 0.0 all-to-all-done.5
  156.5 0.8 shard_map.64
  (5 shorter events, 0.0 us)
Async XLA Ops:
  0.6 0.9 copy-start
  1.5 14.3 %copy-start.1 = (f32[24,768]{1,0:T(8,128)S(1)}, f32[24,768]{1,0:T(8,128)}, u32[]{:S(2)}) copy-start(f32[24,768]{1,0:T(8,128)} %values_ref.7) | copy-start | bytes 221188
  1.5 14.3 %copy-start.2 = (f32[24,768]{1,0:T(8,128)S(1)}, f32[24,768]{1,0:T(8,128)}, u32[]{:S(2)}) copy-start(f32[24,768]{1,0:T(8,128)} %paired_ref.3) | copy-start | bytes 221188
  2.5 31.6 %all-to-all-start = ((bf16[16,24,768]{2,1,0:T(8,128)(2,1)}), bf16[16,24,768]{2,1,0:T(8,128)(2,1)S(1)}, u32[]{:S(2)}, u32[]{:S(2)}) async-start(bf16[16,24,768]{2,1,0:T(8,128)(2,1)} %bitcast.1), calls=%async_computation | async-start | bytes 1179648 | tf_op jit(solution)/shard_map/all_to_all | solution.py:157
  34.1 23.4 %all-to-all-start.1 = ((bf16[16,24,768]{2,1,0:T(8,128)(2,1)}), bf16[16,24,768]{2,1,0:T(8,128)(2,1)S(1)}, u32[]{:S(2)}, u32[]{:S(2)}) async-start(bf16[16,24,768]{2,1,0:T(8,128)(2,1)} %bitcast.3), calls=%async_computation.1 | async-start | bytes 1179648 | tf_op jit(solution)/shard_map/all_to_all | solution.py:157
  41.9 3.9 %collective-permute-start = (bf16[384,768]{1,0:T(8,128)(2,1)S(1)}, bf16[384,768]{1,0:T(8,128)(2,1)S(1)}, u32[]{:S(2)}, u32[]{:S(2)}) collective-permute-start(bf16[384,768]{1,0:T(8,128)(2,1)S(1)} %bitcast.20), channel_id=1, source_target_pairs={{0,1},{1,0},{2,3},{3,2},{4,5},{5,4},{6,7},{7,6},{8,9},{9,8},{10,11... | collective-permute-start | bytes 1769480 | tf_op jit(solution)/shard_map/ppermute | solution.py:161
  91.3 0.8 copy-start.3
  92.1 4.5 %copy-start.4 = (bf16[384,768]{1,0:T(8,128)(2,1)S(1)}, bf16[384,768]{1,0:T(8,128)(2,1)}, u32[]{:S(2)}) copy-start(bf16[384,768]{1,0:T(8,128)(2,1)} %copy-done.3) | copy-start | bytes 1769476
  92.1 22.3 %all-to-all-start.4 = ((bf16[16,24,768]{2,1,0:T(8,128)(2,1)}), bf16[16,24,768]{2,1,0:T(8,128)(2,1)S(1)}, u32[]{:S(2)}, u32[]{:S(2)}) async-start(bf16[16,24,768]{2,1,0:T(8,128)(2,1)} %bitcast.12), calls=%async_computation.4 | async-start | bytes 1179648 | tf_op jit(solution)/shard_map/all_to_all | solution.py:157
  96.7 3.9 %collective-permute-start.5 = (bf16[384,768]{1,0:T(8,128)(2,1)S(1)}, bf16[384,768]{1,0:T(8,128)(2,1)S(1)}, u32[]{:S(2)}, u32[]{:S(2)}) collective-permute-start(bf16[384,768]{1,0:T(8,128)(2,1)S(1)} %copy-done.4), channel_id=1, source_target_pairs={{0,1},{1,0},{2,3},{3,2},{4,5},{5,4},{6,7},{7,6},{8,9},{9,8},{10,11... | collective-permute-start | bytes 1769480 | tf_op jit(solution)/shard_map/ppermute | solution.py:161
  114.4 42.1 %all-to-all-start.5 = ((bf16[16,24,768]{2,1,0:T(8,128)(2,1)}), bf16[16,24,768]{2,1,0:T(8,128)(2,1)S(1)}, u32[]{:S(2)}, u32[]{:S(2)}) async-start(bf16[16,24,768]{2,1,0:T(8,128)(2,1)} %bitcast.14), calls=%async_computation.5 | async-start | bytes 1179648 | tf_op jit(solution)/shard_map/all_to_all | solution.py:157
  119.3 13.2 %collective-permute-start.1 = (f32[8,128]{1,0:T(8,128)S(1)}, f32[8,128]{1,0:T(8,128)S(1)}, u32[]{:S(2)}, u32[]{:S(2)}) collective-permute-start(f32[8,128]{1,0:T(8,128)S(1)} %slice.9), channel_id=1, source_target_pairs={{0,256},{256,0},{1,257},{257,1},{2,258},{258,2},{3,259},{259,3},{4... | collective-permute-start | bytes 12296 | tf_op jit(solution)/shard_map/ppermute | solution.py:161
  132.6 9.4 %collective-permute-start.2 = (f32[8,128]{1,0:T(8,128)S(1)}, f32[8,128]{1,0:T(8,128)S(1)}, u32[]{:S(2)}, u32[]{:S(2)}) collective-permute-start(f32[8,128]{1,0:T(8,128)S(1)} %slice_add_fusion), channel_id=1, source_target_pairs={{0,128},{128,0},{1,129},{129,1},{2,130},{130,2},{3,131},{131,3},{4... | collective-permute-start | bytes 12296 | tf_op jit(solution)/shard_map/ppermute | solution.py:161
  142.0 6.4 %collective-permute-start.3 = (f32[8,128]{1,0:T(8,128)S(1)}, f32[8,128]{1,0:T(8,128)S(1)}, u32[]{:S(2)}, u32[]{:S(2)}) collective-permute-start(f32[8,128]{1,0:T(8,128)S(1)} %add.20), channel_id=1, source_target_pairs={{0,64},{64,0},{1,65},{65,1},{2,66},{66,2},{3,67},{67,3},{4,68},{68... | collective-permute-start | bytes 12296 | tf_op jit(solution)/shard_map/ppermute | solution.py:161
  148.4 5.5 %collective-permute-start.4 = (f32[8,128]{1,0:T(8,128)S(1)}, f32[8,128]{1,0:T(8,128)S(1)}, u32[]{:S(2)}, u32[]{:S(2)}) collective-permute-start(f32[8,128]{1,0:T(8,128)S(1)} %add.21), channel_id=1, source_target_pairs={{0,32},{32,0},{1,33},{33,1},{2,34},{34,2},{3,35},{35,3},{4,36},{36... | collective-permute-start | bytes 12296 | tf_op jit(solution)/shard_map/ppermute | solution.py:161

commit v2 on v1

v2 whole, which is shorter than its diff:
```python
import functools

import jax
import jax.numpy as jnp
from jax import lax
from jax.experimental import pallas as pl
from jax.experimental.pallas import tpu as pltpu
from jax.sharding import Mesh
from jax.sharding import PartitionSpec as P

ALL = ("z0", "y2", "y1", "y0", "x", "zh", "c")
INNER = ("z0", "y2", "y1", "y0")
CHIPS = ("x", "zh")
NEAR = ("z0", "y0")
NEAR_STATS = ("z0", "y0", "y1")
MIDDLE = "y1"
FAR = "y2"
CORE = "c"

EPSILON = 1e-06
LAST = (((1,), (1,)), ((), ()))
FIRST = (((0,), (0,)), ((), ()))
VMEM_LIMIT = 24 * 1024 * 1024
EXTRA = 128


def f32_dot(a, b, dims):
    return lax.dot_general(a, b, dims, preferred_element_type=jnp.float32)


def unit_rows(values):
    inverse = lax.rsqrt(jnp.sum(values * values, axis=1, keepdims=True) + EPSILON)
    return values * inverse, inverse


def kernel_call(body, out_shape, *args, flops=0):
    def spec(a):
        return pl.BlockSpec(memory_space=pltpu.SMEM if a.size == 1 else pltpu.VMEM)

    outs = jax.tree.leaves(out_shape)
    moved = sum(a.size * a.dtype.itemsize for a in (*args, *outs))
    return pl.pallas_call(
        body,
        out_shape=out_shape,
        in_specs=[spec(a) for a in args],
        out_specs=jax.tree.map(spec, out_shape),
        compiler_params=pltpu.CompilerParams(vmem_limit_bytes=VMEM_LIMIT),
        cost_estimate=pl.CostEstimate(flops=flops, bytes_accessed=moved, transcendentals=0),
    )(*args)


def packed(value, rows):
    value = jnp.broadcast_to(value, (rows, EXTRA))
    high = value.astype(jnp.bfloat16).astype(jnp.float32)
    middle = (value - high).astype(jnp.bfloat16).astype(jnp.float32)
    low = value - high - middle
    lane = lax.broadcasted_iota(jnp.int32, (rows, EXTRA), 1)
    parts = jnp.where(lane == 0, high, jnp.where(lane == 1, middle, jnp.where(lane == 2, low, 0.0)))
    return parts.astype(jnp.bfloat16)


def unpacked(values, width):
    return jnp.sum(values[0:1, width:])


def text_units_kernel(values_ref, copies_ref):
    unit, _ = unit_rows(values_ref[...])
    half = jnp.concatenate([unit, unit], axis=0).astype(jnp.bfloat16)
    rows = half.shape[0]
    for k in range(copies_ref.shape[0] // rows):
        copies_ref[k * rows : (k + 1) * rows, :] = half


def image_units_kernel(values_ref, other_ref, half_ref, diagonal_ref):
    first = unit_rows(values_ref[...])[0].astype(jnp.bfloat16)
    second = unit_rows(other_ref[...])[0].astype(jnp.bfloat16)
    half_ref[...] = first
    products = first.astype(jnp.float32) * second.astype(jnp.float32)
    diagonal_ref[...] = jnp.broadcast_to(jnp.sum(products), diagonal_ref.shape)


def join_kernel(side_ref, mine_ref, theirs_ref, joined_ref):
    mine, theirs = mine_ref[...].astype(jnp.float32), theirs_ref[...].astype(jnp.float32)
    first = side_ref[0] == 0
    joined = jnp.concatenate(
        [jnp.where(first, mine, theirs), jnp.where(first, theirs, mine)], axis=0
    ).astype(jnp.bfloat16)
    rows = joined.shape[0]
    for k in range(joined_ref.shape[0] // rows):
        joined_ref[k * rows : (k + 1) * rows, :] = joined


def lines(row):
    return [row[:, k * 128 : (k + 1) * 128] for k in range(row.shape[1] // 128)]


def line(rows):
    return jnp.concatenate([rows[k : k + 1, :] for k in range(rows.shape[0])], axis=1)


def eight(rows):
    zero = jnp.zeros((1, 128), jnp.float32)
    return jnp.concatenate([*rows, *[zero] * (8 - len(rows))], axis=0)


def lse_of(parts):
    peak = functools.reduce(jnp.maximum, [jnp.max(p, axis=0, keepdims=True) for p in parts])
    total = sum(jnp.sum(jnp.exp(p - peak), axis=0, keepdims=True) for p in parts)
    return peak + jnp.log(total)


def pieces_lse(pieces):
    peak = jnp.max(pieces, axis=0)
    return peak + jnp.log(jnp.sum(jnp.exp(pieces - peak[None]), axis=0))


def pair_lse(a, b):
    peak = jnp.maximum(a, b)
    return peak + jnp.log(jnp.exp(a - peak) + jnp.exp(b - peak))


def stats_kernel(factor_ref, image_ref, own_ref, other_ref, diagonal_ref, row_ref, col_ref):
    factor = factor_ref[0]
    image, own, other = image_ref[...], own_ref[...], other_ref[...]
    own_lse = lse_of([factor * f32_dot(image, own, LAST)])
    other_lse = lse_of([factor * f32_dot(image, other, LAST)])
    row_lse = lse_of([factor * f32_dot(own, image, LAST), factor * f32_dot(other, image, LAST)])
    message = eight([*lines(row_lse), factor * diagonal_ref[0:1, :]])
    row_ref[...] = jnp.broadcast_to(message[None], row_ref.shape)
    col_ref[...] = eight([*lines(own_lse), *lines(other_lse)])


def pair_columns_kernel(mine_ref, theirs_ref, message_ref):
    mine, theirs = mine_ref[...], theirs_ref[...]
    own = pair_lse(mine[0:3], theirs[3:6])
    other = pair_lse(mine[3:6], theirs[0:3])
    message = jnp.concatenate([own, other, jnp.zeros((2, 128), jnp.float32)], axis=0)
    message_ref[...] = jnp.broadcast_to(message[None], message_ref.shape)


def near_rows_kernel(pieces_ref, message_ref):
    pieces = pieces_ref[...]
    place = lax.broadcasted_iota(jnp.int32, (8, 128), 0)
    message_ref[...] = jnp.where(place == 3, jnp.sum(pieces, axis=0), pieces_lse(pieces))


def weights_kernel(
    factor_ref, image_ref, own_ref, other_ref, row_ref, far_row_ref, pieces_ref,
    image_out, own_out, other_out, share_ref,
):
    factor = factor_ref[0]
    width = own_ref.shape[1]
    cols = pieces_lse(pieces_ref[...])
    own_lse, other_lse = line(cols[0:3]), line(cols[3:6])
    col_share = jnp.sum(own_lse) + jnp.sum(other_lse)
    near, far = row_ref[...], far_row_ref[...]
    rows = pair_lse(near[0:3], far[0:3])
    row_share = jnp.sum(rows) - 2.0 * jnp.max(near[3:4] + far[3:4])
    share_ref[...] = jnp.broadcast_to(row_share, share_ref.shape)
    row_lse = jnp.concatenate(
        [jnp.transpose(jnp.broadcast_to(rows[k : k + 1, :], (128, 128))) for k in range(3)], axis=0
    )[:, 0:1]
    image = image_ref[...]
    image_sum = None
    for text_ref, col_lse in ((own_ref, own_lse), (other_ref, other_lse)):
        text = text_ref[...]
        logits = factor * f32_dot(image, text, LAST)
        weights = (
            (0.5 * factor) * (jnp.exp(logits - row_lse) + jnp.exp(logits - col_lse))
        ).astype(jnp.bfloat16)
        part = jnp.dot(weights, text, preferred_element_type=jnp.float32)
        image_sum = part if image_sum is None else image_sum + part
        text_sum = f32_dot(weights, image, FIRST)
        if text_ref is own_ref:
            own_out[...] = text_sum
        else:
            other_out[:, :width] = text_sum.astype(jnp.bfloat16)
    other_out[:, width:] = packed(row_share, other_out.shape[0])
    image_out[:, :width] = image_sum.astype(jnp.bfloat16)
    image_out[:, width:] = packed(col_share, image_out.shape[0])


def pair_sums_kernel(own_ref, theirs_ref, share_ref, message_ref):
    width = own_ref.shape[1]
    theirs = theirs_ref[...].astype(jnp.float32)
    message_ref[:, :width] = (own_ref[...] + theirs[:, :width]).astype(jnp.bfloat16)
    share = jnp.max(share_ref[...]) + unpacked(theirs, width)
    message_ref[:, width:] = packed(share, message_ref.shape[0])


def slabs_sum(pieces_ref, rows):
    total = None
    for k in range(pieces_ref.shape[0] // (2 * rows)):
        both = pieces_ref[2 * rows * k : 2 * rows * (k + 1), :].astype(jnp.float32)
        both = both[:rows] + both[rows:]
        total = both if total is None else total + both
    return total


def keep_and_send(total, share, side_ref, keep_ref, send_ref, share_ref):
    rows, width = keep_ref.shape
    first = side_ref[0] == 0
    lower, upper = total[:rows, :width], total[rows:, :width]
    keep_ref[...] = jnp.where(first, lower, upper)
    send_ref[:, :width] = jnp.where(first, upper, lower).astype(jnp.bfloat16)
    send_ref[:, width:] = packed(share, rows)
    share_ref[...] = jnp.broadcast_to(share, share_ref.shape)


def near_sums_kernel(side_ref, pieces_ref, keep_ref, send_ref, share_ref):
    rows, width = keep_ref.shape
    total = slabs_sum(pieces_ref, 2 * rows)
    keep_and_send(total, unpacked(total, width), side_ref, keep_ref, send_ref, share_ref)


def middle_sums_kernel(side_ref, kept_ref, theirs_ref, shared_ref, keep_ref, send_ref, share_ref):
    width = kept_ref.shape[1]
    theirs = theirs_ref[...].astype(jnp.float32)
    share = jnp.max(shared_ref[...]) + unpacked(theirs, width)
    keep_and_send(kept_ref[...] + theirs[:, :width], share, side_ref, keep_ref, send_ref, share_ref)


def gradient(factor, values, paired, total):
    unit, inverse = unit_rows(values)
    pull = total - factor * unit_rows(paired)[0].astype(jnp.bfloat16).astype(jnp.float32)
    return (pull - unit * jnp.sum(pull * unit, axis=1, keepdims=True)) * inverse


def image_gradient_kernel(
    factor_ref, values_ref, paired_ref, kept_ref, theirs_ref, shared_ref, gradient_ref, share_ref
):
    width = kept_ref.shape[1]
    theirs = theirs_ref[...].astype(jnp.float32)
    total = kept_ref[...] + theirs[:, :width]
    gradient_ref[...] = gradient(factor_ref[0], values_ref[...], paired_ref[...], total)
    share = jnp.max(shared_ref[...]) + unpacked(theirs, width)
    share_ref[...] = jnp.broadcast_to(share, share_ref.shape)


def text_gradient_kernel(
    factor_ref, values_ref, paired_ref, pieces_ref, shared_ref, gradient_ref, share_ref
):
    rows, width = values_ref.shape
    total = slabs_sum(pieces_ref, rows)
    gradient_ref[...] = gradient(
        factor_ref[0], values_ref[...], paired_ref[...], total[:, :width]
    )
    share = jnp.max(shared_ref[...]) + unpacked(total, width)
    share_ref[...] = jnp.broadcast_to(share, share_ref.shape)


def exchanged(blocks, axis):
    count = lax.axis_size(axis)
    split = blocks.reshape(count, -1, blocks.shape[-1])
    return lax.all_to_all(split, axis, split_axis=0, concat_axis=0, tiled=True).reshape(blocks.shape)


def swapped(x, axis):
    return lax.ppermute(x, axis, [(0, 1), (1, 0)])


def after(x, first):
    return lax.optimization_barrier((x, first))[0]


def shape(dims, dtype):
    return jax.ShapeDtypeStruct(dims, dtype)


def place(axis):
    return lax.axis_index(axis).astype(jnp.int32).reshape(1)


def on_device(image_emb, text_emb, factor):
    own_rows, width = image_emb.shape
    inner, chips, near = (lax.axis_size(a) for a in (INNER, CHIPS, NEAR))
    bf16, f32 = jnp.bfloat16, jnp.float32
    image_rows, text_rows = own_rows * inner, own_rows * chips
    wide = width + EXTRA
    work = 2 * image_rows * text_rows * width
    middle, far = place(MIDDLE), place(FAR)
    tile = shape((8, 128), f32)

    text_copies = kernel_call(text_units_kernel, shape((text_rows, width), bf16), text_emb)
    text_own = exchanged(text_copies, CHIPS)
    text_other = swapped(text_own, CORE)
    half, diagonal = kernel_call(
        image_units_kernel, (shape((own_rows, width), bf16), tile), image_emb, text_emb
    )
    two = kernel_call(
        join_kernel, shape((2 * own_rows, width), bf16), far, half, swapped(half, FAR)
    )
    image_copies = kernel_call(
        join_kernel, shape((image_rows, width), bf16), middle, two, swapped(two, MIDDLE)
    )
    image_group = exchanged(after(image_copies, text_own), NEAR)

    row_message, col_part = kernel_call(
        stats_kernel,
        (shape((lax.axis_size(NEAR_STATS), 8, 128), f32), tile),
        factor, image_group, text_own, text_other, diagonal,
        flops=4 * work,
    )
    row_pieces = exchanged(row_message, NEAR_STATS)
    col_message = kernel_call(
        pair_columns_kernel, shape((chips, 8, 128), f32), col_part, swapped(col_part, CORE)
    )
    col_pieces = exchanged(after(col_message, row_pieces), CHIPS)
    near_rows = kernel_call(near_rows_kernel, tile, row_pieces)

    image_part, own_part, other_part, row_share = kernel_call(
        weights_kernel,
        (
            shape((image_rows, wide), bf16),
            shape((text_rows, width), f32),
            shape((text_rows, wide), bf16),
            tile,
        ),
        factor, image_group, text_own, text_other, near_rows, swapped(near_rows, FAR), col_pieces,
        flops=6 * work,
    )
    image_pieces = exchanged(image_part, NEAR)
    text_part = kernel_call(
        pair_sums_kernel, shape((text_rows, wide), bf16),
        own_part, swapped(other_part, CORE), row_share,
    )
    text_pieces = exchanged(after(text_part, image_pieces), CHIPS)

    kept, sent, share = kernel_call(
        near_sums_kernel,
        (shape((2 * own_rows, width), f32), shape((2 * own_rows, wide), bf16), tile),
        middle, image_pieces,
    )
    kept, sent, share = kernel_call(
        middle_sums_kernel,
        (shape((own_rows, width), f32), shape((own_rows, wide), bf16), tile),
        far, kept, swapped(sent, MIDDLE), share,
    )
    out = shape((own_rows, width), f32)
    image_grad, share = kernel_call(
        image_gradient_kernel, (out, tile),
        factor, image_emb, text_emb, kept, swapped(sent, FAR), share,
    )
    text_grad, share = kernel_call(
        text_gradient_kernel, (out, tile), factor, text_emb, image_emb, text_pieces, share
    )
    whole = 2.0 * own_rows * inner * chips * lax.axis_size(CORE)
    return ((share[0, 0] / whole).reshape(1), image_grad, text_grad)


def solution(mesh):
    split = Mesh(mesh.devices.reshape(2, 2, 2, 2, 4, 4, 2), ALL)
    in_specs = (P(ALL, None), P(ALL, None), P())
    out_specs = (P(), P(ALL, None), P(ALL, None))
    return jax.shard_map(
        on_device, mesh=split, in_specs=in_specs, out_specs=out_specs, check_vma=False
    )
```

time: 159 us -> 126 us (0.79)
  the two profiles are of different devices: /device:TPU:10 before, /device:TPU:72 now
where the time goes in v2:
time: 126 us; the launch traced here: 125 us
  starting transfers between devices  78.2 us (62%)
  waiting for transfers between devices  30.2 us (24%)
  Pallas kernels  11.3 us (9%)
  between operations  3.22 us (3%)
  local copies, waits for them, and re-layouts  2.46 us (2%)
    all_to_all x6, starting transfers between devices, exchanged(): lax.all_to_all(split, axis, split_axis=0, concat_axis=0, tiled=True)  45.7 us
    ppermute x8, starting transfers between devices, swapped(): return lax.ppermute(x, axis, [(0, 1), (1, 0)])  32.5 us
    ppermute x8, waiting for transfers between devices, swapped(): return lax.ppermute(x, axis, [(0, 1), (1, 0)])  21.4 us
    pallas_call x13, Pallas kernels, kernel_call(): pl.pallas_call(body, out_shape=out_shape, in_specs=[spec(a) for a in args...  11.3 us
    all_to_all x6, waiting for transfers between devices, exchanged(): lax.all_to_all(split, axis, split_axis=0, concat_axis=0, tiled=True)  8.81 us
  transfers between devices with their start and end apart: 14, of which 14 were waited for; matrix products, arithmetic and copies ran while one was open for 0% of the time, Pallas kernels for 3%

profile of v2, /device:TPU:72, one launch (start us, length us, event | category | flops | bytes accessed | tf_op | source)
XLA Modules:
  0.0 125.3 jit_solution(5452221992343987337)
XLA Ops:
  0.6 0.0 copy-start
  0.6 0.9 copy-done
  1.5 0.0 copy-start.1
  1.5 0.0 copy-start.2
  1.5 1.0 shard_map.61
  2.5 12.0 %all-to-all-start = ((bf16[16,24,768]{2,1,0:T(8,128)(2,1)}), bf16[16,24,768]{2,1,0:T(8,128)(2,1)S(1)}, u32[]{:S(2)}, u32[]{:S(2)}) async-start(bf16[16,24,768]{2,1,0:T(8,128)(2,1)} %bitcast.2), calls=%async_computation | async-start | bytes 1179648 | tf_op jit(solution)/shard_map/all_to_all | solution.py:255
  14.5 0.0 copy-done.1
  14.5 0.0 copy-done.2
  14.5 0.2 shard_map.58
  14.7 6.8 %collective-permute-start = (bf16[24,768]{1,0:T(8,128)(2,1)S(1)}, bf16[24,768]{1,0:T(8,128)(2,1)S(1)}, u32[]{:S(2)}, u32[]{:S(2)}) collective-permute-start(bf16[24,768]{1,0:T(8,128)(2,1)S(1)} %get-tuple-element.24.mine_ref), channel_id=1, source_target_pairs={{0,128},{128,0},{1,129},{129,1},{2,130},{130,2},{3,131},{131,3},{4... | collective-permute-start | bytes 110600 | tf_op jit(solution)/shard_map/ppermute | solution.py:259
  21.6 3.0 %collective-permute-done.theirs_ref = bf16[24,768]{1,0:T(8,128)(2,1)S(1)} collective-permute-done((bf16[24,768]{1,0:T(8,128)(2,1)S(1)}, bf16[24,768]{1,0:T(8,128)(2,1)S(1)}, u32[]{:S(2)}, u32[]{:S(2)}) %collective-permute-start) | collective-permute-done | bytes 36896 | tf_op jit(solution)/shard_map/ppermute | solution.py:259
  24.6 4.4 %collective-permute-start.1 = (bf16[48,768]{1,0:T(8,128)(2,1)S(1)}, bf16[48,768]{1,0:T(8,128)(2,1)S(1)}, u32[]{:S(2)}, u32[]{:S(2)}) collective-permute-start(bf16[48,768]{1,0:T(8,128)(2,1)S(1)} %shard_map.59.mine_ref), channel_id=1, source_target_pairs={{0,64},{64,0},{1,65},{65,1},{2,66},{66,2},{3,67},{67,3},{4,68},{68... | collective-permute-start | bytes 221192 | tf_op jit(solution)/shard_map/ppermute | solution.py:259
  29.0 2.7 %collective-permute-done.1.theirs_ref = bf16[48,768]{1,0:T(8,128)(2,1)S(1)} collective-permute-done((bf16[48,768]{1,0:T(8,128)(2,1)S(1)}, bf16[48,768]{1,0:T(8,128)(2,1)S(1)}, u32[]{:S(2)}, u32[]{:S(2)}) %collective-permute-start.1) | collective-permute-done | bytes 73760 | tf_op jit(solution)/shard_map/ppermute | solution.py:259
  31.8 0.9 shard_map.60
  32.6 1.9 %all-to-all-done = bf16[16,24,768]{2,1,0:T(8,128)(2,1)S(1)} async-done(((bf16[16,24,768]{2,1,0:T(8,128)(2,1)}), bf16[16,24,768]{2,1,0:T(8,128)(2,1)S(1)}, u32[]{:S(2)}, u32[]{:S(2)}) %all-to-all-start) | async-done | bytes 589856 | tf_op jit(solution)/shard_map/all_to_all | solution.py:255
  34.5 4.2 %all-to-all-start.1 = ((bf16[4,96,768]{2,1,0:T(8,128)(2,1)}), bf16[4,96,768]{2,1,0:T(8,128)(2,1)S(1)}, u32[]{:S(2)}, u32[]{:S(2)}) async-start(bf16[4,96,768]{2,1,0:T(8,128)(2,1)} %bitcast.4), calls=%async_computation.1 | async-start | bytes 1179648 | tf_op jit(solution)/shard_map/all_to_all | solution.py:255
  38.7 1.9 %collective-permute-start.2 = (bf16[384,768]{1,0:T(8,128)(2,1)S(1)}, bf16[384,768]{1,0:T(8,128)(2,1)S(1)}, u32[]{:S(2)}, u32[]{:S(2)}) collective-permute-start(bf16[384,768]{1,0:T(8,128)(2,1)S(1)} %bitcast.13), channel_id=1, source_target_pairs={{0,1},{1,0},{2,3},{3,2},{4,5},{5,4},{6,7},{7,6},{8,9},{9,8},{10,11... | collective-permute-start | bytes 1769480 | tf_op jit(solution)/shard_map/ppermute | solution.py:259
  41.2 1.3 %collective-permute-done.2.other_ref = bf16[384,768]{1,0:T(8,128)(2,1)S(1)} collective-permute-done((bf16[384,768]{1,0:T(8,128)(2,1)S(1)}, bf16[384,768]{1,0:T(8,128)(2,1)S(1)}, u32[]{:S(2)}, u32[]{:S(2)}) %collective-permute-start.2) | collective-permute-done | bytes 589856 | tf_op jit(solution)/shard_map/ppermute | solution.py:259
  42.5 0.0 copy-start.3
  42.5 1.6 %all-to-all-done.1 = bf16[4,96,768]{2,1,0:T(8,128)(2,1)S(1)} async-done(((bf16[4,96,768]{2,1,0:T(8,128)(2,1)}), bf16[4,96,768]{2,1,0:T(8,128)(2,1)S(1)}, u32[]{:S(2)}, u32[]{:S(2)}) %all-to-all-start.1) | async-done | bytes 589856 | tf_op jit(solution)/shard_map/all_to_all | solution.py:255
  44.1 2.2 %shard_map.62 = (f32[8,8,128]{2,1,0:T(8,128)}, f32[8,128]{1,0:T(8,128)S(1)}) custom-call(f32[1]{0:T(128)S(6)} %copy.6.factor_ref, bf16[384,768]{1,0:T(8,128)(2,1)S(1)} %bitcast.16, bf16[384,768]{1,0:T(8,128)(2,1)S(1)} %bitcast.14, bf16[384,768]{1,0:T(8,128)(2,1)S(1)} %collective-permute-done.2.other_ref, f32[8,128]{1,0:T(8,128)S(1)} %get-tuple-element.26.diagonal_ref), custom_call_target="tpu_custom_call" | custom-call | flops 905969664 | bytes 1810436 | tf_op jit(solution)/shard_map/pallas_call | solution.py:42
  46.4 0.0 copy-done.3
  46.4 6.3 %all-to-all-start.2 = ((f32[8,8,128]{2,1,0:T(8,128)}), f32[8,8,128]{2,1,0:T(8,128)S(1)}, u32[]{:S(2)}, u32[]{:S(2)}) async-start(f32[8,8,128]{2,1,0:T(8,128)} %get-tuple-element.27), calls=%async_computation.2 | async-start | bytes 65536 | tf_op jit(solution)/shard_map/all_to_all | solution.py:255
  52.6 1.9 %collective-permute-start.4 = (f32[8,128]{1,0:T(8,128)S(1)}, f32[8,128]{1,0:T(8,128)S(1)}, u32[]{:S(2)}, u32[]{:S(2)}) collective-permute-start(f32[8,128]{1,0:T(8,128)S(1)} %get-tuple-element.28.mine_ref), channel_id=1, source_target_pairs={{0,1},{1,0},{2,3},{3,2},{4,5},{5,4},{6,7},{7,6},{8,9},{9,8},{10,11... | collective-permute-start | bytes 12296 | tf_op jit(solution)/shard_map/ppermute | solution.py:259
  54.5 1.1 collective-permute-done.4.theirs_ref
  55.7 0.7 shard_map.64
  56.3 0.5 all-to-all-done.2.pieces_ref
  56.8 8.4 %all-to-all-start.3 = ((f32[16,8,128]{2,1,0:T(8,128)}), f32[16,8,128]{2,1,0:T(8,128)S(1)}, u32[]{:S(2)}, u32[]{:S(2)}) async-start(f32[16,8,128]{2,1,0:T(8,128)} %shard_map.64), calls=%async_computation.3 | async-start | bytes 131072 | tf_op jit(solution)/shard_map/all_to_all | solution.py:255
  65.3 6.3 %collective-permute-start.3 = (f32[8,128]{1,0:T(8,128)S(1)}, f32[8,128]{1,0:T(8,128)S(1)}, u32[]{:S(2)}, u32[]{:S(2)}) collective-permute-start(f32[8,128]{1,0:T(8,128)S(1)} %shard_map.63.row_ref), channel_id=1, source_target_pairs={{0,128},{128,0},{1,129},{129,1},{2,130},{130,2},{3,131},{131,3},{4... | collective-permute-start | bytes 12296 | tf_op jit(solution)/shard_map/ppermute | solution.py:259
  71.6 3.1 %collective-permute-done.3.far_row_ref = f32[8,128]{1,0:T(8,128)S(1)} collective-permute-done((f32[8,128]{1,0:T(8,128)S(1)}, f32[8,128]{1,0:T(8,128)S(1)}, u32[]{:S(2)}, u32[]{:S(2)}) %collective-permute-start.3) | collective-permute-done | bytes 4128 | tf_op jit(solution)/shard_map/ppermute | solution.py:259
  74.7 0.8 all-to-all-done.3.pieces_ref
  75.5 0.0 copy-start.4
  75.5 1.1 copy-done.4
  76.6 3.3 %shard_map.65 = (bf16[384,896]{1,0:T(8,128)(2,1)}, f32[384,768]{1,0:T(8,128)S(1)}, bf16[384,896]{1,0:T(8,128)(2,1)S(1)}, f32[8,128]{1,0:T(8,128)S(1)}) custom-call(f32[1]{0:T(128)S(6)} %copy.6.factor_ref, bf16[384,768]{1,0:T(8,128)(2,1)S(1)} %bitcast.17, bf16[384,768]{1,0:T(8,128)(2,1)S(1)} %bitcast.15, bf16[384,768]{1,0:T(8,128)(2,1)S(1)} %copy-done.4, ...), custom_call_target="tpu_custom_call" | custom-call | flops 1358954496 | bytes 4403204 | tf_op jit(solution)/shard_map/pallas_call | solution.py:42
  79.8 5.9 %all-to-all-start.4 = ((bf16[4,96,896]{2,1,0:T(8,128)(2,1)}), bf16[4,96,896]{2,1,0:T(8,128)(2,1)S(1)}, u32[]{:S(2)}, u32[]{:S(2)}) async-start(bf16[4,96,896]{2,1,0:T(8,128)(2,1)} %bitcast.6), calls=%async_computation.4 | async-start | bytes 1376256 | tf_op jit(solution)/shard_map/all_to_all | solution.py:255
  85.8 1.9 %collective-permute-start.5 = (bf16[384,896]{1,0:T(8,128)(2,1)S(1)}, bf16[384,896]{1,0:T(8,128)(2,1)S(1)}, u32[]{:S(2)}, u32[]{:S(2)}) collective-permute-start(bf16[384,896]{1,0:T(8,128)(2,1)S(1)} %get-tuple-element.31), channel_id=1, source_target_pairs={{0,1},{1,0},{2,3},{3,2},{4,5},{5,4},{6,7},{7,6},{8,9},{9,8},{10,11... | collective-permute-start | bytes 2064392 | tf_op jit(solution)/shard_map/ppermute | solution.py:259
  87.7 2.1 %collective-permute-done.5.theirs_ref = bf16[384,896]{1,0:T(8,128)(2,1)S(1)} collective-permute-done((bf16[384,896]{1,0:T(8,128)(2,1)S(1)}, bf16[384,896]{1,0:T(8,128)(2,1)S(1)}, u32[]{:S(2)}, u32[]{:S(2)}) %collective-permute-start.5) | collective-permute-done | bytes 688160 | tf_op jit(solution)/shard_map/ppermute | solution.py:259
  89.8 1.1 shard_map.66
  90.9 0.9 all-to-all-done.4
  91.8 8.9 %all-to-all-start.5 = ((bf16[16,24,896]{2,1,0:T(8,128)(2,1)}), bf16[16,24,896]{2,1,0:T(8,128)(2,1)S(1)}, u32[]{:S(2)}, u32[]{:S(2)}) async-start(bf16[16,24,896]{2,1,0:T(8,128)(2,1)} %bitcast.8), calls=%async_computation.5 | async-start | bytes 1376256 | tf_op jit(solution)/shard_map/all_to_all | solution.py:255
  100.7 0.2 shard_map.67
  100.8 3.0 %collective-permute-start.6 = (bf16[48,896]{1,0:T(8,128)(2,1)S(1)}, bf16[48,896]{1,0:T(8,128)(2,1)S(1)}, u32[]{:S(2)}, u32[]{:S(2)}) collective-permute-start(bf16[48,896]{1,0:T(8,128)(2,1)S(1)} %get-tuple-element.36), channel_id=1, source_target_pairs={{0,64},{64,0},{1,65},{65,1},{2,66},{66,2},{3,67},{67,3},{4,68},{68... | collective-permute-start | bytes 258056 | tf_op jit(solution)/shard_map/ppermute | solution.py:259
  103.8 4.4 %collective-permute-done.6.theirs_ref = bf16[48,896]{1,0:T(8,128)(2,1)S(1)} collective-permute-done((bf16[48,896]{1,0:T(8,128)(2,1)S(1)}, bf16[48,896]{1,0:T(8,128)(2,1)S(1)}, u32[]{:S(2)}, u32[]{:S(2)}) %collective-permute-start.6) | collective-permute-done | bytes 86048 | tf_op jit(solution)/shard_map/ppermute | solution.py:259
  108.2 0.1 shard_map.68
  108.3 6.3 %collective-permute-start.7 = (bf16[24,896]{1,0:T(8,128)(2,1)S(1)}, bf16[24,896]{1,0:T(8,128)(2,1)S(1)}, u32[]{:S(2)}, u32[]{:S(2)}) collective-permute-start(bf16[24,896]{1,0:T(8,128)(2,1)S(1)} %get-tuple-element.39), channel_id=1, source_target_pairs={{0,128},{128,0},{1,129},{129,1},{2,130},{130,2},{3,131},{131,3},{4... | collective-permute-start | bytes 129032 | tf_op jit(solution)/shard_map/ppermute | solution.py:259
  114.6 3.5 %collective-permute-done.7.theirs_ref = bf16[24,896]{1,0:T(8,128)(2,1)S(1)} collective-permute-done((bf16[24,896]{1,0:T(8,128)(2,1)S(1)}, bf16[24,896]{1,0:T(8,128)(2,1)S(1)}, u32[]{:S(2)}, u32[]{:S(2)}) %collective-permute-start.7) | collective-permute-done | bytes 43040 | tf_op jit(solution)/shard_map/ppermute | solution.py:259
  118.2 0.8 shard_map.69
  119.0 3.2 %all-to-all-done.5 = bf16[16,24,896]{2,1,0:T(8,128)(2,1)S(1)} async-done(((bf16[16,24,896]{2,1,0:T(8,128)(2,1)}), bf16[16,24,896]{2,1,0:T(8,128)(2,1)S(1)}, u32[]{:S(2)}, u32[]{:S(2)}) %all-to-all-start.5) | async-done | bytes 688160 | tf_op jit(solution)/shard_map/all_to_all | solution.py:255
  122.2 0.8 shard_map.70
  123.1 0.5 slice.3
  (2 shorter events, 0.0 us)
Async XLA Ops:
  0.6 0.9 copy-start
  1.5 12.9 %copy-start.1 = (f32[24,768]{1,0:T(8,128)S(1)}, f32[24,768]{1,0:T(8,128)}, u32[]{:S(2)}) copy-start(f32[24,768]{1,0:T(8,128)} %values_ref.7) | copy-start | bytes 221188
  1.5 13.0 %copy-start.2 = (f32[24,768]{1,0:T(8,128)S(1)}, f32[24,768]{1,0:T(8,128)}, u32[]{:S(2)}) copy-start(f32[24,768]{1,0:T(8,128)} %paired_ref.3) | copy-start | bytes 221188
  2.5 32.0 %all-to-all-start = ((bf16[16,24,768]{2,1,0:T(8,128)(2,1)}), bf16[16,24,768]{2,1,0:T(8,128)(2,1)S(1)}, u32[]{:S(2)}, u32[]{:S(2)}) async-start(bf16[16,24,768]{2,1,0:T(8,128)(2,1)} %bitcast.2), calls=%async_computation | async-start | bytes 1179648 | tf_op jit(solution)/shard_map/all_to_all | solution.py:255
  14.7 9.9 %collective-permute-start = (bf16[24,768]{1,0:T(8,128)(2,1)S(1)}, bf16[24,768]{1,0:T(8,128)(2,1)S(1)}, u32[]{:S(2)}, u32[]{:S(2)}) collective-permute-start(bf16[24,768]{1,0:T(8,128)(2,1)S(1)} %get-tuple-element.24.mine_ref), channel_id=1, source_target_pairs={{0,128},{128,0},{1,129},{129,1},{2,130},{130,2},{3,131},{131,3},{4... | collective-permute-start | bytes 110600 | tf_op jit(solution)/shard_map/ppermute | solution.py:259
  24.6 7.1 %collective-permute-start.1 = (bf16[48,768]{1,0:T(8,128)(2,1)S(1)}, bf16[48,768]{1,0:T(8,128)(2,1)S(1)}, u32[]{:S(2)}, u32[]{:S(2)}) collective-permute-start(bf16[48,768]{1,0:T(8,128)(2,1)S(1)} %shard_map.59.mine_ref), channel_id=1, source_target_pairs={{0,64},{64,0},{1,65},{65,1},{2,66},{66,2},{3,67},{67,3},{4,68},{68... | collective-permute-start | bytes 221192 | tf_op jit(solution)/shard_map/ppermute | solution.py:259
  34.5 9.7 %all-to-all-start.1 = ((bf16[4,96,768]{2,1,0:T(8,128)(2,1)}), bf16[4,96,768]{2,1,0:T(8,128)(2,1)S(1)}, u32[]{:S(2)}, u32[]{:S(2)}) async-start(bf16[4,96,768]{2,1,0:T(8,128)(2,1)} %bitcast.4), calls=%async_computation.1 | async-start | bytes 1179648 | tf_op jit(solution)/shard_map/all_to_all | solution.py:255
  38.7 3.9 %collective-permute-start.2 = (bf16[384,768]{1,0:T(8,128)(2,1)S(1)}, bf16[384,768]{1,0:T(8,128)(2,1)S(1)}, u32[]{:S(2)}, u32[]{:S(2)}) collective-permute-start(bf16[384,768]{1,0:T(8,128)(2,1)S(1)} %bitcast.13), channel_id=1, source_target_pairs={{0,1},{1,0},{2,3},{3,2},{4,5},{5,4},{6,7},{7,6},{8,9},{9,8},{10,11... | collective-permute-start | bytes 1769480 | tf_op jit(solution)/shard_map/ppermute | solution.py:259
  42.5 3.8 %copy-start.3 = (bf16[384,768]{1,0:T(8,128)(2,1)}, bf16[384,768]{1,0:T(8,128)(2,1)S(1)}, u32[]{:S(2)}) copy-start(bf16[384,768]{1,0:T(8,128)(2,1)S(1)} %collective-permute-done.2.other_ref) | copy-start | bytes 1769476
  46.4 10.5 %all-to-all-start.2 = ((f32[8,8,128]{2,1,0:T(8,128)}), f32[8,8,128]{2,1,0:T(8,128)S(1)}, u32[]{:S(2)}, u32[]{:S(2)}) async-start(f32[8,8,128]{2,1,0:T(8,128)} %get-tuple-element.27), calls=%async_computation.2 | async-start | bytes 65536 | tf_op jit(solution)/shard_map/all_to_all | solution.py:255
  52.6 3.0 %collective-permute-start.4 = (f32[8,128]{1,0:T(8,128)S(1)}, f32[8,128]{1,0:T(8,128)S(1)}, u32[]{:S(2)}, u32[]{:S(2)}) collective-permute-start(f32[8,128]{1,0:T(8,128)S(1)} %get-tuple-element.28.mine_ref), channel_id=1, source_target_pairs={{0,1},{1,0},{2,3},{3,2},{4,5},{5,4},{6,7},{7,6},{8,9},{9,8},{10,11... | collective-permute-start | bytes 12296 | tf_op jit(solution)/shard_map/ppermute | solution.py:259
  56.8 18.7 %all-to-all-start.3 = ((f32[16,8,128]{2,1,0:T(8,128)}), f32[16,8,128]{2,1,0:T(8,128)S(1)}, u32[]{:S(2)}, u32[]{:S(2)}) async-start(f32[16,8,128]{2,1,0:T(8,128)} %shard_map.64), calls=%async_computation.3 | async-start | bytes 131072 | tf_op jit(solution)/shard_map/all_to_all | solution.py:255
  65.3 9.4 %collective-permute-start.3 = (f32[8,128]{1,0:T(8,128)S(1)}, f32[8,128]{1,0:T(8,128)S(1)}, u32[]{:S(2)}, u32[]{:S(2)}) collective-permute-start(f32[8,128]{1,0:T(8,128)S(1)} %shard_map.63.row_ref), channel_id=1, source_target_pairs={{0,128},{128,0},{1,129},{129,1},{2,130},{130,2},{3,131},{131,3},{4... | collective-permute-start | bytes 12296 | tf_op jit(solution)/shard_map/ppermute | solution.py:259
  75.5 1.1 copy-start.4
  79.8 11.9 %all-to-all-start.4 = ((bf16[4,96,896]{2,1,0:T(8,128)(2,1)}), bf16[4,96,896]{2,1,0:T(8,128)(2,1)S(1)}, u32[]{:S(2)}, u32[]{:S(2)}) async-start(bf16[4,96,896]{2,1,0:T(8,128)(2,1)} %bitcast.6), calls=%async_computation.4 | async-start | bytes 1376256 | tf_op jit(solution)/shard_map/all_to_all | solution.py:255
  85.8 4.0 %collective-permute-start.5 = (bf16[384,896]{1,0:T(8,128)(2,1)S(1)}, bf16[384,896]{1,0:T(8,128)(2,1)S(1)}, u32[]{:S(2)}, u32[]{:S(2)}) collective-permute-start(bf16[384,896]{1,0:T(8,128)(2,1)S(1)} %get-tuple-element.31), channel_id=1, source_target_pairs={{0,1},{1,0},{2,3},{3,2},{4,5},{5,4},{6,7},{7,6},{8,9},{9,8},{10,11... | collective-permute-start | bytes 2064392 | tf_op jit(solution)/shard_map/ppermute | solution.py:259
  91.8 30.4 %all-to-all-start.5 = ((bf16[16,24,896]{2,1,0:T(8,128)(2,1)}), bf16[16,24,896]{2,1,0:T(8,128)(2,1)S(1)}, u32[]{:S(2)}, u32[]{:S(2)}) async-start(bf16[16,24,896]{2,1,0:T(8,128)(2,1)} %bitcast.8), calls=%async_computation.5 | async-start | bytes 1376256 | tf_op jit(solution)/shard_map/all_to_all | solution.py:255
  100.8 7.4 %collective-permute-start.6 = (bf16[48,896]{1,0:T(8,128)(2,1)S(1)}, bf16[48,896]{1,0:T(8,128)(2,1)S(1)}, u32[]{:S(2)}, u32[]{:S(2)}) collective-permute-start(bf16[48,896]{1,0:T(8,128)(2,1)S(1)} %get-tuple-element.36), channel_id=1, source_target_pairs={{0,64},{64,0},{1,65},{65,1},{2,66},{66,2},{3,67},{67,3},{4,68},{68... | collective-permute-start | bytes 258056 | tf_op jit(solution)/shard_map/ppermute | solution.py:259
  108.3 9.8 %collective-permute-start.7 = (bf16[24,896]{1,0:T(8,128)(2,1)S(1)}, bf16[24,896]{1,0:T(8,128)(2,1)S(1)}, u32[]{:S(2)}, u32[]{:S(2)}) collective-permute-start(bf16[24,896]{1,0:T(8,128)(2,1)S(1)} %get-tuple-element.39), channel_id=1, source_target_pairs={{0,128},{128,0},{1,129},{129,1},{2,130},{130,2},{3,131},{131,3},{4... | collective-permute-start | bytes 129032 | tf_op jit(solution)/shard_map/ppermute | solution.py:259

commit v3 on v2

--- a/solution.py
+++ b/solution.py
@@ -11,9 +11,7 @@
 ALL = ("z0", "y2", "y1", "y0", "x", "zh", "c")
 INNER = ("z0", "y2", "y1", "y0")
 CHIPS = ("x", "zh")
-NEAR = ("z0", "y0")
-NEAR_STATS = ("z0", "y0", "y1")
-MIDDLE = "y1"
+NEAR = ("z0", "y0", "y1")
 FAR = "y2"
 CORE = "c"
 
@@ -22,6 +20,7 @@
 FIRST = (((0,), (0,)), ((), ()))
 VMEM_LIMIT = 24 * 1024 * 1024
 EXTRA = 128
+LOG2_E = 1.4426950408889634
 
 
 def f32_dot(a, b, dims):
@@ -105,22 +104,22 @@
 
 def lse_of(parts):
     peak = functools.reduce(jnp.maximum, [jnp.max(p, axis=0, keepdims=True) for p in parts])
-    total = sum(jnp.sum(jnp.exp(p - peak), axis=0, keepdims=True) for p in parts)
-    return peak + jnp.log(total)
+    total = sum(jnp.sum(jnp.exp2(p - peak), axis=0, keepdims=True) for p in parts)
+    return peak + jnp.log2(total)
 
 
 def pieces_lse(pieces):
     peak = jnp.max(pieces, axis=0)
-    return peak + jnp.log(jnp.sum(jnp.exp(pieces - peak[None]), axis=0))
+    return peak + jnp.log2(jnp.sum(jnp.exp2(pieces - peak[None]), axis=0))
 
 
 def pair_lse(a, b):
     peak = jnp.maximum(a, b)
-    return peak + jnp.log(jnp.exp(a - peak) + jnp.exp(b - peak))
+    return peak + jnp.log2(jnp.exp2(a - peak) + jnp.exp2(b - peak))
 
 
 def stats_kernel(factor_ref, image_ref, own_ref, other_ref, diagonal_ref, row_ref, col_ref):
-    factor = factor_ref[0]
+    factor = factor_ref[0] * LOG2_E
     image, own, other = image_ref[...], own_ref[...], other_ref[...]
     own_lse = lse_of([factor * f32_dot(image, own, LAST)])
     other_lse = lse_of([factor * f32_dot(image, other, LAST)])
@@ -138,14 +137,8 @@
     message_ref[...] = jnp.broadcast_to(message[None], message_ref.shape)
 
 
-def near_rows_kernel(pieces_ref, message_ref):
-    pieces = pieces_ref[...]
-    place = lax.broadcasted_iota(jnp.int32, (8, 128), 0)
-    message_ref[...] = jnp.where(place == 3, jnp.sum(pieces, axis=0), pieces_lse(pieces))
-
-
 def weights_kernel(
-    factor_ref, image_ref, own_ref, other_ref, row_ref, far_row_ref, pieces_ref,
+    factor_ref, image_ref, own_ref, other_ref, row_ref, pieces_ref,
     image_out, own_out, other_out, share_ref,
 ):
     factor = factor_ref[0]
@@ -153,9 +146,9 @@
     cols = pieces_lse(pieces_ref[...])
     own_lse, other_lse = line(cols[0:3]), line(cols[3:6])
     col_share = jnp.sum(own_lse) + jnp.sum(other_lse)
-    near, far = row_ref[...], far_row_ref[...]
-    rows = pair_lse(near[0:3], far[0:3])
-    row_share = jnp.sum(rows) - 2.0 * jnp.max(near[3:4] + far[3:4])
+    row_pieces = row_ref[...]
+    rows = pieces_lse(row_pieces)[0:3]
+    row_share = jnp.sum(rows) - 2.0 * jnp.max(jnp.sum(row_pieces, axis=0)[3:4])
     share_ref[...] = jnp.broadcast_to(row_share, share_ref.shape)
     row_lse = jnp.concatenate(
         [jnp.transpose(jnp.broadcast_to(rows[k : k + 1, :], (128, 128))) for k in range(3)], axis=0
@@ -164,9 +157,9 @@
     image_sum = None
     for text_ref, col_lse in ((own_ref, own_lse), (other_ref, other_lse)):
         text = text_ref[...]
-        logits = factor * f32_dot(image, text, LAST)
+        logits = (factor * LOG2_E) * f32_dot(image, text, LAST)
         weights = (
-            (0.5 * factor) * (jnp.exp(logits - row_lse) + jnp.exp(logits - col_lse))
+            (0.5 * factor) * (jnp.exp2(logits - row_lse) + jnp.exp2(logits - col_lse))
         ).astype(jnp.bfloat16)
         part = jnp.dot(weights, text, preferred_element_type=jnp.float32)
         image_sum = part if image_sum is None else image_sum + part
@@ -197,27 +190,16 @@
     return total
 
 
-def keep_and_send(total, share, side_ref, keep_ref, send_ref, share_ref):
+def near_sums_kernel(side_ref, pieces_ref, keep_ref, send_ref, share_ref):
     rows, width = keep_ref.shape
+    total = slabs_sum(pieces_ref, 2 * rows)
+    share = unpacked(total, width)
     first = side_ref[0] == 0
     lower, upper = total[:rows, :width], total[rows:, :width]
     keep_ref[...] = jnp.where(first, lower, upper)
     send_ref[:, :width] = jnp.where(first, upper, lower).astype(jnp.bfloat16)
     send_ref[:, width:] = packed(share, rows)
     share_ref[...] = jnp.broadcast_to(share, share_ref.shape)
-
-
-def near_sums_kernel(side_ref, pieces_ref, keep_ref, send_ref, share_ref):
-    rows, width = keep_ref.shape
-    total = slabs_sum(pieces_ref, 2 * rows)
-    keep_and_send(total, unpacked(total, width), side_ref, keep_ref, send_ref, share_ref)
-
-
-def middle_sums_kernel(side_ref, kept_ref, theirs_ref, shared_ref, keep_ref, send_ref, share_ref):
-    width = kept_ref.shape[1]
-    theirs = theirs_ref[...].astype(jnp.float32)
-    share = jnp.max(shared_ref[...]) + unpacked(theirs, width)
-    keep_and_send(kept_ref[...] + theirs[:, :width], share, side_ref, keep_ref, send_ref, share_ref)
 
 
 def gradient(factor, values, paired, total):
@@ -238,15 +220,14 @@
 
 
 def text_gradient_kernel(
-    factor_ref, values_ref, paired_ref, pieces_ref, shared_ref, gradient_ref, share_ref
+    whole, factor_ref, values_ref, paired_ref, pieces_ref, shared_ref, gradient_ref, loss_ref
 ):
     rows, width = values_ref.shape
     total = slabs_sum(pieces_ref, rows)
     gradient_ref[...] = gradient(
         factor_ref[0], values_ref[...], paired_ref[...], total[:, :width]
     )
-    share = jnp.max(shared_ref[...]) + unpacked(total, width)
-    share_ref[...] = jnp.broadcast_to(share, share_ref.shape)
+    loss_ref[0] = (jnp.max(shared_ref[...]) + unpacked(total, width)) * (1.0 / (LOG2_E * whole))
 
 
 def exchanged(blocks, axis):
@@ -273,12 +254,12 @@
 
 def on_device(image_emb, text_emb, factor):
     own_rows, width = image_emb.shape
-    inner, chips, near = (lax.axis_size(a) for a in (INNER, CHIPS, NEAR))
+    inner, chips = lax.axis_size(INNER), lax.axis_size(CHIPS)
     bf16, f32 = jnp.bfloat16, jnp.float32
     image_rows, text_rows = own_rows * inner, own_rows * chips
     wide = width + EXTRA
     work = 2 * image_rows * text_rows * width
-    middle, far = place(MIDDLE), place(FAR)
+    far = place(FAR)
     tile = shape((8, 128), f32)
 
     text_copies = kernel_call(text_units_kernel, shape((text_rows, width), bf16), text_emb)
@@ -287,26 +268,22 @@
     half, diagonal = kernel_call(
         image_units_kernel, (shape((own_rows, width), bf16), tile), image_emb, text_emb
     )
-    two = kernel_call(
-        join_kernel, shape((2 * own_rows, width), bf16), far, half, swapped(half, FAR)
-    )
     image_copies = kernel_call(
-        join_kernel, shape((image_rows, width), bf16), middle, two, swapped(two, MIDDLE)
+        join_kernel, shape((image_rows, width), bf16), far, half, swapped(half, FAR)
     )
     image_group = exchanged(after(image_copies, text_own), NEAR)
 
     row_message, col_part = kernel_call(
         stats_kernel,
-        (shape((lax.axis_size(NEAR_STATS), 8, 128), f32), tile),
+        (shape((inner, 8, 128), f32), tile),
         factor, image_group, text_own, text_other, diagonal,
         flops=4 * work,
     )
-    row_pieces = exchanged(row_message, NEAR_STATS)
+    row_pieces = exchanged(row_message, INNER)
     col_message = kernel_call(
         pair_columns_kernel, shape((chips, 8, 128), f32), col_part, swapped(col_part, CORE)
     )
     col_pieces = exchanged(after(col_message, row_pieces), CHIPS)
-    near_rows = kernel_call(near_rows_kernel, tile, row_pieces)
 
     image_part, own_part, other_part, row_share = kernel_call(
         weights_kernel,
@@ -316,7 +293,7 @@
             shape((text_rows, wide), bf16),
             tile,
         ),
-        factor, image_group, text_own, text_other, near_rows, swapped(near_rows, FAR), col_pieces,
+        factor, image_group, text_own, text_other, row_pieces, col_pieces,
         flops=6 * work,
     )
     image_pieces = exchanged(image_part, NEAR)
@@ -328,24 +305,20 @@
 
     kept, sent, share = kernel_call(
         near_sums_kernel,
-        (shape((2 * own_rows, width), f32), shape((2 * own_rows, wide), bf16), tile),
-        middle, image_pieces,
-    )
-    kept, sent, share = kernel_call(
-        middle_sums_kernel,
         (shape((own_rows, width), f32), shape((own_rows, wide), bf16), tile),
-        far, kept, swapped(sent, MIDDLE), share,
+        far, image_pieces,
     )
     out = shape((own_rows, width), f32)
     image_grad, share = kernel_call(
         image_gradient_kernel, (out, tile),
         factor, image_emb, text_emb, kept, swapped(sent, FAR), share,
     )
-    text_grad, share = kernel_call(
-        text_gradient_kernel, (out, tile), factor, text_emb, image_emb, text_pieces, share
-    )
     whole = 2.0 * own_rows * inner * chips * lax.axis_size(CORE)
-    return ((share[0, 0] / whole).reshape(1), image_grad, text_grad)
+    text_grad, mean_loss = kernel_call(
+        functools.partial(text_gradient_kernel, whole), (out, shape((1,), f32)),
+        factor, text_emb, image_emb, text_pieces, share,
+    )
+    return (mean_loss, image_grad, text_grad)
 
 
 def solution(mesh):

time: 126 us -> 134 us (1.063)
  the two profiles are of different devices: /device:TPU:72 before, /device:TPU:8 now
where the time goes in v3:
time: 134 us; the launch traced here: 133 us
  starting transfers between devices  52.7 us (39%)
  waiting for transfers between devices  51.1 us (38%)
  blocking collectives  15.7 us (12%)
  Pallas kernels  10.5 us (8%)
  local copies, waits for them, and re-layouts  1.95 us (1%)
  between operations  1.39 us (1%)
    all_to_all x5, waiting for transfers between devices, exchanged(): lax.all_to_all(split, axis, split_axis=0, concat_axis=0, tiled=True)  38.2 us
    all_to_all x5, starting transfers between devices, exchanged(): lax.all_to_all(split, axis, split_axis=0, concat_axis=0, tiled=True)  35.6 us
    ppermute x5, starting transfers between devices, swapped(): return lax.ppermute(x, axis, [(0, 1), (1, 0)])  17 us
    all_to_all x1, blocking collectives, exchanged(): lax.all_to_all(split, axis, split_axis=0, concat_axis=0, tiled=True)  15.7 us
    ppermute x5, waiting for transfers between devices, swapped(): return lax.ppermute(x, axis, [(0, 1), (1, 0)])  12.9 us
    pallas_call x10, Pallas kernels, kernel_call(): pl.pallas_call(body, out_shape=out_shape, in_specs=[spec(a) for a in args...  10.5 us
  transfers between devices with their start and end apart: 10, of which 10 were waited for; matrix products, arithmetic and copies ran while one was open for 0% of the time, Pallas kernels for 2%

profile of v3, /device:TPU:8, one launch (start us, length us, event | category | flops | bytes accessed | tf_op | source)
XLA Modules:
  0.0 133.4 jit_solution(171097460290050966)
XLA Ops:
  0.6 0.0 copy-start
  0.6 0.9 copy-done
  1.5 0.0 copy-start.1
  1.5 0.0 copy-start.2
  1.5 1.0 shard_map.60
  2.5 12.9 %all-to-all-start = ((bf16[16,24,768]{2,1,0:T(8,128)(2,1)}), bf16[16,24,768]{2,1,0:T(8,128)(2,1)S(1)}, u32[]{:S(2)}, u32[]{:S(2)}) async-start(bf16[16,24,768]{2,1,0:T(8,128)(2,1)} %bitcast.1), calls=%async_computation | async-start | bytes 1179648 | tf_op jit(solution)/shard_map/all_to_all | solution.py:236
  15.4 0.0 copy-done.1
  15.4 0.0 copy-done.2
  15.4 0.2 shard_map.58
  15.6 6.8 %collective-permute-start = (bf16[24,768]{1,0:T(8,128)(2,1)S(1)}, bf16[24,768]{1,0:T(8,128)(2,1)S(1)}, u32[]{:S(2)}, u32[]{:S(2)}) collective-permute-start(bf16[24,768]{1,0:T(8,128)(2,1)S(1)} %get-tuple-element.21.mine_ref), channel_id=1, source_target_pairs={{0,128},{128,0},{1,129},{129,1},{2,130},{130,2},{3,131},{131,3},{4... | collective-permute-start | bytes 110600 | tf_op jit(solution)/shard_map/ppermute | solution.py:240
  22.5 3.0 %collective-permute-done.theirs_ref = bf16[24,768]{1,0:T(8,128)(2,1)S(1)} collective-permute-done((bf16[24,768]{1,0:T(8,128)(2,1)S(1)}, bf16[24,768]{1,0:T(8,128)(2,1)S(1)}, u32[]{:S(2)}, u32[]{:S(2)}) %collective-permute-start) | collective-permute-done | bytes 36896 | tf_op jit(solution)/shard_map/ppermute | solution.py:240
  25.5 0.9 shard_map.59
  26.4 6.3 %all-to-all-done = bf16[16,24,768]{2,1,0:T(8,128)(2,1)S(1)} async-done(((bf16[16,24,768]{2,1,0:T(8,128)(2,1)}), bf16[16,24,768]{2,1,0:T(8,128)(2,1)S(1)}, u32[]{:S(2)}, u32[]{:S(2)}) %all-to-all-start) | async-done | bytes 589856 | tf_op jit(solution)/shard_map/all_to_all | solution.py:236
  32.7 8.9 %all-to-all-start.1 = ((bf16[8,48,768]{2,1,0:T(8,128)(2,1)}), bf16[8,48,768]{2,1,0:T(8,128)(2,1)S(1)}, u32[]{:S(2)}, u32[]{:S(2)}) async-start(bf16[8,48,768]{2,1,0:T(8,128)(2,1)} %bitcast.3), calls=%async_computation.1 | async-start | bytes 1179648 | tf_op jit(solution)/shard_map/all_to_all | solution.py:236
  41.6 1.9 %collective-permute-start.1 = (bf16[384,768]{1,0:T(8,128)(2,1)S(1)}, bf16[384,768]{1,0:T(8,128)(2,1)S(1)}, u32[]{:S(2)}, u32[]{:S(2)}) collective-permute-start(bf16[384,768]{1,0:T(8,128)(2,1)S(1)} %bitcast.11), channel_id=1, source_target_pairs={{0,1},{1,0},{2,3},{3,2},{4,5},{5,4},{6,7},{7,6},{8,9},{9,8},{10,11... | collective-permute-start | bytes 1769480 | tf_op jit(solution)/shard_map/ppermute | solution.py:240
  44.2 1.3 collective-permute-done.1.other_ref
  45.5 0.0 copy-start.3
  45.5 8.8 %all-to-all-done.1 = bf16[8,48,768]{2,1,0:T(8,128)(2,1)S(1)} async-done(((bf16[8,48,768]{2,1,0:T(8,128)(2,1)}), bf16[8,48,768]{2,1,0:T(8,128)(2,1)S(1)}, u32[]{:S(2)}, u32[]{:S(2)}) %all-to-all-start.1) | async-done | bytes 589856 | tf_op jit(solution)/shard_map/all_to_all | solution.py:236
  54.3 2.2 %shard_map.61 = (f32[16,8,128]{2,1,0:T(8,128)}, f32[8,128]{1,0:T(8,128)S(1)}) custom-call(f32[1]{0:T(128)S(6)} %copy.6.factor_ref, bf16[384,768]{1,0:T(8,128)(2,1)S(1)} %bitcast.14, bf16[384,768]{1,0:T(8,128)(2,1)S(1)} %bitcast.12, bf16[384,768]{1,0:T(8,128)(2,1)S(1)} %collective-permute-done.1.other_ref, f32[8,128]{1,0:T(8,128)S(1)} %get-tuple-element.23.diagonal_ref), custom_call_target="tpu_custom_call" | custom-call | flops 905969664 | bytes 1843204 | tf_op jit(solution)/shard_map/pallas_call | solution.py:41
  56.5 0.0 copy-done.3
  56.5 5.8 %all-to-all-start.2 = ((f32[16,8,128]{2,1,0:T(8,128)}), f32[16,8,128]{2,1,0:T(8,128)S(1)}, u32[]{:S(2)}, u32[]{:S(2)}) async-start(f32[16,8,128]{2,1,0:T(8,128)} %get-tuple-element.24), calls=%async_computation.2 | async-start | bytes 131072 | tf_op jit(solution)/shard_map/all_to_all | solution.py:236
  62.3 1.9 %collective-permute-start.2 = (f32[8,128]{1,0:T(8,128)S(1)}, f32[8,128]{1,0:T(8,128)S(1)}, u32[]{:S(2)}, u32[]{:S(2)}) collective-permute-start(f32[8,128]{1,0:T(8,128)S(1)} %get-tuple-element.25.mine_ref), channel_id=1, source_target_pairs={{0,1},{1,0},{2,3},{3,2},{4,5},{5,4},{6,7},{7,6},{8,9},{9,8},{10,11... | collective-permute-start | bytes 12296 | tf_op jit(solution)/shard_map/ppermute | solution.py:240
  64.2 1.1 collective-permute-done.2.theirs_ref
  65.4 4.5 %all-to-all-done.2.row_ref = f32[16,8,128]{2,1,0:T(8,128)S(1)} async-done(((f32[16,8,128]{2,1,0:T(8,128)}), f32[16,8,128]{2,1,0:T(8,128)S(1)}, u32[]{:S(2)}, u32[]{:S(2)}) %all-to-all-start.2) | async-done | bytes 65568 | tf_op jit(solution)/shard_map/all_to_all | solution.py:236
  69.9 15.7 %all_to_all.30.pieces_ref = f32[16,8,128]{2,1,0:T(8,128)S(1)} all-to-all(f32[16,8,128]{2,1,0:T(8,128)S(1)} %shard_map.62), channel_id=1, replica_groups=mesh['z0'=2,'y2'=2,'y1'=2,'y0'=2,'x'=4,'zh'=4,'c'=2] {'x','zh'}, dimensions={0} | all-to-all | bytes 131072 | tf_op jit(solution)/shard_map/all_to_all | solution.py:236
  85.6 0.0 copy-start.4
  85.6 1.1 copy-done.4
  86.7 3.2 %shard_map.63 = (bf16[384,896]{1,0:T(8,128)(2,1)}, f32[384,768]{1,0:T(8,128)S(1)}, bf16[384,896]{1,0:T(8,128)(2,1)S(1)}, f32[8,128]{1,0:T(8,128)S(1)}) custom-call(f32[1]{0:T(128)S(6)} %copy.6.factor_ref, bf16[384,768]{1,0:T(8,128)(2,1)S(1)} %bitcast.15, bf16[384,768]{1,0:T(8,128)(2,1)S(1)} %bitcast.13, bf16[384,768]{1,0:T(8,128)(2,1)S(1)} %copy-done.4, ...), custom_call_target="tpu_custom_call" | custom-call | flops 1358954496 | bytes 4460548 | tf_op jit(solution)/shard_map/pallas_call | solution.py:41
  89.9 4.5 %all-to-all-start.4 = ((bf16[8,48,896]{2,1,0:T(8,128)(2,1)}), bf16[8,48,896]{2,1,0:T(8,128)(2,1)S(1)}, u32[]{:S(2)}, u32[]{:S(2)}) async-start(bf16[8,48,896]{2,1,0:T(8,128)(2,1)} %bitcast.5), calls=%async_computation.4 | async-start | bytes 1376256 | tf_op jit(solution)/shard_map/all_to_all | solution.py:236
  94.4 1.9 %collective-permute-start.3 = (bf16[384,896]{1,0:T(8,128)(2,1)S(1)}, bf16[384,896]{1,0:T(8,128)(2,1)S(1)}, u32[]{:S(2)}, u32[]{:S(2)}) collective-permute-start(bf16[384,896]{1,0:T(8,128)(2,1)S(1)} %get-tuple-element.28), channel_id=1, source_target_pairs={{0,1},{1,0},{2,3},{3,2},{4,5},{5,4},{6,7},{7,6},{8,9},{9,8},{10,11... | collective-permute-start | bytes 2064392 | tf_op jit(solution)/shard_map/ppermute | solution.py:240
  96.3 2.1 %collective-permute-done.3.theirs_ref = bf16[384,896]{1,0:T(8,128)(2,1)S(1)} collective-permute-done((bf16[384,896]{1,0:T(8,128)(2,1)S(1)}, bf16[384,896]{1,0:T(8,128)(2,1)S(1)}, u32[]{:S(2)}, u32[]{:S(2)}) %collective-permute-start.3) | collective-permute-done | bytes 688160 | tf_op jit(solution)/shard_map/ppermute | solution.py:240
  98.4 1.1 shard_map.64
  99.6 8.6 %all-to-all-done.4 = bf16[8,48,896]{2,1,0:T(8,128)(2,1)S(1)} async-done(((bf16[8,48,896]{2,1,0:T(8,128)(2,1)}), bf16[8,48,896]{2,1,0:T(8,128)(2,1)S(1)}, u32[]{:S(2)}, u32[]{:S(2)}) %all-to-all-start.4) | async-done | bytes 688160 | tf_op jit(solution)/shard_map/all_to_all | solution.py:236
  108.1 3.6 %all-to-all-start.5 = ((bf16[16,24,896]{2,1,0:T(8,128)(2,1)}), bf16[16,24,896]{2,1,0:T(8,128)(2,1)S(1)}, u32[]{:S(2)}, u32[]{:S(2)}) async-start(bf16[16,24,896]{2,1,0:T(8,128)(2,1)} %bitcast.7), calls=%async_computation.5 | async-start | bytes 1376256 | tf_op jit(solution)/shard_map/all_to_all | solution.py:236
  111.8 0.2 shard_map.65
  111.9 4.5 %collective-permute-start.4 = (bf16[24,896]{1,0:T(8,128)(2,1)S(1)}, bf16[24,896]{1,0:T(8,128)(2,1)S(1)}, u32[]{:S(2)}, u32[]{:S(2)}) collective-permute-start(bf16[24,896]{1,0:T(8,128)(2,1)S(1)} %get-tuple-element.33), channel_id=1, source_target_pairs={{0,128},{128,0},{1,129},{129,1},{2,130},{130,2},{3,131},{131,3},{4... | collective-permute-start | bytes 129032 | tf_op jit(solution)/shard_map/ppermute | solution.py:240
  116.4 5.3 %collective-permute-done.4.theirs_ref = bf16[24,896]{1,0:T(8,128)(2,1)S(1)} collective-permute-done((bf16[24,896]{1,0:T(8,128)(2,1)S(1)}, bf16[24,896]{1,0:T(8,128)(2,1)S(1)}, u32[]{:S(2)}, u32[]{:S(2)}) %collective-permute-start.4) | collective-permute-done | bytes 43040 | tf_op jit(solution)/shard_map/ppermute | solution.py:240
  121.7 0.8 shard_map.66
  122.6 10.0 %all-to-all-done.5 = bf16[16,24,896]{2,1,0:T(8,128)(2,1)S(1)} async-done(((bf16[16,24,896]{2,1,0:T(8,128)(2,1)}), bf16[16,24,896]{2,1,0:T(8,128)(2,1)S(1)}, u32[]{:S(2)}, u32[]{:S(2)}) %all-to-all-start.5) | async-done | bytes 688160 | tf_op jit(solution)/shard_map/all_to_all | solution.py:236
  132.5 0.8 shard_map.67
  (1 shorter events, 0.0 us)
Async XLA Ops:
  0.6 0.9 copy-start
  1.5 13.8 %copy-start.1 = (f32[24,768]{1,0:T(8,128)S(1)}, f32[24,768]{1,0:T(8,128)}, u32[]{:S(2)}) copy-start(f32[24,768]{1,0:T(8,128)} %values_ref.7) | copy-start | bytes 221188
  1.5 13.9 %copy-start.2 = (f32[24,768]{1,0:T(8,128)S(1)}, f32[24,768]{1,0:T(8,128)}, u32[]{:S(2)}) copy-start(f32[24,768]{1,0:T(8,128)} %paired_ref.3) | copy-start | bytes 221188
  2.5 30.2 %all-to-all-start = ((bf16[16,24,768]{2,1,0:T(8,128)(2,1)}), bf16[16,24,768]{2,1,0:T(8,128)(2,1)S(1)}, u32[]{:S(2)}, u32[]{:S(2)}) async-start(bf16[16,24,768]{2,1,0:T(8,128)(2,1)} %bitcast.1), calls=%async_computation | async-start | bytes 1179648 | tf_op jit(solution)/shard_map/all_to_all | solution.py:236
  15.6 9.9 %collective-permute-start = (bf16[24,768]{1,0:T(8,128)(2,1)S(1)}, bf16[24,768]{1,0:T(8,128)(2,1)S(1)}, u32[]{:S(2)}, u32[]{:S(2)}) collective-permute-start(bf16[24,768]{1,0:T(8,128)(2,1)S(1)} %get-tuple-element.21.mine_ref), channel_id=1, source_target_pairs={{0,128},{128,0},{1,129},{129,1},{2,130},{130,2},{3,131},{131,3},{4... | collective-permute-start | bytes 110600 | tf_op jit(solution)/shard_map/ppermute | solution.py:240
  32.7 21.6 %all-to-all-start.1 = ((bf16[8,48,768]{2,1,0:T(8,128)(2,1)}), bf16[8,48,768]{2,1,0:T(8,128)(2,1)S(1)}, u32[]{:S(2)}, u32[]{:S(2)}) async-start(bf16[8,48,768]{2,1,0:T(8,128)(2,1)} %bitcast.3), calls=%async_computation.1 | async-start | bytes 1179648 | tf_op jit(solution)/shard_map/all_to_all | solution.py:236
  41.6 3.9 %collective-permute-start.1 = (bf16[384,768]{1,0:T(8,128)(2,1)S(1)}, bf16[384,768]{1,0:T(8,128)(2,1)S(1)}, u32[]{:S(2)}, u32[]{:S(2)}) collective-permute-start(bf16[384,768]{1,0:T(8,128)(2,1)S(1)} %bitcast.11), channel_id=1, source_target_pairs={{0,1},{1,0},{2,3},{3,2},{4,5},{5,4},{6,7},{7,6},{8,9},{9,8},{10,11... | collective-permute-start | bytes 1769480 | tf_op jit(solution)/shard_map/ppermute | solution.py:240
  45.5 11.0 %copy-start.3 = (bf16[384,768]{1,0:T(8,128)(2,1)}, bf16[384,768]{1,0:T(8,128)(2,1)S(1)}, u32[]{:S(2)}) copy-start(bf16[384,768]{1,0:T(8,128)(2,1)S(1)} %collective-permute-done.1.other_ref) | copy-start | bytes 1769476
  56.5 13.4 %all-to-all-start.2 = ((f32[16,8,128]{2,1,0:T(8,128)}), f32[16,8,128]{2,1,0:T(8,128)S(1)}, u32[]{:S(2)}, u32[]{:S(2)}) async-start(f32[16,8,128]{2,1,0:T(8,128)} %get-tuple-element.24), calls=%async_computation.2 | async-start | bytes 131072 | tf_op jit(solution)/shard_map/all_to_all | solution.py:236
  62.3 3.0 %collective-permute-start.2 = (f32[8,128]{1,0:T(8,128)S(1)}, f32[8,128]{1,0:T(8,128)S(1)}, u32[]{:S(2)}, u32[]{:S(2)}) collective-permute-start(f32[8,128]{1,0:T(8,128)S(1)} %get-tuple-element.25.mine_ref), channel_id=1, source_target_pairs={{0,1},{1,0},{2,3},{3,2},{4,5},{5,4},{6,7},{7,6},{8,9},{9,8},{10,11... | collective-permute-start | bytes 12296 | tf_op jit(solution)/shard_map/ppermute | solution.py:240
  85.6 1.1 copy-start.4
  89.9 18.2 %all-to-all-start.4 = ((bf16[8,48,896]{2,1,0:T(8,128)(2,1)}), bf16[8,48,896]{2,1,0:T(8,128)(2,1)S(1)}, u32[]{:S(2)}, u32[]{:S(2)}) async-start(bf16[8,48,896]{2,1,0:T(8,128)(2,1)} %bitcast.5), calls=%async_computation.4 | async-start | bytes 1376256 | tf_op jit(solution)/shard_map/all_to_all | solution.py:236
  94.4 4.0 %collective-permute-start.3 = (bf16[384,896]{1,0:T(8,128)(2,1)S(1)}, bf16[384,896]{1,0:T(8,128)(2,1)S(1)}, u32[]{:S(2)}, u32[]{:S(2)}) collective-permute-start(bf16[384,896]{1,0:T(8,128)(2,1)S(1)} %get-tuple-element.28), channel_id=1, source_target_pairs={{0,1},{1,0},{2,3},{3,2},{4,5},{5,4},{6,7},{7,6},{8,9},{9,8},{10,11... | collective-permute-start | bytes 2064392 | tf_op jit(solution)/shard_map/ppermute | solution.py:240
  108.1 24.4 %all-to-all-start.5 = ((bf16[16,24,896]{2,1,0:T(8,128)(2,1)}), bf16[16,24,896]{2,1,0:T(8,128)(2,1)S(1)}, u32[]{:S(2)}, u32[]{:S(2)}) async-start(bf16[16,24,896]{2,1,0:T(8,128)(2,1)} %bitcast.7), calls=%async_computation.5 | async-start | bytes 1376256 | tf_op jit(solution)/shard_map/all_to_all | solution.py:236
  111.9 9.8 %collective-permute-start.4 = (bf16[24,896]{1,0:T(8,128)(2,1)S(1)}, bf16[24,896]{1,0:T(8,128)(2,1)S(1)}, u32[]{:S(2)}, u32[]{:S(2)}) collective-permute-start(bf16[24,896]{1,0:T(8,128)(2,1)S(1)} %get-tuple-element.33), channel_id=1, source_target_pairs={{0,128},{128,0},{1,129},{129,1},{2,130},{130,2},{3,131},{131,3},{4... | collective-permute-start | bytes 129032 | tf_op jit(solution)/shard_map/ppermute | solution.py:240

commit v4 on v3

--- a/solution.py
+++ b/solution.py
@@ -11,8 +11,8 @@
 ALL = ("z0", "y2", "y1", "y0", "x", "zh", "c")
 INNER = ("z0", "y2", "y1", "y0")
 CHIPS = ("x", "zh")
-NEAR = ("z0", "y0", "y1")
-FAR = "y2"
+NEAR = ("z0", "y0")
+FAR = ("y2", "y1")
 CORE = "c"
 
 EPSILON = 1e-06
@@ -78,15 +78,22 @@
     diagonal_ref[...] = jnp.broadcast_to(jnp.sum(products), diagonal_ref.shape)
 
 
-def join_kernel(side_ref, mine_ref, theirs_ref, joined_ref):
-    mine, theirs = mine_ref[...].astype(jnp.float32), theirs_ref[...].astype(jnp.float32)
-    first = side_ref[0] == 0
-    joined = jnp.concatenate(
-        [jnp.where(first, mine, theirs), jnp.where(first, theirs, mine)], axis=0
-    ).astype(jnp.bfloat16)
-    rows = joined.shape[0]
-    for k in range(joined_ref.shape[0] // rows):
-        joined_ref[k * rows : (k + 1) * rows, :] = joined
+def chosen(number, blocks):
+    found = blocks[0]
+    for k in range(1, len(blocks)):
+        found = jnp.where(number == k, blocks[k], found)
+    return found
+
+
+def join_kernel(place_ref, *refs):
+    *block_refs, joined_ref = refs
+    blocks = [ref[...].astype(jnp.float32) for ref in block_refs]
+    ordered = [chosen(place_ref[0] ^ k, blocks) for k in range(len(blocks))]
+    rows = 2 * blocks[0].shape[0]
+    for pair in range(len(blocks) // 2):
+        half = jnp.concatenate(ordered[2 * pair : 2 * pair + 2], axis=0).astype(jnp.bfloat16)
+        for at in range(pair * rows, joined_ref.shape[0], rows * len(blocks) // 2):
+            joined_ref[at : at + rows, :] = half
 
 
 def lines(row):
@@ -190,15 +197,17 @@
     return total
 
 
-def near_sums_kernel(side_ref, pieces_ref, keep_ref, send_ref, share_ref):
+def near_sums_kernel(place_ref, pieces_ref, keep_ref, *refs):
+    *send_refs, share_ref = refs
     rows, width = keep_ref.shape
-    total = slabs_sum(pieces_ref, 2 * rows)
+    count = len(send_refs) + 1
+    total = slabs_sum(pieces_ref, count * rows)
     share = unpacked(total, width)
-    first = side_ref[0] == 0
-    lower, upper = total[:rows, :width], total[rows:, :width]
-    keep_ref[...] = jnp.where(first, lower, upper)
-    send_ref[:, :width] = jnp.where(first, upper, lower).astype(jnp.bfloat16)
-    send_ref[:, width:] = packed(share, rows)
+    blocks = [total[k * rows : (k + 1) * rows, :width] for k in range(count)]
+    keep_ref[...] = chosen(place_ref[0], blocks)
+    for k, send_ref in enumerate(send_refs):
+        send_ref[:, :width] = chosen(place_ref[0] ^ (k + 1), blocks).astype(jnp.bfloat16)
+        send_ref[:, width:] = packed(share, rows)
     share_ref[...] = jnp.broadcast_to(share, share_ref.shape)
 
 
@@ -209,13 +218,18 @@
 
 
 def image_gradient_kernel(
-    factor_ref, values_ref, paired_ref, kept_ref, theirs_ref, shared_ref, gradient_ref, share_ref
+    factor_ref, values_ref, paired_ref, kept_ref, shared_ref, first_ref, second_ref, third_ref,
+    gradient_ref, share_ref,
 ):
     width = kept_ref.shape[1]
-    theirs = theirs_ref[...].astype(jnp.float32)
-    total = kept_ref[...] + theirs[:, :width]
+    first, second, third = (
+        ref[...].astype(jnp.float32) for ref in (first_ref, second_ref, third_ref)
+    )
+    total = (kept_ref[...] + first[:, :width]) + (second[:, :width] + third[:, :width])
     gradient_ref[...] = gradient(factor_ref[0], values_ref[...], paired_ref[...], total)
-    share = jnp.max(shared_ref[...]) + unpacked(theirs, width)
+    share = (jnp.max(shared_ref[...]) + unpacked(first, width)) + (
+        unpacked(second, width) + unpacked(third, width)
+    )
     share_ref[...] = jnp.broadcast_to(share, share_ref.shape)
 
 
@@ -236,8 +250,8 @@
     return lax.all_to_all(split, axis, split_axis=0, concat_axis=0, tiled=True).reshape(blocks.shape)
 
 
-def swapped(x, axis):
-    return lax.ppermute(x, axis, [(0, 1), (1, 0)])
+def swapped(x, axis, offset=1):
+    return lax.ppermute(x, axis, [(k, k ^ offset) for k in range(lax.axis_size(axis))])
 
 
 def after(x, first):
@@ -259,7 +273,7 @@
     image_rows, text_rows = own_rows * inner, own_rows * chips
     wide = width + EXTRA
     work = 2 * image_rows * text_rows * width
-    far = place(FAR)
+    far, fars = place(FAR), lax.axis_size(FAR)
     tile = shape((8, 128), f32)
 
     text_copies = kernel_call(text_units_kernel, shape((text_rows, width), bf16), text_emb)
@@ -269,7 +283,8 @@
         image_units_kernel, (shape((own_rows, width), bf16), tile), image_emb, text_emb
     )
     image_copies = kernel_call(
-        join_kernel, shape((image_rows, width), bf16), far, half, swapped(half, FAR)
+        join_kernel, shape((image_rows, width), bf16),
+        far, half, *(swapped(half, FAR, k) for k in range(1, fars)),
     )
     image_group = exchanged(after(image_copies, text_own), NEAR)
 
@@ -303,15 +318,15 @@
     )
     text_pieces = exchanged(after(text_part, image_pieces), CHIPS)
 
-    kept, sent, share = kernel_call(
-        near_sums_kernel,
-        (shape((own_rows, width), f32), shape((own_rows, wide), bf16), tile),
-        far, image_pieces,
+    sent = [shape((own_rows, wide), bf16)] * (fars - 1)
+    kept, *sent, share = kernel_call(
+        near_sums_kernel, (shape((own_rows, width), f32), *sent, tile), far, image_pieces
     )
     out = shape((own_rows, width), f32)
     image_grad, share = kernel_call(
         image_gradient_kernel, (out, tile),
-        factor, image_emb, text_emb, kept, swapped(sent, FAR), share,
+        factor, image_emb, text_emb, kept, share,
+        *(swapped(block, FAR, k + 1) for k, block in enumerate(sent)),
     )
     whole = 2.0 * own_rows * inner * chips * lax.axis_size(CORE)
     text_grad, mean_loss = kernel_call(

time: 134 us -> 121 us (0.903)
  the two profiles are of different devices: /device:TPU:8 before, /device:TPU:72 now
where the time goes in v4:
time: 121 us
  starting transfers between devices  63.7 us (53%)
  waiting for transfers between devices  25.9 us (21%)
  blocking collectives  17 us (14%)
  Pallas kernels  10.5 us (9%)
  local copies, waits for them, and re-layouts  1.95 us (2%)
  between operations  1.44 us (1%)
    all_to_all x5, starting transfers between devices, exchanged(): lax.all_to_all(split, axis, split_axis=0, concat_axis=0, tiled=True)  33.6 us
    ppermute x9, starting transfers between devices, swapped(): lax.ppermute(x, axis, [(k, k ^ offset) for k in range(lax.axis_size(axis))])  30.2 us
    all_to_all x1, blocking collectives, exchanged(): lax.all_to_all(split, axis, split_axis=0, concat_axis=0, tiled=True)  17 us
    all_to_all x5, waiting for transfers between devices, exchanged(): lax.all_to_all(split, axis, split_axis=0, concat_axis=0, tiled=True)  13.8 us
    ppermute x9, waiting for transfers between devices, swapped(): lax.ppermute(x, axis, [(k, k ^ offset) for k in range(lax.axis_size(axis))])  12.1 us
    pallas_call x10, Pallas kernels, kernel_call(): pl.pallas_call(body, out_shape=out_shape, in_specs=[spec(a) for a in args...  10.5 us
  transfers between devices with their start and end apart: 14, of which 12 were waited for; matrix products, arithmetic and copies ran while one was open for 0% of the time, Pallas kernels for 3%

profile of v4, /device:TPU:72, one launch (start us, length us, event | category | flops | bytes accessed | tf_op | source)
XLA Modules:
  0.0 120.6 jit_solution(346791195911356205)
XLA Ops:
  0.6 0.0 copy-start
  0.6 0.9 copy-done
  1.5 0.0 copy-start.1
  1.5 0.0 copy-start.2
  1.5 1.0 shard_map.60
  2.5 12.0 %all-to-all-start = ((bf16[16,24,768]{2,1,0:T(8,128)(2,1)}), bf16[16,24,768]{2,1,0:T(8,128)(2,1)S(1)}, u32[]{:S(2)}, u32[]{:S(2)}) async-start(bf16[16,24,768]{2,1,0:T(8,128)(2,1)} %bitcast.1), calls=%async_computation | async-start | bytes 1179648 | tf_op jit(solution)/shard_map/all_to_all | solution.py:250
  14.5 0.0 copy-done.1
  14.5 0.0 copy-done.2
  14.5 0.2 shard_map.58
  14.7 5.3 %collective-permute-start.2 = (bf16[24,768]{1,0:T(8,128)(2,1)S(1)}, bf16[24,768]{1,0:T(8,128)(2,1)S(1)}, u32[]{:S(2)}, u32[]{:S(2)}) collective-permute-start(bf16[24,768]{1,0:T(8,128)(2,1)S(1)} %get-tuple-element.23.refs_0_), channel_id=1, source_target_pairs={{0,192},{64,128},{128,64},{192,0},{1,193},{65,129},{129,65},{193,1... | collective-permute-start | bytes 110600 | tf_op jit(solution)/shard_map/ppermute | solution.py:254
  20.0 4.7 %collective-permute-start.1 = (bf16[24,768]{1,0:T(8,128)(2,1)S(1)}, bf16[24,768]{1,0:T(8,128)(2,1)S(1)}, u32[]{:S(2)}, u32[]{:S(2)}) collective-permute-start(bf16[24,768]{1,0:T(8,128)(2,1)S(1)} %get-tuple-element.23.refs_0_), channel_id=1, source_target_pairs={{0,128},{64,192},{128,0},{192,64},{1,129},{65,193},{129,1},{193,65... | collective-permute-start | bytes 110600 | tf_op jit(solution)/shard_map/ppermute | solution.py:254
  24.7 2.2 %collective-permute-start = (bf16[24,768]{1,0:T(8,128)(2,1)S(1)}, bf16[24,768]{1,0:T(8,128)(2,1)S(1)}, u32[]{:S(2)}, u32[]{:S(2)}) collective-permute-start(bf16[24,768]{1,0:T(8,128)(2,1)S(1)} %get-tuple-element.23.refs_0_), channel_id=1, source_target_pairs={{0,64},{64,0},{128,192},{192,128},{1,65},{65,1},{129,193},{193,129... | collective-permute-start | bytes 110600 | tf_op jit(solution)/shard_map/ppermute | solution.py:254
  27.0 0.0 collective-permute-done.2.refs_3_
  27.0 3.0 %collective-permute-done.1.refs_2_ = bf16[24,768]{1,0:T(8,128)(2,1)S(1)} collective-permute-done((bf16[24,768]{1,0:T(8,128)(2,1)S(1)}, bf16[24,768]{1,0:T(8,128)(2,1)S(1)}, u32[]{:S(2)}, u32[]{:S(2)}) %collective-permute-start.1) | collective-permute-done | bytes 36896 | tf_op jit(solution)/shard_map/ppermute | solution.py:254
  30.0 1.4 %collective-permute-done.refs_1_ = bf16[24,768]{1,0:T(8,128)(2,1)S(1)} collective-permute-done((bf16[24,768]{1,0:T(8,128)(2,1)S(1)}, bf16[24,768]{1,0:T(8,128)(2,1)S(1)}, u32[]{:S(2)}, u32[]{:S(2)}) %collective-permute-start) | collective-permute-done | bytes 36896 | tf_op jit(solution)/shard_map/ppermute | solution.py:254
  31.5 0.9 shard_map.59
  32.3 2.1 %all-to-all-done = bf16[16,24,768]{2,1,0:T(8,128)(2,1)S(1)} async-done(((bf16[16,24,768]{2,1,0:T(8,128)(2,1)}), bf16[16,24,768]{2,1,0:T(8,128)(2,1)S(1)}, u32[]{:S(2)}, u32[]{:S(2)}) %all-to-all-start) | async-done | bytes 589856 | tf_op jit(solution)/shard_map/all_to_all | solution.py:250
  34.5 4.2 %all-to-all-start.1 = ((bf16[4,96,768]{2,1,0:T(8,128)(2,1)}), bf16[4,96,768]{2,1,0:T(8,128)(2,1)S(1)}, u32[]{:S(2)}, u32[]{:S(2)}) async-start(bf16[4,96,768]{2,1,0:T(8,128)(2,1)} %bitcast.3), calls=%async_computation.1 | async-start | bytes 1179648 | tf_op jit(solution)/shard_map/all_to_all | solution.py:250
  38.7 1.9 %collective-permute-start.3 = (bf16[384,768]{1,0:T(8,128)(2,1)S(1)}, bf16[384,768]{1,0:T(8,128)(2,1)S(1)}, u32[]{:S(2)}, u32[]{:S(2)}) collective-permute-start(bf16[384,768]{1,0:T(8,128)(2,1)S(1)} %bitcast.11), channel_id=1, source_target_pairs={{0,1},{1,0},{2,3},{3,2},{4,5},{5,4},{6,7},{7,6},{8,9},{9,8},{10,11... | collective-permute-start | bytes 1769480 | tf_op jit(solution)/shard_map/ppermute | solution.py:254
  41.2 1.3 %collective-permute-done.3.other_ref = bf16[384,768]{1,0:T(8,128)(2,1)S(1)} collective-permute-done((bf16[384,768]{1,0:T(8,128)(2,1)S(1)}, bf16[384,768]{1,0:T(8,128)(2,1)S(1)}, u32[]{:S(2)}, u32[]{:S(2)}) %collective-permute-start.3) | collective-permute-done | bytes 589856 | tf_op jit(solution)/shard_map/ppermute | solution.py:254
  42.5 0.0 copy-start.3
  42.5 1.6 %all-to-all-done.1 = bf16[4,96,768]{2,1,0:T(8,128)(2,1)S(1)} async-done(((bf16[4,96,768]{2,1,0:T(8,128)(2,1)}), bf16[4,96,768]{2,1,0:T(8,128)(2,1)S(1)}, u32[]{:S(2)}, u32[]{:S(2)}) %all-to-all-start.1) | async-done | bytes 589856 | tf_op jit(solution)/shard_map/all_to_all | solution.py:250
  44.1 2.2 %shard_map.61 = (f32[16,8,128]{2,1,0:T(8,128)}, f32[8,128]{1,0:T(8,128)S(1)}) custom-call(f32[1]{0:T(128)S(6)} %copy.6.factor_ref, bf16[384,768]{1,0:T(8,128)(2,1)S(1)} %bitcast.14, bf16[384,768]{1,0:T(8,128)(2,1)S(1)} %bitcast.12, bf16[384,768]{1,0:T(8,128)(2,1)S(1)} %collective-permute-done.3.other_ref, f32[8,128]{1,0:T(8,128)S(1)} %get-tuple-element.25.diagonal_ref), custom_call_target="tpu_custom_call" | custom-call | flops 905969664 | bytes 1843204 | tf_op jit(solution)/shard_map/pallas_call | solution.py:41
  46.3 0.0 copy-done.3
  46.4 8.6 %all-to-all-start.2 = ((f32[16,8,128]{2,1,0:T(8,128)}), f32[16,8,128]{2,1,0:T(8,128)S(1)}, u32[]{:S(2)}, u32[]{:S(2)}) async-start(f32[16,8,128]{2,1,0:T(8,128)} %get-tuple-element.26), calls=%async_computation.2 | async-start | bytes 131072 | tf_op jit(solution)/shard_map/all_to_all | solution.py:250
  55.0 1.9 %collective-permute-start.4 = (f32[8,128]{1,0:T(8,128)S(1)}, f32[8,128]{1,0:T(8,128)S(1)}, u32[]{:S(2)}, u32[]{:S(2)}) collective-permute-start(f32[8,128]{1,0:T(8,128)S(1)} %get-tuple-element.27.mine_ref), channel_id=1, source_target_pairs={{0,1},{1,0},{2,3},{3,2},{4,5},{5,4},{6,7},{7,6},{8,9},{9,8},{10,11... | collective-permute-start | bytes 12296 | tf_op jit(solution)/shard_map/ppermute | solution.py:254
  56.9 1.1 collective-permute-done.4.theirs_ref
  58.1 3.8 %all-to-all-done.2.row_ref = f32[16,8,128]{2,1,0:T(8,128)S(1)} async-done(((f32[16,8,128]{2,1,0:T(8,128)}), f32[16,8,128]{2,1,0:T(8,128)S(1)}, u32[]{:S(2)}, u32[]{:S(2)}) %all-to-all-start.2) | async-done | bytes 65568 | tf_op jit(solution)/shard_map/all_to_all | solution.py:250
  61.8 17.0 %all_to_all.30.pieces_ref = f32[16,8,128]{2,1,0:T(8,128)S(1)} all-to-all(f32[16,8,128]{2,1,0:T(8,128)S(1)} %shard_map.62), channel_id=1, replica_groups=mesh['z0'=2,'y2'=2,'y1'=2,'y0'=2,'x'=4,'zh'=4,'c'=2] {'x','zh'}, dimensions={0} | all-to-all | bytes 131072 | tf_op jit(solution)/shard_map/all_to_all | solution.py:250
  78.8 0.0 copy-start.4
  78.8 1.1 copy-done.4
  79.8 3.2 %shard_map.63 = (bf16[384,896]{1,0:T(8,128)(2,1)}, f32[384,768]{1,0:T(8,128)S(1)}, bf16[384,896]{1,0:T(8,128)(2,1)S(1)}, f32[8,128]{1,0:T(8,128)S(1)}) custom-call(f32[1]{0:T(128)S(6)} %copy.6.factor_ref, bf16[384,768]{1,0:T(8,128)(2,1)S(1)} %bitcast.15, bf16[384,768]{1,0:T(8,128)(2,1)S(1)} %bitcast.13, bf16[384,768]{1,0:T(8,128)(2,1)S(1)} %copy-done.4, ...), custom_call_target="tpu_custom_call" | custom-call | flops 1358954496 | bytes 4460548 | tf_op jit(solution)/shard_map/pallas_call | solution.py:41
  83.1 5.2 %all-to-all-start.4 = ((bf16[4,96,896]{2,1,0:T(8,128)(2,1)}), bf16[4,96,896]{2,1,0:T(8,128)(2,1)S(1)}, u32[]{:S(2)}, u32[]{:S(2)}) async-start(bf16[4,96,896]{2,1,0:T(8,128)(2,1)} %bitcast.5), calls=%async_computation.4 | async-start | bytes 1376256 | tf_op jit(solution)/shard_map/all_to_all | solution.py:250
  88.3 1.9 %collective-permute-start.5 = (bf16[384,896]{1,0:T(8,128)(2,1)S(1)}, bf16[384,896]{1,0:T(8,128)(2,1)S(1)}, u32[]{:S(2)}, u32[]{:S(2)}) collective-permute-start(bf16[384,896]{1,0:T(8,128)(2,1)S(1)} %get-tuple-element.30), channel_id=1, source_target_pairs={{0,1},{1,0},{2,3},{3,2},{4,5},{5,4},{6,7},{7,6},{8,9},{9,8},{10,11... | collective-permute-start | bytes 2064392 | tf_op jit(solution)/shard_map/ppermute | solution.py:254
  90.2 2.1 %collective-permute-done.5.theirs_ref = bf16[384,896]{1,0:T(8,128)(2,1)S(1)} collective-permute-done((bf16[384,896]{1,0:T(8,128)(2,1)S(1)}, bf16[384,896]{1,0:T(8,128)(2,1)S(1)}, u32[]{:S(2)}, u32[]{:S(2)}) %collective-permute-start.5) | collective-permute-done | bytes 688160 | tf_op jit(solution)/shard_map/ppermute | solution.py:254
  92.3 1.1 shard_map.64
  93.4 0.8 all-to-all-done.4
  94.2 3.6 %all-to-all-start.5 = ((bf16[16,24,896]{2,1,0:T(8,128)(2,1)}), bf16[16,24,896]{2,1,0:T(8,128)(2,1)S(1)}, u32[]{:S(2)}, u32[]{:S(2)}) async-start(bf16[16,24,896]{2,1,0:T(8,128)(2,1)} %bitcast.7), calls=%async_computation.5 | async-start | bytes 1376256 | tf_op jit(solution)/shard_map/all_to_all | solution.py:250
  97.9 0.2 shard_map.65
  98.0 2.9 %collective-permute-start.6 = (bf16[24,896]{1,0:T(8,128)(2,1)S(1)}, bf16[24,896]{1,0:T(8,128)(2,1)S(1)}, u32[]{:S(2)}, u32[]{:S(2)}) collective-permute-start(bf16[24,896]{1,0:T(8,128)(2,1)S(1)} %get-tuple-element.36), channel_id=1, source_target_pairs={{0,64},{64,0},{128,192},{192,128},{1,65},{65,1},{129,193},{193,129... | collective-permute-start | bytes 129032 | tf_op jit(solution)/shard_map/ppermute | solution.py:254
  101.0 4.3 %collective-permute-start.7 = (bf16[24,896]{1,0:T(8,128)(2,1)S(1)}, bf16[24,896]{1,0:T(8,128)(2,1)S(1)}, u32[]{:S(2)}, u32[]{:S(2)}) collective-permute-start(bf16[24,896]{1,0:T(8,128)(2,1)S(1)} %get-tuple-element.37), channel_id=1, source_target_pairs={{0,128},{64,192},{128,0},{192,64},{1,129},{65,193},{129,1},{193,65... | collective-permute-start | bytes 129032 | tf_op jit(solution)/shard_map/ppermute | solution.py:254
  105.3 5.0 %collective-permute-start.8 = (bf16[24,896]{1,0:T(8,128)(2,1)S(1)}, bf16[24,896]{1,0:T(8,128)(2,1)S(1)}, u32[]{:S(2)}, u32[]{:S(2)}) collective-permute-start(bf16[24,896]{1,0:T(8,128)(2,1)S(1)} %get-tuple-element.38), channel_id=1, source_target_pairs={{0,192},{64,128},{128,64},{192,0},{1,193},{65,129},{129,65},{193,1... | collective-permute-start | bytes 129032 | tf_op jit(solution)/shard_map/ppermute | solution.py:254
  110.3 0.0 collective-permute-done.6.first_ref
  110.3 0.6 collective-permute-done.7.second_ref
  110.9 2.4 %collective-permute-done.8.third_ref = bf16[24,896]{1,0:T(8,128)(2,1)S(1)} collective-permute-done((bf16[24,896]{1,0:T(8,128)(2,1)S(1)}, bf16[24,896]{1,0:T(8,128)(2,1)S(1)}, u32[]{:S(2)}, u32[]{:S(2)}) %collective-permute-start.8) | collective-permute-done | bytes 43040 | tf_op jit(solution)/shard_map/ppermute | solution.py:254
  113.3 0.8 shard_map.66
  114.2 5.5 %all-to-all-done.5 = bf16[16,24,896]{2,1,0:T(8,128)(2,1)S(1)} async-done(((bf16[16,24,896]{2,1,0:T(8,128)(2,1)}), bf16[16,24,896]{2,1,0:T(8,128)(2,1)S(1)}, u32[]{:S(2)}, u32[]{:S(2)}) %all-to-all-start.5) | async-done | bytes 688160 | tf_op jit(solution)/shard_map/all_to_all | solution.py:250
  119.7 0.8 shard_map.67
  (1 shorter events, 0.0 us)
Async XLA Ops:
  0.6 0.9 copy-start
  1.5 12.9 %copy-start.1 = (f32[24,768]{1,0:T(8,128)S(1)}, f32[24,768]{1,0:T(8,128)}, u32[]{:S(2)}) copy-start(f32[24,768]{1,0:T(8,128)} %values_ref.7) | copy-start | bytes 221188
  1.5 12.9 %copy-start.2 = (f32[24,768]{1,0:T(8,128)S(1)}, f32[24,768]{1,0:T(8,128)}, u32[]{:S(2)}) copy-start(f32[24,768]{1,0:T(8,128)} %paired_ref.3) | copy-start | bytes 221188
  2.5 32.0 %all-to-all-start = ((bf16[16,24,768]{2,1,0:T(8,128)(2,1)}), bf16[16,24,768]{2,1,0:T(8,128)(2,1)S(1)}, u32[]{:S(2)}, u32[]{:S(2)}) async-start(bf16[16,24,768]{2,1,0:T(8,128)(2,1)} %bitcast.1), calls=%async_computation | async-start | bytes 1179648 | tf_op jit(solution)/shard_map/all_to_all | solution.py:250
  14.7 12.3 %collective-permute-start.2 = (bf16[24,768]{1,0:T(8,128)(2,1)S(1)}, bf16[24,768]{1,0:T(8,128)(2,1)S(1)}, u32[]{:S(2)}, u32[]{:S(2)}) collective-permute-start(bf16[24,768]{1,0:T(8,128)(2,1)S(1)} %get-tuple-element.23.refs_0_), channel_id=1, source_target_pairs={{0,192},{64,128},{128,64},{192,0},{1,193},{65,129},{129,65},{193,1... | collective-permute-start | bytes 110600 | tf_op jit(solution)/shard_map/ppermute | solution.py:254
  20.0 10.0 %collective-permute-start.1 = (bf16[24,768]{1,0:T(8,128)(2,1)S(1)}, bf16[24,768]{1,0:T(8,128)(2,1)S(1)}, u32[]{:S(2)}, u32[]{:S(2)}) collective-permute-start(bf16[24,768]{1,0:T(8,128)(2,1)S(1)} %get-tuple-element.23.refs_0_), channel_id=1, source_target_pairs={{0,128},{64,192},{128,0},{192,64},{1,129},{65,193},{129,1},{193,65... | collective-permute-start | bytes 110600 | tf_op jit(solution)/shard_map/ppermute | solution.py:254
  24.7 6.8 %collective-permute-start = (bf16[24,768]{1,0:T(8,128)(2,1)S(1)}, bf16[24,768]{1,0:T(8,128)(2,1)S(1)}, u32[]{:S(2)}, u32[]{:S(2)}) collective-permute-start(bf16[24,768]{1,0:T(8,128)(2,1)S(1)} %get-tuple-element.23.refs_0_), channel_id=1, source_target_pairs={{0,64},{64,0},{128,192},{192,128},{1,65},{65,1},{129,193},{193,129... | collective-permute-start | bytes 110600 | tf_op jit(solution)/shard_map/ppermute | solution.py:254
  34.5 9.7 %all-to-all-start.1 = ((bf16[4,96,768]{2,1,0:T(8,128)(2,1)}), bf16[4,96,768]{2,1,0:T(8,128)(2,1)S(1)}, u32[]{:S(2)}, u32[]{:S(2)}) async-start(bf16[4,96,768]{2,1,0:T(8,128)(2,1)} %bitcast.3), calls=%async_computation.1 | async-start | bytes 1179648 | tf_op jit(solution)/shard_map/all_to_all | solution.py:250
  38.7 3.9 %collective-permute-start.3 = (bf16[384,768]{1,0:T(8,128)(2,1)S(1)}, bf16[384,768]{1,0:T(8,128)(2,1)S(1)}, u32[]{:S(2)}, u32[]{:S(2)}) collective-permute-start(bf16[384,768]{1,0:T(8,128)(2,1)S(1)} %bitcast.11), channel_id=1, source_target_pairs={{0,1},{1,0},{2,3},{3,2},{4,5},{5,4},{6,7},{7,6},{8,9},{9,8},{10,11... | collective-permute-start | bytes 1769480 | tf_op jit(solution)/shard_map/ppermute | solution.py:254
  42.5 3.8 %copy-start.3 = (bf16[384,768]{1,0:T(8,128)(2,1)}, bf16[384,768]{1,0:T(8,128)(2,1)S(1)}, u32[]{:S(2)}) copy-start(bf16[384,768]{1,0:T(8,128)(2,1)S(1)} %collective-permute-done.3.other_ref) | copy-start | bytes 1769476
  46.4 15.5 %all-to-all-start.2 = ((f32[16,8,128]{2,1,0:T(8,128)}), f32[16,8,128]{2,1,0:T(8,128)S(1)}, u32[]{:S(2)}, u32[]{:S(2)}) async-start(f32[16,8,128]{2,1,0:T(8,128)} %get-tuple-element.26), calls=%async_computation.2 | async-start | bytes 131072 | tf_op jit(solution)/shard_map/all_to_all | solution.py:250
  55.0 3.0 %collective-permute-start.4 = (f32[8,128]{1,0:T(8,128)S(1)}, f32[8,128]{1,0:T(8,128)S(1)}, u32[]{:S(2)}, u32[]{:S(2)}) collective-permute-start(f32[8,128]{1,0:T(8,128)S(1)} %get-tuple-element.27.mine_ref), channel_id=1, source_target_pairs={{0,1},{1,0},{2,3},{3,2},{4,5},{5,4},{6,7},{7,6},{8,9},{9,8},{10,11... | collective-permute-start | bytes 12296 | tf_op jit(solution)/shard_map/ppermute | solution.py:254
  78.8 1.1 copy-start.4
  83.1 11.2 %all-to-all-start.4 = ((bf16[4,96,896]{2,1,0:T(8,128)(2,1)}), bf16[4,96,896]{2,1,0:T(8,128)(2,1)S(1)}, u32[]{:S(2)}, u32[]{:S(2)}) async-start(bf16[4,96,896]{2,1,0:T(8,128)(2,1)} %bitcast.5), calls=%async_computation.4 | async-start | bytes 1376256 | tf_op jit(solution)/shard_map/all_to_all | solution.py:250
  88.3 4.0 %collective-permute-start.5 = (bf16[384,896]{1,0:T(8,128)(2,1)S(1)}, bf16[384,896]{1,0:T(8,128)(2,1)S(1)}, u32[]{:S(2)}, u32[]{:S(2)}) collective-permute-start(bf16[384,896]{1,0:T(8,128)(2,1)S(1)} %get-tuple-element.30), channel_id=1, source_target_pairs={{0,1},{1,0},{2,3},{3,2},{4,5},{5,4},{6,7},{7,6},{8,9},{9,8},{10,11... | collective-permute-start | bytes 2064392 | tf_op jit(solution)/shard_map/ppermute | solution.py:254
  94.2 25.5 %all-to-all-start.5 = ((bf16[16,24,896]{2,1,0:T(8,128)(2,1)}), bf16[16,24,896]{2,1,0:T(8,128)(2,1)S(1)}, u32[]{:S(2)}, u32[]{:S(2)}) async-start(bf16[16,24,896]{2,1,0:T(8,128)(2,1)} %bitcast.7), calls=%async_computation.5 | async-start | bytes 1376256 | tf_op jit(solution)/shard_map/all_to_all | solution.py:250
  98.0 12.2 %collective-permute-start.6 = (bf16[24,896]{1,0:T(8,128)(2,1)S(1)}, bf16[24,896]{1,0:T(8,128)(2,1)S(1)}, u32[]{:S(2)}, u32[]{:S(2)}) collective-permute-start(bf16[24,896]{1,0:T(8,128)(2,1)S(1)} %get-tuple-element.36), channel_id=1, source_target_pairs={{0,64},{64,0},{128,192},{192,128},{1,65},{65,1},{129,193},{193,129... | collective-permute-start | bytes 129032 | tf_op jit(solution)/shard_map/ppermute | solution.py:254
  101.0 10.0 %collective-permute-start.7 = (bf16[24,896]{1,0:T(8,128)(2,1)S(1)}, bf16[24,896]{1,0:T(8,128)(2,1)S(1)}, u32[]{:S(2)}, u32[]{:S(2)}) collective-permute-start(bf16[24,896]{1,0:T(8,128)(2,1)S(1)} %get-tuple-element.37), channel_id=1, source_target_pairs={{0,128},{64,192},{128,0},{192,64},{1,129},{65,193},{129,1},{193,65... | collective-permute-start | bytes 129032 | tf_op jit(solution)/shard_map/ppermute | solution.py:254
  105.3 8.0 %collective-permute-start.8 = (bf16[24,896]{1,0:T(8,128)(2,1)S(1)}, bf16[24,896]{1,0:T(8,128)(2,1)S(1)}, u32[]{:S(2)}, u32[]{:S(2)}) collective-permute-start(bf16[24,896]{1,0:T(8,128)(2,1)S(1)} %get-tuple-element.38), channel_id=1, source_target_pairs={{0,192},{64,128},{128,64},{192,0},{1,193},{65,129},{129,65},{193,1... | collective-permute-start | bytes 129032 | tf_op jit(solution)/shard_map/ppermute | solution.py:254

commit v5 on v4

--- a/solution.py
+++ b/solution.py
@@ -125,15 +125,21 @@
     return peak + jnp.log2(jnp.exp2(a - peak) + jnp.exp2(b - peak))
 
 
-def stats_kernel(factor_ref, image_ref, own_ref, other_ref, diagonal_ref, row_ref, col_ref):
+def rows_kernel(factor_ref, image_ref, own_ref, other_ref, diagonal_ref, message_ref):
     factor = factor_ref[0] * LOG2_E
-    image, own, other = image_ref[...], own_ref[...], other_ref[...]
-    own_lse = lse_of([factor * f32_dot(image, own, LAST)])
-    other_lse = lse_of([factor * f32_dot(image, other, LAST)])
-    row_lse = lse_of([factor * f32_dot(own, image, LAST), factor * f32_dot(other, image, LAST)])
-    message = eight([*lines(row_lse), factor * diagonal_ref[0:1, :]])
-    row_ref[...] = jnp.broadcast_to(message[None], row_ref.shape)
-    col_ref[...] = eight([*lines(own_lse), *lines(other_lse)])
+    image = image_ref[...]
+    lse = lse_of([factor * f32_dot(text[...], image, LAST) for text in (own_ref, other_ref)])
+    message = eight([*lines(lse), factor * diagonal_ref[0:1, :]])
+    message_ref[...] = jnp.broadcast_to(message[None], message_ref.shape)
+
+
+def columns_kernel(factor_ref, image_ref, own_ref, other_ref, message_ref):
+    factor = factor_ref[0] * LOG2_E
+    image = image_ref[...]
+    own, other = (
+        lse_of([factor * f32_dot(image, text[...], LAST)]) for text in (own_ref, other_ref)
+    )
+    message_ref[...] = eight([*lines(own), *lines(other)])
 
 
 def pair_columns_kernel(mine_ref, theirs_ref, message_ref):
@@ -161,23 +167,27 @@
         [jnp.transpose(jnp.broadcast_to(rows[k : k + 1, :], (128, 128))) for k in range(3)], axis=0
     )[:, 0:1]
     image = image_ref[...]
-    image_sum = None
-    for text_ref, col_lse in ((own_ref, own_lse), (other_ref, other_lse)):
+    sums = []
+    for text_ref, weights_ref, col_lse in (
+        (own_ref, own_out, own_lse), (other_ref, other_out, other_lse)
+    ):
         text = text_ref[...]
         logits = (factor * LOG2_E) * f32_dot(image, text, LAST)
         weights = (
             (0.5 * factor) * (jnp.exp2(logits - row_lse) + jnp.exp2(logits - col_lse))
         ).astype(jnp.bfloat16)
-        part = jnp.dot(weights, text, preferred_element_type=jnp.float32)
-        image_sum = part if image_sum is None else image_sum + part
-        text_sum = f32_dot(weights, image, FIRST)
-        if text_ref is own_ref:
-            own_out[...] = text_sum
-        else:
-            other_out[:, :width] = text_sum.astype(jnp.bfloat16)
-    other_out[:, width:] = packed(row_share, other_out.shape[0])
-    image_out[:, :width] = image_sum.astype(jnp.bfloat16)
+        weights_ref[...] = weights
+        sums.append(jnp.dot(weights, text, preferred_element_type=jnp.float32))
+    image_out[:, :width] = (sums[0] + sums[1]).astype(jnp.bfloat16)
     image_out[:, width:] = packed(col_share, image_out.shape[0])
+
+
+def text_sums_kernel(image_ref, own_ref, other_ref, share_ref, own_out, other_out):
+    image = image_ref[...]
+    width = image.shape[1]
+    other_out[:, :width] = f32_dot(other_ref[...], image, FIRST).astype(jnp.bfloat16)
+    other_out[:, width:] = packed(jnp.max(share_ref[...]), other_out.shape[0])
+    own_out[...] = f32_dot(own_ref[...], image, FIRST)
 
 
 def pair_sums_kernel(own_ref, theirs_ref, share_ref, message_ref):
@@ -288,28 +298,29 @@
     )
     image_group = exchanged(after(image_copies, text_own), NEAR)
 
-    row_message, col_part = kernel_call(
-        stats_kernel,
-        (shape((inner, 8, 128), f32), tile),
-        factor, image_group, text_own, text_other, diagonal,
-        flops=4 * work,
+    tile_of = (factor, image_group, text_own, text_other)
+    row_message = kernel_call(
+        rows_kernel, shape((inner, 8, 128), f32), *tile_of, diagonal, flops=2 * work
     )
     row_pieces = exchanged(row_message, INNER)
+    col_part = kernel_call(columns_kernel, tile, *tile_of, flops=2 * work)
     col_message = kernel_call(
         pair_columns_kernel, shape((chips, 8, 128), f32), col_part, swapped(col_part, CORE)
     )
     col_pieces = exchanged(after(col_message, row_pieces), CHIPS)
 
-    image_part, own_part, other_part, row_share = kernel_call(
+    half_tile = shape((image_rows, text_rows), bf16)
+    image_part, *weights, row_share = kernel_call(
         weights_kernel,
-        (
-            shape((image_rows, wide), bf16),
-            shape((text_rows, width), f32),
-            shape((text_rows, wide), bf16),
-            tile,
-        ),
-        factor, image_group, text_own, text_other, row_pieces, col_pieces,
-        flops=6 * work,
+        (shape((image_rows, wide), bf16), half_tile, half_tile, tile),
+        *tile_of, row_pieces, col_pieces,
+        flops=4 * work,
+    )
+    own_part, other_part = kernel_call(
+        text_sums_kernel,
+        (shape((text_rows, width), f32), shape((text_rows, wide), bf16)),
+        image_group, *weights, row_share,
+        flops=2 * work,
     )
     image_pieces = exchanged(image_part, NEAR)
     text_part = kernel_call(

time: 121 us -> 121 us (level)
  the two profiles are of different devices: /device:TPU:72 before, /device:TPU:8 now
where the time goes in v5:
time: 121 us
  starting transfers between devices  64.4 us (53%)
  waiting for transfers between devices  26.2 us (22%)
  blocking collectives  16.7 us (14%)
  Pallas kernels  11 us (9%)
  between operations  1.44 us (1%)
    all_to_all x5, starting transfers between devices, exchanged(): lax.all_to_all(split, axis, split_axis=0, concat_axis=0, tiled=True)  34.2 us
    ppermute x9, starting transfers between devices, swapped(): lax.ppermute(x, axis, [(k, k ^ offset) for k in range(lax.axis_size(axis))])  30.2 us
    all_to_all x1, blocking collectives, exchanged(): lax.all_to_all(split, axis, split_axis=0, concat_axis=0, tiled=True)  16.7 us
    ppermute x9, waiting for transfers between devices, swapped(): lax.ppermute(x, axis, [(k, k ^ offset) for k in range(lax.axis_size(axis))])  13.3 us
    all_to_all x5, waiting for transfers between devices, exchanged(): lax.all_to_all(split, axis, split_axis=0, concat_axis=0, tiled=True)  12.9 us
    pallas_call x12, Pallas kernels, kernel_call(): pl.pallas_call(body, out_shape=out_shape, in_specs=[spec(a) for a in args...  11 us
  transfers between devices with their start and end apart: 14, of which 11 were waited for; matrix products, arithmetic and copies ran while one was open for 0% of the time, Pallas kernels for 4%

profile of v5, /device:TPU:8, one launch (start us, length us, event | category | flops | bytes accessed | tf_op | source)
XLA Modules:
  0.0 120.7 jit_solution(16039265408839739783)
XLA Ops:
  0.6 0.0 copy-start
  0.6 0.9 copy-done
  1.5 0.0 copy-start.1
  1.5 0.0 copy-start.2
  1.5 1.0 shard_map.60
  2.5 12.9 %all-to-all-start = ((bf16[16,24,768]{2,1,0:T(8,128)(2,1)}), bf16[16,24,768]{2,1,0:T(8,128)(2,1)S(1)}, u32[]{:S(2)}, u32[]{:S(2)}) async-start(bf16[16,24,768]{2,1,0:T(8,128)(2,1)} %bitcast.1), calls=%async_computation | async-start | bytes 1179648 | tf_op jit(solution)/shard_map/all_to_all | solution.py:260
  15.4 0.0 copy-done.1
  15.4 0.0 copy-done.2
  15.4 0.2 shard_map.58
  15.6 4.5 %collective-permute-start = (bf16[24,768]{1,0:T(8,128)(2,1)S(1)}, bf16[24,768]{1,0:T(8,128)(2,1)S(1)}, u32[]{:S(2)}, u32[]{:S(2)}) collective-permute-start(bf16[24,768]{1,0:T(8,128)(2,1)S(1)} %get-tuple-element.23.refs_0_), channel_id=1, source_target_pairs={{0,64},{64,0},{128,192},{192,128},{1,65},{65,1},{129,193},{193,129... | collective-permute-start | bytes 110600 | tf_op jit(solution)/shard_map/ppermute | solution.py:264
  20.1 5.0 %collective-permute-start.1 = (bf16[24,768]{1,0:T(8,128)(2,1)S(1)}, bf16[24,768]{1,0:T(8,128)(2,1)S(1)}, u32[]{:S(2)}, u32[]{:S(2)}) collective-permute-start(bf16[24,768]{1,0:T(8,128)(2,1)S(1)} %get-tuple-element.23.refs_0_), channel_id=1, source_target_pairs={{0,128},{64,192},{128,0},{192,64},{1,129},{65,193},{129,1},{193,65... | collective-permute-start | bytes 110600 | tf_op jit(solution)/shard_map/ppermute | solution.py:264
  25.2 2.7 %collective-permute-start.2 = (bf16[24,768]{1,0:T(8,128)(2,1)S(1)}, bf16[24,768]{1,0:T(8,128)(2,1)S(1)}, u32[]{:S(2)}, u32[]{:S(2)}) collective-permute-start(bf16[24,768]{1,0:T(8,128)(2,1)S(1)} %get-tuple-element.23.refs_0_), channel_id=1, source_target_pairs={{0,192},{64,128},{128,64},{192,0},{1,193},{65,129},{129,65},{193,1... | collective-permute-start | bytes 110600 | tf_op jit(solution)/shard_map/ppermute | solution.py:264
  27.9 0.0 collective-permute-done.refs_1_
  27.9 2.2 %collective-permute-done.1.refs_2_ = bf16[24,768]{1,0:T(8,128)(2,1)S(1)} collective-permute-done((bf16[24,768]{1,0:T(8,128)(2,1)S(1)}, bf16[24,768]{1,0:T(8,128)(2,1)S(1)}, u32[]{:S(2)}, u32[]{:S(2)}) %collective-permute-start.1) | collective-permute-done | bytes 36896 | tf_op jit(solution)/shard_map/ppermute | solution.py:264
  30.0 3.1 %collective-permute-done.2.refs_3_ = bf16[24,768]{1,0:T(8,128)(2,1)S(1)} collective-permute-done((bf16[24,768]{1,0:T(8,128)(2,1)S(1)}, bf16[24,768]{1,0:T(8,128)(2,1)S(1)}, u32[]{:S(2)}, u32[]{:S(2)}) %collective-permute-start.2) | collective-permute-done | bytes 36896 | tf_op jit(solution)/shard_map/ppermute | solution.py:264
  33.1 0.9 shard_map.59
  34.0 0.0 all-to-all-done
  34.0 5.5 %all-to-all-start.1 = ((bf16[4,96,768]{2,1,0:T(8,128)(2,1)}), bf16[4,96,768]{2,1,0:T(8,128)(2,1)S(1)}, u32[]{:S(2)}, u32[]{:S(2)}) async-start(bf16[4,96,768]{2,1,0:T(8,128)(2,1)} %bitcast.3), calls=%async_computation.1 | async-start | bytes 1179648 | tf_op jit(solution)/shard_map/all_to_all | solution.py:260
  39.6 1.9 %collective-permute-start.3 = (bf16[384,768]{1,0:T(8,128)(2,1)S(1)}, bf16[384,768]{1,0:T(8,128)(2,1)S(1)}, u32[]{:S(2)}, u32[]{:S(2)}) collective-permute-start(bf16[384,768]{1,0:T(8,128)(2,1)S(1)} %bitcast.9), channel_id=1, source_target_pairs={{0,1},{1,0},{2,3},{3,2},{4,5},{5,4},{6,7},{7,6},{8,9},{9,8},{10,11... | collective-permute-start | bytes 1769480 | tf_op jit(solution)/shard_map/ppermute | solution.py:264
  42.1 1.3 %collective-permute-done.3.other_ref = bf16[384,768]{1,0:T(8,128)(2,1)S(1)} collective-permute-done((bf16[384,768]{1,0:T(8,128)(2,1)S(1)}, bf16[384,768]{1,0:T(8,128)(2,1)S(1)}, u32[]{:S(2)}, u32[]{:S(2)}) %collective-permute-start.3) | collective-permute-done | bytes 589856 | tf_op jit(solution)/shard_map/ppermute | solution.py:264
  43.5 2.5 %all-to-all-done.1 = bf16[4,96,768]{2,1,0:T(8,128)(2,1)S(1)} async-done(((bf16[4,96,768]{2,1,0:T(8,128)(2,1)}), bf16[4,96,768]{2,1,0:T(8,128)(2,1)S(1)}, u32[]{:S(2)}, u32[]{:S(2)}) %all-to-all-start.1) | async-done | bytes 589856 | tf_op jit(solution)/shard_map/all_to_all | solution.py:260
  45.9 1.6 %shard_map.61 = f32[16,8,128]{2,1,0:T(8,128)} custom-call(f32[1]{0:T(128)S(6)} %copy.6.factor_ref, bf16[384,768]{1,0:T(8,128)(2,1)S(1)} %bitcast.13, bf16[384,768]{1,0:T(8,128)(2,1)S(1)} %bitcast.10, bf16[384,768]{1,0:T(8,128)(2,1)S(1)} %collective-permute-done.3.other_ref, f32[8,128]{1,0:T(8,128)S(1)} %get-tuple-element.25.diagonal_ref), custom_call_target="tpu_custom_call" | custom-call | flops 452984832 | bytes 1839108 | tf_op jit(solution)/shard_map/pallas_call | solution.py:41
  47.5 7.7 %all-to-all-start.2 = ((f32[16,8,128]{2,1,0:T(8,128)}), f32[16,8,128]{2,1,0:T(8,128)S(1)}, u32[]{:S(2)}, u32[]{:S(2)}) async-start(f32[16,8,128]{2,1,0:T(8,128)} %shard_map.61), calls=%async_computation.2 | async-start | bytes 131072 | tf_op jit(solution)/shard_map/all_to_all | solution.py:260
  55.3 0.9 shard_map.62.mine_ref
  56.2 1.9 %collective-permute-start.4 = (f32[8,128]{1,0:T(8,128)S(1)}, f32[8,128]{1,0:T(8,128)S(1)}, u32[]{:S(2)}, u32[]{:S(2)}) collective-permute-start(f32[8,128]{1,0:T(8,128)S(1)} %shard_map.62.mine_ref), channel_id=1, source_target_pairs={{0,1},{1,0},{2,3},{3,2},{4,5},{5,4},{6,7},{7,6},{8,9},{9,8},{10,11... | collective-permute-start | bytes 12296 | tf_op jit(solution)/shard_map/ppermute | solution.py:264
  58.1 1.1 collective-permute-done.4.theirs_ref
  59.2 3.6 %all-to-all-done.2.row_ref = f32[16,8,128]{2,1,0:T(8,128)S(1)} async-done(((f32[16,8,128]{2,1,0:T(8,128)}), f32[16,8,128]{2,1,0:T(8,128)S(1)}, u32[]{:S(2)}, u32[]{:S(2)}) %all-to-all-start.2) | async-done | bytes 65568 | tf_op jit(solution)/shard_map/all_to_all | solution.py:260
  62.9 16.7 %all_to_all.30.pieces_ref = f32[16,8,128]{2,1,0:T(8,128)S(1)} all-to-all(f32[16,8,128]{2,1,0:T(8,128)S(1)} %shard_map.63), channel_id=1, replica_groups=mesh['z0'=2,'y2'=2,'y1'=2,'y0'=2,'x'=4,'zh'=4,'c'=2] {'x','zh'}, dimensions={0} | all-to-all | bytes 131072 | tf_op jit(solution)/shard_map/all_to_all | solution.py:260
  79.6 2.5 %shard_map.64 = (bf16[384,896]{1,0:T(8,128)(2,1)}, bf16[384,384]{1,0:T(8,128)(2,1)S(1)}, bf16[384,384]{1,0:T(8,128)(2,1)S(1)}, f32[8,128]{1,0:T(8,128)S(1)}) custom-call(f32[1]{0:T(128)S(6)} %copy.6.factor_ref, bf16[384,768]{1,0:T(8,128)(2,1)S(1)} %bitcast.15, bf16[384,768]{1,0:T(8,128)(2,1)S(1)} %bitcast.12, ...), custom_call_target="tpu_custom_call" | custom-call | flops 905969664 | bytes 3182596 | tf_op jit(solution)/shard_map/pallas_call | solution.py:41
  82.1 4.5 %all-to-all-start.4 = ((bf16[4,96,896]{2,1,0:T(8,128)(2,1)}), bf16[4,96,896]{2,1,0:T(8,128)(2,1)S(1)}, u32[]{:S(2)}, u32[]{:S(2)}) async-start(bf16[4,96,896]{2,1,0:T(8,128)(2,1)} %bitcast.5), calls=%async_computation.4 | async-start | bytes 1376256 | tf_op jit(solution)/shard_map/all_to_all | solution.py:260
  86.6 0.8 shard_map.65
  87.4 1.9 %collective-permute-start.5 = (bf16[384,896]{1,0:T(8,128)(2,1)S(1)}, bf16[384,896]{1,0:T(8,128)(2,1)S(1)}, u32[]{:S(2)}, u32[]{:S(2)}) collective-permute-start(bf16[384,896]{1,0:T(8,128)(2,1)S(1)} %get-tuple-element.31), channel_id=1, source_target_pairs={{0,1},{1,0},{2,3},{3,2},{4,5},{5,4},{6,7},{7,6},{8,9},{9,8},{10,11... | collective-permute-start | bytes 2064392 | tf_op jit(solution)/shard_map/ppermute | solution.py:264
  89.4 2.1 %collective-permute-done.5.theirs_ref = bf16[384,896]{1,0:T(8,128)(2,1)S(1)} collective-permute-done((bf16[384,896]{1,0:T(8,128)(2,1)S(1)}, bf16[384,896]{1,0:T(8,128)(2,1)S(1)}, u32[]{:S(2)}, u32[]{:S(2)}) %collective-permute-start.5) | collective-permute-done | bytes 688160 | tf_op jit(solution)/shard_map/ppermute | solution.py:264
  91.5 1.2 shard_map.66
  92.6 0.9 all-to-all-done.4
  93.5 3.6 %all-to-all-start.5 = ((bf16[16,24,896]{2,1,0:T(8,128)(2,1)}), bf16[16,24,896]{2,1,0:T(8,128)(2,1)S(1)}, u32[]{:S(2)}, u32[]{:S(2)}) async-start(bf16[16,24,896]{2,1,0:T(8,128)(2,1)} %bitcast.7), calls=%async_computation.5 | async-start | bytes 1376256 | tf_op jit(solution)/shard_map/all_to_all | solution.py:260
  97.1 0.2 shard_map.67
  97.3 2.9 %collective-permute-start.6 = (bf16[24,896]{1,0:T(8,128)(2,1)S(1)}, bf16[24,896]{1,0:T(8,128)(2,1)S(1)}, u32[]{:S(2)}, u32[]{:S(2)}) collective-permute-start(bf16[24,896]{1,0:T(8,128)(2,1)S(1)} %get-tuple-element.36), channel_id=1, source_target_pairs={{0,64},{64,0},{128,192},{192,128},{1,65},{65,1},{129,193},{193,129... | collective-permute-start | bytes 129032 | tf_op jit(solution)/shard_map/ppermute | solution.py:264
  100.2 4.4 %collective-permute-start.7 = (bf16[24,896]{1,0:T(8,128)(2,1)S(1)}, bf16[24,896]{1,0:T(8,128)(2,1)S(1)}, u32[]{:S(2)}, u32[]{:S(2)}) collective-permute-start(bf16[24,896]{1,0:T(8,128)(2,1)S(1)} %get-tuple-element.37), channel_id=1, source_target_pairs={{0,128},{64,192},{128,0},{192,64},{1,129},{65,193},{129,1},{193,65... | collective-permute-start | bytes 129032 | tf_op jit(solution)/shard_map/ppermute | solution.py:264
  104.6 4.9 %collective-permute-start.8 = (bf16[24,896]{1,0:T(8,128)(2,1)S(1)}, bf16[24,896]{1,0:T(8,128)(2,1)S(1)}, u32[]{:S(2)}, u32[]{:S(2)}) collective-permute-start(bf16[24,896]{1,0:T(8,128)(2,1)S(1)} %get-tuple-element.38), channel_id=1, source_target_pairs={{0,192},{64,128},{128,64},{192,0},{1,193},{65,129},{129,65},{193,1... | collective-permute-start | bytes 129032 | tf_op jit(solution)/shard_map/ppermute | solution.py:264
  109.6 0.0 collective-permute-done.6.first_ref
  109.6 0.4 collective-permute-done.7.second_ref
  110.0 3.1 %collective-permute-done.8.third_ref = bf16[24,896]{1,0:T(8,128)(2,1)S(1)} collective-permute-done((bf16[24,896]{1,0:T(8,128)(2,1)S(1)}, bf16[24,896]{1,0:T(8,128)(2,1)S(1)}, u32[]{:S(2)}, u32[]{:S(2)}) %collective-permute-start.8) | collective-permute-done | bytes 43040 | tf_op jit(solution)/shard_map/ppermute | solution.py:264
  113.1 0.8 shard_map.68
  113.9 5.9 %all-to-all-done.5 = bf16[16,24,896]{2,1,0:T(8,128)(2,1)S(1)} async-done(((bf16[16,24,896]{2,1,0:T(8,128)(2,1)}), bf16[16,24,896]{2,1,0:T(8,128)(2,1)S(1)}, u32[]{:S(2)}, u32[]{:S(2)}) %all-to-all-start.5) | async-done | bytes 688160 | tf_op jit(solution)/shard_map/all_to_all | solution.py:260
  119.8 0.8 shard_map.69
  (1 shorter events, 0.0 us)
Async XLA Ops:
  0.6 0.9 copy-start
  1.5 13.8 %copy-start.1 = (f32[24,768]{1,0:T(8,128)S(1)}, f32[24,768]{1,0:T(8,128)}, u32[]{:S(2)}) copy-start(f32[24,768]{1,0:T(8,128)} %values_ref.7) | copy-start | bytes 221188
  1.5 13.8 %copy-start.2 = (f32[24,768]{1,0:T(8,128)S(1)}, f32[24,768]{1,0:T(8,128)}, u32[]{:S(2)}) copy-start(f32[24,768]{1,0:T(8,128)} %paired_ref.3) | copy-start | bytes 221188
  2.5 31.6 %all-to-all-start = ((bf16[16,24,768]{2,1,0:T(8,128)(2,1)}), bf16[16,24,768]{2,1,0:T(8,128)(2,1)S(1)}, u32[]{:S(2)}, u32[]{:S(2)}) async-start(bf16[16,24,768]{2,1,0:T(8,128)(2,1)} %bitcast.1), calls=%async_computation | async-start | bytes 1179648 | tf_op jit(solution)/shard_map/all_to_all | solution.py:260
  15.6 12.3 %collective-permute-start = (bf16[24,768]{1,0:T(8,128)(2,1)S(1)}, bf16[24,768]{1,0:T(8,128)(2,1)S(1)}, u32[]{:S(2)}, u32[]{:S(2)}) collective-permute-start(bf16[24,768]{1,0:T(8,128)(2,1)S(1)} %get-tuple-element.23.refs_0_), channel_id=1, source_target_pairs={{0,64},{64,0},{128,192},{192,128},{1,65},{65,1},{129,193},{193,129... | collective-permute-start | bytes 110600 | tf_op jit(solution)/shard_map/ppermute | solution.py:264
  20.1 9.9 %collective-permute-start.1 = (bf16[24,768]{1,0:T(8,128)(2,1)S(1)}, bf16[24,768]{1,0:T(8,128)(2,1)S(1)}, u32[]{:S(2)}, u32[]{:S(2)}) collective-permute-start(bf16[24,768]{1,0:T(8,128)(2,1)S(1)} %get-tuple-element.23.refs_0_), channel_id=1, source_target_pairs={{0,128},{64,192},{128,0},{192,64},{1,129},{65,193},{129,1},{193,65... | collective-permute-start | bytes 110600 | tf_op jit(solution)/shard_map/ppermute | solution.py:264
  25.2 8.0 %collective-permute-start.2 = (bf16[24,768]{1,0:T(8,128)(2,1)S(1)}, bf16[24,768]{1,0:T(8,128)(2,1)S(1)}, u32[]{:S(2)}, u32[]{:S(2)}) collective-permute-start(bf16[24,768]{1,0:T(8,128)(2,1)S(1)} %get-tuple-element.23.refs_0_), channel_id=1, source_target_pairs={{0,192},{64,128},{128,64},{192,0},{1,193},{65,129},{129,65},{193,1... | collective-permute-start | bytes 110600 | tf_op jit(solution)/shard_map/ppermute | solution.py:264
  34.0 11.9 %all-to-all-start.1 = ((bf16[4,96,768]{2,1,0:T(8,128)(2,1)}), bf16[4,96,768]{2,1,0:T(8,128)(2,1)S(1)}, u32[]{:S(2)}, u32[]{:S(2)}) async-start(bf16[4,96,768]{2,1,0:T(8,128)(2,1)} %bitcast.3), calls=%async_computation.1 | async-start | bytes 1179648 | tf_op jit(solution)/shard_map/all_to_all | solution.py:260
  39.6 3.9 %collective-permute-start.3 = (bf16[384,768]{1,0:T(8,128)(2,1)S(1)}, bf16[384,768]{1,0:T(8,128)(2,1)S(1)}, u32[]{:S(2)}, u32[]{:S(2)}) collective-permute-start(bf16[384,768]{1,0:T(8,128)(2,1)S(1)} %bitcast.9), channel_id=1, source_target_pairs={{0,1},{1,0},{2,3},{3,2},{4,5},{5,4},{6,7},{7,6},{8,9},{9,8},{10,11... | collective-permute-start | bytes 1769480 | tf_op jit(solution)/shard_map/ppermute | solution.py:264
  47.5 15.3 %all-to-all-start.2 = ((f32[16,8,128]{2,1,0:T(8,128)}), f32[16,8,128]{2,1,0:T(8,128)S(1)}, u32[]{:S(2)}, u32[]{:S(2)}) async-start(f32[16,8,128]{2,1,0:T(8,128)} %shard_map.61), calls=%async_computation.2 | async-start | bytes 131072 | tf_op jit(solution)/shard_map/all_to_all | solution.py:260
  56.2 3.1 %collective-permute-start.4 = (f32[8,128]{1,0:T(8,128)S(1)}, f32[8,128]{1,0:T(8,128)S(1)}, u32[]{:S(2)}, u32[]{:S(2)}) collective-permute-start(f32[8,128]{1,0:T(8,128)S(1)} %shard_map.62.mine_ref), channel_id=1, source_target_pairs={{0,1},{1,0},{2,3},{3,2},{4,5},{5,4},{6,7},{7,6},{8,9},{9,8},{10,11... | collective-permute-start | bytes 12296 | tf_op jit(solution)/shard_map/ppermute | solution.py:264
  82.1 11.4 %all-to-all-start.4 = ((bf16[4,96,896]{2,1,0:T(8,128)(2,1)}), bf16[4,96,896]{2,1,0:T(8,128)(2,1)S(1)}, u32[]{:S(2)}, u32[]{:S(2)}) async-start(bf16[4,96,896]{2,1,0:T(8,128)(2,1)} %bitcast.5), calls=%async_computation.4 | async-start | bytes 1376256 | tf_op jit(solution)/shard_map/all_to_all | solution.py:260
  87.4 4.0 %collective-permute-start.5 = (bf16[384,896]{1,0:T(8,128)(2,1)S(1)}, bf16[384,896]{1,0:T(8,128)(2,1)S(1)}, u32[]{:S(2)}, u32[]{:S(2)}) collective-permute-start(bf16[384,896]{1,0:T(8,128)(2,1)S(1)} %get-tuple-element.31), channel_id=1, source_target_pairs={{0,1},{1,0},{2,3},{3,2},{4,5},{5,4},{6,7},{7,6},{8,9},{9,8},{10,11... | collective-permute-start | bytes 2064392 | tf_op jit(solution)/shard_map/ppermute | solution.py:264
  93.5 26.3 %all-to-all-start.5 = ((bf16[16,24,896]{2,1,0:T(8,128)(2,1)}), bf16[16,24,896]{2,1,0:T(8,128)(2,1)S(1)}, u32[]{:S(2)}, u32[]{:S(2)}) async-start(bf16[16,24,896]{2,1,0:T(8,128)(2,1)} %bitcast.7), calls=%async_computation.5 | async-start | bytes 1376256 | tf_op jit(solution)/shard_map/all_to_all | solution.py:260
  97.3 12.2 %collective-permute-start.6 = (bf16[24,896]{1,0:T(8,128)(2,1)S(1)}, bf16[24,896]{1,0:T(8,128)(2,1)S(1)}, u32[]{:S(2)}, u32[]{:S(2)}) collective-permute-start(bf16[24,896]{1,0:T(8,128)(2,1)S(1)} %get-tuple-element.36), channel_id=1, source_target_pairs={{0,64},{64,0},{128,192},{192,128},{1,65},{65,1},{129,193},{193,129... | collective-permute-start | bytes 129032 | tf_op jit(solution)/shard_map/ppermute | solution.py:264
  100.2 9.8 %collective-permute-start.7 = (bf16[24,896]{1,0:T(8,128)(2,1)S(1)}, bf16[24,896]{1,0:T(8,128)(2,1)S(1)}, u32[]{:S(2)}, u32[]{:S(2)}) collective-permute-start(bf16[24,896]{1,0:T(8,128)(2,1)S(1)} %get-tuple-element.37), channel_id=1, source_target_pairs={{0,128},{64,192},{128,0},{192,64},{1,129},{65,193},{129,1},{193,65... | collective-permute-start | bytes 129032 | tf_op jit(solution)/shard_map/ppermute | solution.py:264
  104.6 8.5 %collective-permute-start.8 = (bf16[24,896]{1,0:T(8,128)(2,1)S(1)}, bf16[24,896]{1,0:T(8,128)(2,1)S(1)}, u32[]{:S(2)}, u32[]{:S(2)}) collective-permute-start(bf16[24,896]{1,0:T(8,128)(2,1)S(1)} %get-tuple-element.38), channel_id=1, source_target_pairs={{0,192},{64,128},{128,64},{192,0},{1,193},{65,129},{129,65},{193,1... | collective-permute-start | bytes 129032 | tf_op jit(solution)/shard_map/ppermute | solution.py:264

commit v6 on v5

--- a/solution.py
+++ b/solution.py
@@ -8,11 +8,11 @@
 from jax.sharding import Mesh
 from jax.sharding import PartitionSpec as P
 
-ALL = ("z0", "y2", "y1", "y0", "x", "zh", "c")
-INNER = ("z0", "y2", "y1", "y0")
-CHIPS = ("x", "zh")
-NEAR = ("z0", "y0")
-FAR = ("y2", "y1")
+ALL = ("z0", "y2", "y1", "y0", "x", "z2", "z1", "c")
+INNER = ("y2", "y1", "z2", "z1")
+CHIPS = ("x", "y0", "z0")
+NEAR = ("y2", "y1", "z1")
+FAR = "z2"
 CORE = "c"
 
 EPSILON = 1e-06
@@ -227,19 +227,19 @@
     return (pull - unit * jnp.sum(pull * unit, axis=1, keepdims=True)) * inverse
 
 
-def image_gradient_kernel(
-    factor_ref, values_ref, paired_ref, kept_ref, shared_ref, first_ref, second_ref, third_ref,
-    gradient_ref, share_ref,
-):
+def tree_sum(terms):
+    while len(terms) > 1:
+        terms = [a + b for a, b in zip(terms[::2], terms[1::2])]
+    return terms[0]
+
+
+def image_gradient_kernel(factor_ref, values_ref, paired_ref, kept_ref, shared_ref, *refs):
+    *far_refs, gradient_ref, share_ref = refs
     width = kept_ref.shape[1]
-    first, second, third = (
-        ref[...].astype(jnp.float32) for ref in (first_ref, second_ref, third_ref)
-    )
-    total = (kept_ref[...] + first[:, :width]) + (second[:, :width] + third[:, :width])
+    fars = [ref[...].astype(jnp.float32) for ref in far_refs]
+    total = tree_sum([kept_ref[...]] + [far[:, :width] for far in fars])
     gradient_ref[...] = gradient(factor_ref[0], values_ref[...], paired_ref[...], total)
-    share = (jnp.max(shared_ref[...]) + unpacked(first, width)) + (
-        unpacked(second, width) + unpacked(third, width)
-    )
+    share = tree_sum([jnp.max(shared_ref[...])] + [unpacked(far, width) for far in fars])
     share_ref[...] = jnp.broadcast_to(share, share_ref.shape)
 
 
@@ -348,7 +348,7 @@
 
 
 def solution(mesh):
-    split = Mesh(mesh.devices.reshape(2, 2, 2, 2, 4, 4, 2), ALL)
+    split = Mesh(mesh.devices.reshape(2, 2, 2, 2, 4, 2, 2, 2), ALL)
     in_specs = (P(ALL, None), P(ALL, None), P())
     out_specs = (P(), P(ALL, None), P(ALL, None))
     return jax.shard_map(

time: 121 us -> 129 us (1.066)
  the two profiles are of different devices: /device:TPU:8 before, /device:TPU:1 now
where the time goes in v6:
time: 129 us; the launch traced here: 128 us
  starting transfers between devices  67.1 us (52%)
  waiting for transfers between devices  36.2 us (28%)
  blocking collectives  11.8 us (9%)
  Pallas kernels  10.9 us (8%)
  between operations  1.41 us (1%)
    all_to_all x5, starting transfers between devices, exchanged(): lax.all_to_all(split, axis, split_axis=0, concat_axis=0, tiled=True)  38.4 us
    ppermute x5, starting transfers between devices, swapped(): lax.ppermute(x, axis, [(k, k ^ offset) for k in range(lax.axis_size(axis))])  28.7 us
    all_to_all x5, waiting for transfers between devices, exchanged(): lax.all_to_all(split, axis, split_axis=0, concat_axis=0, tiled=True)  22.1 us
    ppermute x5, waiting for transfers between devices, swapped(): lax.ppermute(x, axis, [(k, k ^ offset) for k in range(lax.axis_size(axis))])  14.1 us
    all_to_all x1, blocking collectives, exchanged(): lax.all_to_all(split, axis, split_axis=0, concat_axis=0, tiled=True)  11.8 us
    pallas_call x12, Pallas kernels, kernel_call(): pl.pallas_call(body, out_shape=out_shape, in_specs=[spec(a) for a in args...  10.9 us
  transfers between devices with their start and end apart: 10, of which 8 were waited for; matrix products, arithmetic and copies ran while one was open for 0% of the time, Pallas kernels for 4%

profile of v6, /device:TPU:1, one launch (start us, length us, event | category | flops | bytes accessed | tf_op | source)
XLA Modules:
  0.0 128.2 jit_solution(15987774220814241014)
XLA Ops:
  0.6 0.0 copy-start
  0.6 0.9 copy-done
  1.5 0.0 copy-start.1
  1.5 0.0 copy-start.2
  1.5 1.0 shard_map.60
  2.5 7.8 %all-to-all-start = ((bf16[16,24,768]{2,1,0:T(8,128)(2,1)}), bf16[16,24,768]{2,1,0:T(8,128)(2,1)S(1)}, u32[]{:S(2)}, u32[]{:S(2)}) async-start(bf16[16,24,768]{2,1,0:T(8,128)(2,1)} %bitcast.1), calls=%async_computation | async-start | bytes 1179648 | tf_op jit(solution)/shard_map/all_to_all | solution.py:260
  10.3 0.0 copy-done.1
  10.3 0.0 copy-done.2
  10.3 0.2 shard_map.58
  10.5 9.7 %collective-permute-start = (bf16[24,768]{1,0:T(8,128)(2,1)S(1)}, bf16[24,768]{1,0:T(8,128)(2,1)S(1)}, u32[]{:S(2)}, u32[]{:S(2)}) collective-permute-start(bf16[24,768]{1,0:T(8,128)(2,1)S(1)} %get-tuple-element.21.refs_0_), channel_id=1, source_target_pairs={{0,4},{4,0},{1,5},{5,1},{2,6},{6,2},{3,7},{7,3},{8,12},{12,8},{9,1... | collective-permute-start | bytes 110600 | tf_op jit(solution)/shard_map/ppermute | solution.py:264
  20.3 2.5 %collective-permute-done.refs_1_ = bf16[24,768]{1,0:T(8,128)(2,1)S(1)} collective-permute-done((bf16[24,768]{1,0:T(8,128)(2,1)S(1)}, bf16[24,768]{1,0:T(8,128)(2,1)S(1)}, u32[]{:S(2)}, u32[]{:S(2)}) %collective-permute-start) | collective-permute-done | bytes 36896 | tf_op jit(solution)/shard_map/ppermute | solution.py:264
  22.8 0.9 shard_map.59
  23.6 0.0 all-to-all-done
  23.6 8.5 %all-to-all-start.1 = ((bf16[8,48,768]{2,1,0:T(8,128)(2,1)}), bf16[8,48,768]{2,1,0:T(8,128)(2,1)S(1)}, u32[]{:S(2)}, u32[]{:S(2)}) async-start(bf16[8,48,768]{2,1,0:T(8,128)(2,1)} %bitcast.3), calls=%async_computation.1 | async-start | bytes 1179648 | tf_op jit(solution)/shard_map/all_to_all | solution.py:260
  32.1 6.4 %collective-permute-start.1 = (bf16[384,768]{1,0:T(8,128)(2,1)S(1)}, bf16[384,768]{1,0:T(8,128)(2,1)S(1)}, u32[]{:S(2)}, u32[]{:S(2)}) collective-permute-start(bf16[384,768]{1,0:T(8,128)(2,1)S(1)} %bitcast.9), channel_id=1, source_target_pairs={{0,1},{1,0},{2,3},{3,2},{4,5},{5,4},{6,7},{7,6},{8,9},{9,8},{10,11... | collective-permute-start | bytes 1769480 | tf_op jit(solution)/shard_map/ppermute | solution.py:264
  39.2 1.0 collective-permute-done.1.other_ref
  40.2 3.3 %all-to-all-done.1 = bf16[8,48,768]{2,1,0:T(8,128)(2,1)S(1)} async-done(((bf16[8,48,768]{2,1,0:T(8,128)(2,1)}), bf16[8,48,768]{2,1,0:T(8,128)(2,1)S(1)}, u32[]{:S(2)}, u32[]{:S(2)}) %all-to-all-start.1) | async-done | bytes 589856 | tf_op jit(solution)/shard_map/all_to_all | solution.py:260
  43.5 1.6 %shard_map.61 = f32[16,8,128]{2,1,0:T(8,128)} custom-call(f32[1]{0:T(128)S(6)} %copy.6.factor_ref, bf16[384,768]{1,0:T(8,128)(2,1)S(1)} %bitcast.13, bf16[384,768]{1,0:T(8,128)(2,1)S(1)} %bitcast.10, bf16[384,768]{1,0:T(8,128)(2,1)S(1)} %collective-permute-done.1.other_ref, f32[8,128]{1,0:T(8,128)S(1)} %get-tuple-element.23.diagonal_ref), custom_call_target="tpu_custom_call" | custom-call | flops 452984832 | bytes 1839108 | tf_op jit(solution)/shard_map/pallas_call | solution.py:41
  45.1 15.0 %all-to-all-start.2 = ((f32[16,8,128]{2,1,0:T(8,128)}), f32[16,8,128]{2,1,0:T(8,128)S(1)}, u32[]{:S(2)}, u32[]{:S(2)}) async-start(f32[16,8,128]{2,1,0:T(8,128)} %shard_map.61), calls=%async_computation.2 | async-start | bytes 131072 | tf_op jit(solution)/shard_map/all_to_all | solution.py:260
  60.1 0.9 shard_map.62.mine_ref
  61.0 2.7 %collective-permute-start.2 = (f32[8,128]{1,0:T(8,128)S(1)}, f32[8,128]{1,0:T(8,128)S(1)}, u32[]{:S(2)}, u32[]{:S(2)}) collective-permute-start(f32[8,128]{1,0:T(8,128)S(1)} %shard_map.62.mine_ref), channel_id=1, source_target_pairs={{0,1},{1,0},{2,3},{3,2},{4,5},{5,4},{6,7},{7,6},{8,9},{9,8},{10,11... | collective-permute-start | bytes 12296 | tf_op jit(solution)/shard_map/ppermute | solution.py:264
  63.7 0.8 collective-permute-done.2.theirs_ref
  64.5 6.9 %all-to-all-done.2.row_ref = f32[16,8,128]{2,1,0:T(8,128)S(1)} async-done(((f32[16,8,128]{2,1,0:T(8,128)}), f32[16,8,128]{2,1,0:T(8,128)S(1)}, u32[]{:S(2)}, u32[]{:S(2)}) %all-to-all-start.2) | async-done | bytes 65568 | tf_op jit(solution)/shard_map/all_to_all | solution.py:260
  71.4 11.8 %all_to_all.30.pieces_ref = f32[16,8,128]{2,1,0:T(8,128)S(1)} all-to-all(f32[16,8,128]{2,1,0:T(8,128)S(1)} %shard_map.63), channel_id=1, replica_groups=mesh['z0'=2,'y2'=2,'y1'=2,'y0'=2,'x'=4,'z2'=2,'z1'=2,'c'=2] {'x','y0','z0'}, dimensions={0} | all-to-all | bytes 131072 | tf_op jit(solution)/shard_map/all_to_all | solution.py:260
  83.2 2.5 %shard_map.64 = (bf16[384,896]{1,0:T(8,128)(2,1)}, bf16[384,384]{1,0:T(8,128)(2,1)S(1)}, bf16[384,384]{1,0:T(8,128)(2,1)S(1)}, f32[8,128]{1,0:T(8,128)S(1)}) custom-call(f32[1]{0:T(128)S(6)} %copy.6.factor_ref, bf16[384,768]{1,0:T(8,128)(2,1)S(1)} %bitcast.15, bf16[384,768]{1,0:T(8,128)(2,1)S(1)} %bitcast.12, ...), custom_call_target="tpu_custom_call" | custom-call | flops 905969664 | bytes 3182596 | tf_op jit(solution)/shard_map/pallas_call | solution.py:41
  85.8 3.5 %all-to-all-start.4 = ((bf16[8,48,896]{2,1,0:T(8,128)(2,1)}), bf16[8,48,896]{2,1,0:T(8,128)(2,1)S(1)}, u32[]{:S(2)}, u32[]{:S(2)}) async-start(bf16[8,48,896]{2,1,0:T(8,128)(2,1)} %bitcast.5), calls=%async_computation.4 | async-start | bytes 1376256 | tf_op jit(solution)/shard_map/all_to_all | solution.py:260
  89.3 0.8 shard_map.65
  90.1 5.5 %collective-permute-start.3 = (bf16[384,896]{1,0:T(8,128)(2,1)S(1)}, bf16[384,896]{1,0:T(8,128)(2,1)S(1)}, u32[]{:S(2)}, u32[]{:S(2)}) collective-permute-start(bf16[384,896]{1,0:T(8,128)(2,1)S(1)} %get-tuple-element.29), channel_id=1, source_target_pairs={{0,1},{1,0},{2,3},{3,2},{4,5},{5,4},{6,7},{7,6},{8,9},{9,8},{10,11... | collective-permute-start | bytes 2064392 | tf_op jit(solution)/shard_map/ppermute | solution.py:264
  95.7 1.7 %collective-permute-done.3.theirs_ref = bf16[384,896]{1,0:T(8,128)(2,1)S(1)} collective-permute-done((bf16[384,896]{1,0:T(8,128)(2,1)S(1)}, bf16[384,896]{1,0:T(8,128)(2,1)S(1)}, u32[]{:S(2)}, u32[]{:S(2)}) %collective-permute-start.3) | collective-permute-done | bytes 688160 | tf_op jit(solution)/shard_map/ppermute | solution.py:264
  97.4 1.1 shard_map.66
  98.6 11.9 %all-to-all-done.4 = bf16[8,48,896]{2,1,0:T(8,128)(2,1)S(1)} async-done(((bf16[8,48,896]{2,1,0:T(8,128)(2,1)}), bf16[8,48,896]{2,1,0:T(8,128)(2,1)S(1)}, u32[]{:S(2)}, u32[]{:S(2)}) %all-to-all-start.4) | async-done | bytes 688160 | tf_op jit(solution)/shard_map/all_to_all | solution.py:260
  110.5 3.6 %all-to-all-start.5 = ((bf16[16,24,896]{2,1,0:T(8,128)(2,1)}), bf16[16,24,896]{2,1,0:T(8,128)(2,1)S(1)}, u32[]{:S(2)}, u32[]{:S(2)}) async-start(bf16[16,24,896]{2,1,0:T(8,128)(2,1)} %bitcast.7), calls=%async_computation.5 | async-start | bytes 1376256 | tf_op jit(solution)/shard_map/all_to_all | solution.py:260
  114.1 0.2 shard_map.67
  114.2 4.2 %collective-permute-start.4 = (bf16[24,896]{1,0:T(8,128)(2,1)S(1)}, bf16[24,896]{1,0:T(8,128)(2,1)S(1)}, u32[]{:S(2)}, u32[]{:S(2)}) collective-permute-start(bf16[24,896]{1,0:T(8,128)(2,1)S(1)} %get-tuple-element.34), channel_id=1, source_target_pairs={{0,4},{4,0},{1,5},{5,1},{2,6},{6,2},{3,7},{7,3},{8,12},{12,8},{9,1... | collective-permute-start | bytes 129032 | tf_op jit(solution)/shard_map/ppermute | solution.py:264
  118.5 8.1 %collective-permute-done.4.refs_0_ = bf16[24,896]{1,0:T(8,128)(2,1)S(1)} collective-permute-done((bf16[24,896]{1,0:T(8,128)(2,1)S(1)}, bf16[24,896]{1,0:T(8,128)(2,1)S(1)}, u32[]{:S(2)}, u32[]{:S(2)}) %collective-permute-start.4) | collective-permute-done | bytes 43040 | tf_op jit(solution)/shard_map/ppermute | solution.py:264
  126.5 0.8 shard_map.68
  127.4 0.0 all-to-all-done.5
  127.4 0.8 shard_map.69
  (1 shorter events, 0.0 us)
Async XLA Ops:
  0.6 0.9 copy-start
  1.5 8.8 %copy-start.1 = (f32[24,768]{1,0:T(8,128)S(1)}, f32[24,768]{1,0:T(8,128)}, u32[]{:S(2)}) copy-start(f32[24,768]{1,0:T(8,128)} %values_ref.7) | copy-start | bytes 221188
  1.5 8.8 %copy-start.2 = (f32[24,768]{1,0:T(8,128)S(1)}, f32[24,768]{1,0:T(8,128)}, u32[]{:S(2)}) copy-start(f32[24,768]{1,0:T(8,128)} %paired_ref.3) | copy-start | bytes 221188
  2.5 21.1 %all-to-all-start = ((bf16[16,24,768]{2,1,0:T(8,128)(2,1)}), bf16[16,24,768]{2,1,0:T(8,128)(2,1)S(1)}, u32[]{:S(2)}, u32[]{:S(2)}) async-start(bf16[16,24,768]{2,1,0:T(8,128)(2,1)} %bitcast.1), calls=%async_computation | async-start | bytes 1179648 | tf_op jit(solution)/shard_map/all_to_all | solution.py:260
  10.5 12.2 %collective-permute-start = (bf16[24,768]{1,0:T(8,128)(2,1)S(1)}, bf16[24,768]{1,0:T(8,128)(2,1)S(1)}, u32[]{:S(2)}, u32[]{:S(2)}) collective-permute-start(bf16[24,768]{1,0:T(8,128)(2,1)S(1)} %get-tuple-element.21.refs_0_), channel_id=1, source_target_pairs={{0,4},{4,0},{1,5},{5,1},{2,6},{6,2},{3,7},{7,3},{8,12},{12,8},{9,1... | collective-permute-start | bytes 110600 | tf_op jit(solution)/shard_map/ppermute | solution.py:264
  23.6 19.9 %all-to-all-start.1 = ((bf16[8,48,768]{2,1,0:T(8,128)(2,1)}), bf16[8,48,768]{2,1,0:T(8,128)(2,1)S(1)}, u32[]{:S(2)}, u32[]{:S(2)}) async-start(bf16[8,48,768]{2,1,0:T(8,128)(2,1)} %bitcast.3), calls=%async_computation.1 | async-start | bytes 1179648 | tf_op jit(solution)/shard_map/all_to_all | solution.py:260
  32.1 8.1 %collective-permute-start.1 = (bf16[384,768]{1,0:T(8,128)(2,1)S(1)}, bf16[384,768]{1,0:T(8,128)(2,1)S(1)}, u32[]{:S(2)}, u32[]{:S(2)}) collective-permute-start(bf16[384,768]{1,0:T(8,128)(2,1)S(1)} %bitcast.9), channel_id=1, source_target_pairs={{0,1},{1,0},{2,3},{3,2},{4,5},{5,4},{6,7},{7,6},{8,9},{9,8},{10,11... | collective-permute-start | bytes 1769480 | tf_op jit(solution)/shard_map/ppermute | solution.py:264
  45.1 26.3 %all-to-all-start.2 = ((f32[16,8,128]{2,1,0:T(8,128)}), f32[16,8,128]{2,1,0:T(8,128)S(1)}, u32[]{:S(2)}, u32[]{:S(2)}) async-start(f32[16,8,128]{2,1,0:T(8,128)} %shard_map.61), calls=%async_computation.2 | async-start | bytes 131072 | tf_op jit(solution)/shard_map/all_to_all | solution.py:260
  61.0 3.5 %collective-permute-start.2 = (f32[8,128]{1,0:T(8,128)S(1)}, f32[8,128]{1,0:T(8,128)S(1)}, u32[]{:S(2)}, u32[]{:S(2)}) collective-permute-start(f32[8,128]{1,0:T(8,128)S(1)} %shard_map.62.mine_ref), channel_id=1, source_target_pairs={{0,1},{1,0},{2,3},{3,2},{4,5},{5,4},{6,7},{7,6},{8,9},{9,8},{10,11... | collective-permute-start | bytes 12296 | tf_op jit(solution)/shard_map/ppermute | solution.py:264
  85.8 24.7 %all-to-all-start.4 = ((bf16[8,48,896]{2,1,0:T(8,128)(2,1)}), bf16[8,48,896]{2,1,0:T(8,128)(2,1)S(1)}, u32[]{:S(2)}, u32[]{:S(2)}) async-start(bf16[8,48,896]{2,1,0:T(8,128)(2,1)} %bitcast.5), calls=%async_computation.4 | async-start | bytes 1376256 | tf_op jit(solution)/shard_map/all_to_all | solution.py:260
  90.1 7.3 %collective-permute-start.3 = (bf16[384,896]{1,0:T(8,128)(2,1)S(1)}, bf16[384,896]{1,0:T(8,128)(2,1)S(1)}, u32[]{:S(2)}, u32[]{:S(2)}) collective-permute-start(bf16[384,896]{1,0:T(8,128)(2,1)S(1)} %get-tuple-element.29), channel_id=1, source_target_pairs={{0,1},{1,0},{2,3},{3,2},{4,5},{5,4},{6,7},{7,6},{8,9},{9,8},{10,11... | collective-permute-start | bytes 2064392 | tf_op jit(solution)/shard_map/ppermute | solution.py:264
  110.5 16.9 %all-to-all-start.5 = ((bf16[16,24,896]{2,1,0:T(8,128)(2,1)}), bf16[16,24,896]{2,1,0:T(8,128)(2,1)S(1)}, u32[]{:S(2)}, u32[]{:S(2)}) async-start(bf16[16,24,896]{2,1,0:T(8,128)(2,1)} %bitcast.7), calls=%async_computation.5 | async-start | bytes 1376256 | tf_op jit(solution)/shard_map/all_to_all | solution.py:260
  114.2 12.3 %collective-permute-start.4 = (bf16[24,896]{1,0:T(8,128)(2,1)S(1)}, bf16[24,896]{1,0:T(8,128)(2,1)S(1)}, u32[]{:S(2)}, u32[]{:S(2)}) collective-permute-start(bf16[24,896]{1,0:T(8,128)(2,1)S(1)} %get-tuple-element.34), channel_id=1, source_target_pairs={{0,4},{4,0},{1,5},{5,1},{2,6},{6,2},{3,7},{7,3},{8,12},{12,8},{9,1... | collective-permute-start | bytes 129032 | tf_op jit(solution)/shard_map/ppermute | solution.py:264

commit v7 on v5

--- a/solution.py
+++ b/solution.py
@@ -78,22 +78,15 @@
     diagonal_ref[...] = jnp.broadcast_to(jnp.sum(products), diagonal_ref.shape)
 
 
-def chosen(number, blocks):
-    found = blocks[0]
-    for k in range(1, len(blocks)):
-        found = jnp.where(number == k, blocks[k], found)
-    return found
-
-
-def join_kernel(place_ref, *refs):
-    *block_refs, joined_ref = refs
-    blocks = [ref[...].astype(jnp.float32) for ref in block_refs]
-    ordered = [chosen(place_ref[0] ^ k, blocks) for k in range(len(blocks))]
-    rows = 2 * blocks[0].shape[0]
-    for pair in range(len(blocks) // 2):
-        half = jnp.concatenate(ordered[2 * pair : 2 * pair + 2], axis=0).astype(jnp.bfloat16)
-        for at in range(pair * rows, joined_ref.shape[0], rows * len(blocks) // 2):
-            joined_ref[at : at + rows, :] = half
+def join_kernel(side_ref, mine_ref, theirs_ref, joined_ref):
+    mine, theirs = mine_ref[...].astype(jnp.float32), theirs_ref[...].astype(jnp.float32)
+    first = side_ref[0] == 0
+    joined = jnp.concatenate(
+        [jnp.where(first, mine, theirs), jnp.where(first, theirs, mine)], axis=0
+    ).astype(jnp.bfloat16)
+    rows = joined.shape[0]
+    for k in range(joined_ref.shape[0] // rows):
+        joined_ref[k * rows : (k + 1) * rows, :] = joined
 
 
 def lines(row):
@@ -142,11 +135,18 @@
     message_ref[...] = eight([*lines(own), *lines(other)])
 
 
-def pair_columns_kernel(mine_ref, theirs_ref, message_ref):
+def pair_columns_kernel(mine_ref, theirs_ref, pair_ref):
     mine, theirs = mine_ref[...], theirs_ref[...]
     own = pair_lse(mine[0:3], theirs[3:6])
     other = pair_lse(mine[3:6], theirs[0:3])
-    message = jnp.concatenate([own, other, jnp.zeros((2, 128), jnp.float32)], axis=0)
+    pair_ref[...] = jnp.concatenate([own, other, jnp.zeros((2, 128), jnp.float32)], axis=0)
+
+
+def message_kernel(row_ref, pair_ref, message_ref):
+    pieces = row_ref[...]
+    share = jnp.sum(pieces_lse(pieces)[0:3]) - 2.0 * jnp.max(jnp.sum(pieces, axis=0)[3:4])
+    number = lax.broadcasted_iota(jnp.int32, (8, 128), 0)
+    message = jnp.where(number == 6, share, pair_ref[...])
     message_ref[...] = jnp.broadcast_to(message[None], message_ref.shape)
 
 
@@ -156,12 +156,12 @@
 ):
     factor = factor_ref[0]
     width = own_ref.shape[1]
-    cols = pieces_lse(pieces_ref[...])
+    pieces = pieces_ref[...]
+    cols = pieces_lse(pieces)
     own_lse, other_lse = line(cols[0:3]), line(cols[3:6])
     col_share = jnp.sum(own_lse) + jnp.sum(other_lse)
-    row_pieces = row_ref[...]
-    rows = pieces_lse(row_pieces)[0:3]
-    row_share = jnp.sum(rows) - 2.0 * jnp.max(jnp.sum(row_pieces, axis=0)[3:4])
+    rows = pieces_lse(row_ref[...])[0:3]
+    row_share = jnp.max(jnp.sum(pieces, axis=0)[6:7])
     share_ref[...] = jnp.broadcast_to(row_share, share_ref.shape)
     row_lse = jnp.concatenate(
         [jnp.transpose(jnp.broadcast_to(rows[k : k + 1, :], (128, 128))) for k in range(3)], axis=0
@@ -190,12 +190,12 @@
     own_out[...] = f32_dot(own_ref[...], image, FIRST)
 
 
-def pair_sums_kernel(own_ref, theirs_ref, share_ref, message_ref):
+def pair_sums_kernel(own_ref, theirs_ref, shared_ref, sums_ref, share_ref):
     width = own_ref.shape[1]
     theirs = theirs_ref[...].astype(jnp.float32)
-    message_ref[:, :width] = (own_ref[...] + theirs[:, :width]).astype(jnp.bfloat16)
-    share = jnp.max(share_ref[...]) + unpacked(theirs, width)
-    message_ref[:, width:] = packed(share, message_ref.shape[0])
+    sums_ref[...] = (own_ref[...] + theirs[:, :width]).astype(jnp.bfloat16)
+    share = jnp.max(shared_ref[...]) + unpacked(theirs, width)
+    share_ref[...] = jnp.broadcast_to(share, share_ref.shape)
 
 
 def slabs_sum(pieces_ref, rows):
@@ -207,18 +207,27 @@
     return total
 
 
-def near_sums_kernel(place_ref, pieces_ref, keep_ref, *refs):
-    *send_refs, share_ref = refs
+def keep_and_send(total, share, side_ref, keep_ref, send_ref, share_ref):
     rows, width = keep_ref.shape
-    count = len(send_refs) + 1
-    total = slabs_sum(pieces_ref, count * rows)
-    share = unpacked(total, width)
-    blocks = [total[k * rows : (k + 1) * rows, :width] for k in range(count)]
-    keep_ref[...] = chosen(place_ref[0], blocks)
-    for k, send_ref in enumerate(send_refs):
-        send_ref[:, :width] = chosen(place_ref[0] ^ (k + 1), blocks).astype(jnp.bfloat16)
-        send_ref[:, width:] = packed(share, rows)
+    first = side_ref[0] == 0
+    lower, upper = total[:rows, :width], total[rows:, :width]
+    keep_ref[...] = jnp.where(first, lower, upper)
+    send_ref[:, :width] = jnp.where(first, upper, lower).astype(jnp.bfloat16)
+    send_ref[:, width:] = packed(share, rows)
     share_ref[...] = jnp.broadcast_to(share, share_ref.shape)
+
+
+def near_sums_kernel(side_ref, pieces_ref, keep_ref, send_ref, share_ref):
+    rows, width = keep_ref.shape
+    total = slabs_sum(pieces_ref, 2 * rows)
+    keep_and_send(total, unpacked(total, width), side_ref, keep_ref, send_ref, share_ref)
+
+
+def middle_sums_kernel(side_ref, kept_ref, theirs_ref, shared_ref, keep_ref, send_ref, share_ref):
+    width = kept_ref.shape[1]
+    theirs = theirs_ref[...].astype(jnp.float32)
+    share = jnp.max(shared_ref[...]) + unpacked(theirs, width)
+    keep_and_send(kept_ref[...] + theirs[:, :width], share, side_ref, keep_ref, send_ref, share_ref)
 
 
 def gradient(factor, values, paired, total):
@@ -228,30 +237,23 @@
 
 
 def image_gradient_kernel(
-    factor_ref, values_ref, paired_ref, kept_ref, shared_ref, first_ref, second_ref, third_ref,
-    gradient_ref, share_ref,
+    factor_ref, values_ref, paired_ref, kept_ref, theirs_ref, shared_ref, gradient_ref, share_ref
 ):
     width = kept_ref.shape[1]
-    first, second, third = (
-        ref[...].astype(jnp.float32) for ref in (first_ref, second_ref, third_ref)
-    )
-    total = (kept_ref[...] + first[:, :width]) + (second[:, :width] + third[:, :width])
+    theirs = theirs_ref[...].astype(jnp.float32)
+    total = kept_ref[...] + theirs[:, :width]
     gradient_ref[...] = gradient(factor_ref[0], values_ref[...], paired_ref[...], total)
-    share = (jnp.max(shared_ref[...]) + unpacked(first, width)) + (
-        unpacked(second, width) + unpacked(third, width)
-    )
+    share = jnp.max(shared_ref[...]) + unpacked(theirs, width)
     share_ref[...] = jnp.broadcast_to(share, share_ref.shape)
 
 
 def text_gradient_kernel(
-    whole, factor_ref, values_ref, paired_ref, pieces_ref, shared_ref, gradient_ref, loss_ref
+    whole, factor_ref, values_ref, paired_ref, pieces_ref, row_share_ref, col_share_ref,
+    gradient_ref, loss_ref,
 ):
-    rows, width = values_ref.shape
-    total = slabs_sum(pieces_ref, rows)
-    gradient_ref[...] = gradient(
-        factor_ref[0], values_ref[...], paired_ref[...], total[:, :width]
-    )
-    loss_ref[0] = (jnp.max(shared_ref[...]) + unpacked(total, width)) * (1.0 / (LOG2_E * whole))
+    total = slabs_sum(pieces_ref, values_ref.shape[0])
+    gradient_ref[...] = gradient(factor_ref[0], values_ref[...], paired_ref[...], total)
+    loss_ref[0] = jnp.max(row_share_ref[...] + col_share_ref[...]) * (1.0 / (LOG2_E * whole))
 
 
 def exchanged(blocks, axis):
@@ -283,7 +285,7 @@
     image_rows, text_rows = own_rows * inner, own_rows * chips
     wide = width + EXTRA
     work = 2 * image_rows * text_rows * width
-    far, fars = place(FAR), lax.axis_size(FAR)
+    high, low = place(FAR[0]), place(FAR[1])
     tile = shape((8, 128), f32)
 
     text_copies = kernel_call(text_units_kernel, shape((text_rows, width), bf16), text_emb)
@@ -292,9 +294,11 @@
     half, diagonal = kernel_call(
         image_units_kernel, (shape((own_rows, width), bf16), tile), image_emb, text_emb
     )
+    two = kernel_call(
+        join_kernel, shape((2 * own_rows, width), bf16), low, half, swapped(half, FAR, 1)
+    )
     image_copies = kernel_call(
-        join_kernel, shape((image_rows, width), bf16),
-        far, half, *(swapped(half, FAR, k) for k in range(1, fars)),
+        join_kernel, shape((image_rows, width), bf16), high, two, swapped(two, FAR, 3)
     )
     image_group = exchanged(after(image_copies, text_own), NEAR)
 
@@ -304,10 +308,11 @@
     )
     row_pieces = exchanged(row_message, INNER)
     col_part = kernel_call(columns_kernel, tile, *tile_of, flops=2 * work)
+    pair = kernel_call(pair_columns_kernel, tile, col_part, swapped(col_part, CORE))
     col_message = kernel_call(
-        pair_columns_kernel, shape((chips, 8, 128), f32), col_part, swapped(col_part, CORE)
-    )
-    col_pieces = exchanged(after(col_message, row_pieces), CHIPS)
+        message_kernel, shape((chips, 8, 128), f32), row_pieces, pair
+    )
+    col_pieces = exchanged(col_message, CHIPS)
 
     half_tile = shape((image_rows, text_rows), bf16)
     image_part, *weights, row_share = kernel_call(
@@ -323,26 +328,31 @@
         flops=2 * work,
     )
     image_pieces = exchanged(image_part, NEAR)
-    text_part = kernel_call(
-        pair_sums_kernel, shape((text_rows, wide), bf16),
+    text_part, row_share = kernel_call(
+        pair_sums_kernel, (shape((text_rows, width), bf16), tile),
         own_part, swapped(other_part, CORE), row_share,
     )
     text_pieces = exchanged(after(text_part, image_pieces), CHIPS)
 
-    sent = [shape((own_rows, wide), bf16)] * (fars - 1)
-    kept, *sent, share = kernel_call(
-        near_sums_kernel, (shape((own_rows, width), f32), *sent, tile), far, image_pieces
+    kept, sent, share = kernel_call(
+        near_sums_kernel,
+        (shape((2 * own_rows, width), f32), shape((2 * own_rows, wide), bf16), tile),
+        high, image_pieces,
+    )
+    kept, sent, share = kernel_call(
+        middle_sums_kernel,
+        (shape((own_rows, width), f32), shape((own_rows, wide), bf16), tile),
+        low, kept, swapped(sent, FAR, 3), share,
     )
     out = shape((own_rows, width), f32)
     image_grad, share = kernel_call(
         image_gradient_kernel, (out, tile),
-        factor, image_emb, text_emb, kept, share,
-        *(swapped(block, FAR, k + 1) for k, block in enumerate(sent)),
+        factor, image_emb, text_emb, kept, swapped(sent, FAR, 1), share,
     )
     whole = 2.0 * own_rows * inner * chips * lax.axis_size(CORE)
     text_grad, mean_loss = kernel_call(
         functools.partial(text_gradient_kernel, whole), (out, shape((1,), f32)),
-        factor, text_emb, image_emb, text_pieces, share,
+        factor, text_emb, image_emb, text_pieces, row_share, share,
     )
     return (mean_loss, image_grad, text_grad)
 

time: 121 us -> 119 us (0.983)
  starting transfers between devices: 64.4 us -> 56.1 us
  waiting for transfers between devices: 26.2 us -> 32.3 us
    ppermute x9 -> x7, starting transfers between devices: 30.2 us -> 20.6 us  [swapped(): lax.ppermute(x, axis, [(k, k ^ offset) for k in range(lax.axis_size(axis))])]
    ppermute x9 -> x7, waiting for transfers between devices: 13.3 us -> 21.8 us  [swapped(): lax.ppermute(x, axis, [(k, k ^ offset) for k in range(lax.axis_size(axis))])]
    all_to_all x5, waiting for transfers between devices: 12.9 us -> 10.5 us  [exchanged(): lax.all_to_all(split, axis, split_axis=0, concat_axis=0, tiled=True)]
    all_to_all x5, starting transfers between devices: 34.2 us -> 35.5 us  [exchanged(): lax.all_to_all(split, axis, split_axis=0, concat_axis=0, tiled=True)]
    pallas_call x12 -> x15, Pallas kernels: 11 us -> 11.1 us  [kernel_call(): pl.pallas_call(body, out_shape=out_shape, in_specs=[spec(a) for a in args...]
  transfers between devices with their start and end apart: 14 -> 12, of which waited for: 11 -> 12; matrix products, arithmetic and copies ran while one was open for 0% -> 0% of each run, Pallas kernels for 4% -> 4%
where the time goes in v7:
time: 119 us
  starting transfers between devices  56.1 us (47%)
  waiting for transfers between devices  32.3 us (27%)
  blocking collectives  16.9 us (14%)
  Pallas kernels  11.1 us (9%)
  between operations  1.43 us (1%)
    all_to_all x5, starting transfers between devices, exchanged(): lax.all_to_all(split, axis, split_axis=0, concat_axis=0, tiled=True)  35.5 us
    ppermute x7, waiting for transfers between devices, swapped(): lax.ppermute(x, axis, [(k, k ^ offset) for k in range(lax.axis_size(axis))])  21.8 us
    ppermute x7, starting transfers between devices, swapped(): lax.ppermute(x, axis, [(k, k ^ offset) for k in range(lax.axis_size(axis))])  20.6 us
    all_to_all x1, blocking collectives, exchanged(): lax.all_to_all(split, axis, split_axis=0, concat_axis=0, tiled=True)  16.9 us
    pallas_call x15, Pallas kernels, kernel_call(): pl.pallas_call(body, out_shape=out_shape, in_specs=[spec(a) for a in args...  11.1 us
    all_to_all x5, waiting for transfers between devices, exchanged(): lax.all_to_all(split, axis, split_axis=0, concat_axis=0, tiled=True)  10.5 us
  transfers between devices with their start and end apart: 12, of which 12 were waited for; matrix products, arithmetic and copies ran while one was open for 0% of the time, Pallas kernels for 4%

profile of v7, /device:TPU:8, one launch (start us, length us, event | category | flops | bytes accessed | tf_op | source)
XLA Modules:
  0.0 118.7 jit_solution(4692921928033978026)
XLA Ops:
  0.6 0.0 copy-start
  0.6 0.9 copy-done
  1.5 0.0 copy-start.1
  1.5 0.0 copy-start.2
  1.5 1.0 shard_map.61
  2.5 12.9 %all-to-all-start = ((bf16[16,24,768]{2,1,0:T(8,128)(2,1)}), bf16[16,24,768]{2,1,0:T(8,128)(2,1)S(1)}, u32[]{:S(2)}, u32[]{:S(2)}) async-start(bf16[16,24,768]{2,1,0:T(8,128)(2,1)} %bitcast.2), calls=%async_computation | async-start | bytes 1179648 | tf_op jit(solution)/shard_map/all_to_all | solution.py:262
  15.4 0.0 copy-done.1
  15.4 0.0 copy-done.2
  15.4 0.2 shard_map.58
  15.6 4.5 %collective-permute-start = (bf16[24,768]{1,0:T(8,128)(2,1)S(1)}, bf16[24,768]{1,0:T(8,128)(2,1)S(1)}, u32[]{:S(2)}, u32[]{:S(2)}) collective-permute-start(bf16[24,768]{1,0:T(8,128)(2,1)S(1)} %get-tuple-element.25.mine_ref), channel_id=1, source_target_pairs={{0,64},{64,0},{128,192},{192,128},{1,65},{65,1},{129,193},{193,129... | collective-permute-start | bytes 110600 | tf_op jit(solution)/shard_map/ppermute | solution.py:266
  20.1 2.2 %collective-permute-done.theirs_ref = bf16[24,768]{1,0:T(8,128)(2,1)S(1)} collective-permute-done((bf16[24,768]{1,0:T(8,128)(2,1)S(1)}, bf16[24,768]{1,0:T(8,128)(2,1)S(1)}, u32[]{:S(2)}, u32[]{:S(2)}) %collective-permute-start) | collective-permute-done | bytes 36896 | tf_op jit(solution)/shard_map/ppermute | solution.py:266
  22.4 5.3 %collective-permute-start.1 = (bf16[48,768]{1,0:T(8,128)(2,1)S(1)}, bf16[48,768]{1,0:T(8,128)(2,1)S(1)}, u32[]{:S(2)}, u32[]{:S(2)}) collective-permute-start(bf16[48,768]{1,0:T(8,128)(2,1)S(1)} %shard_map.59.mine_ref), channel_id=1, source_target_pairs={{0,192},{64,128},{128,64},{192,0},{1,193},{65,129},{129,65},{193,1... | collective-permute-start | bytes 221192 | tf_op jit(solution)/shard_map/ppermute | solution.py:266
  27.7 3.9 %collective-permute-done.1.theirs_ref = bf16[48,768]{1,0:T(8,128)(2,1)S(1)} collective-permute-done((bf16[48,768]{1,0:T(8,128)(2,1)S(1)}, bf16[48,768]{1,0:T(8,128)(2,1)S(1)}, u32[]{:S(2)}, u32[]{:S(2)}) %collective-permute-start.1) | collective-permute-done | bytes 73760 | tf_op jit(solution)/shard_map/ppermute | solution.py:266
  31.5 0.9 shard_map.60
  32.4 0.3 all-to-all-done
  32.7 6.9 %all-to-all-start.1 = ((bf16[4,96,768]{2,1,0:T(8,128)(2,1)}), bf16[4,96,768]{2,1,0:T(8,128)(2,1)S(1)}, u32[]{:S(2)}, u32[]{:S(2)}) async-start(bf16[4,96,768]{2,1,0:T(8,128)(2,1)} %bitcast.4), calls=%async_computation.1 | async-start | bytes 1179648 | tf_op jit(solution)/shard_map/all_to_all | solution.py:262
  39.6 1.9 %collective-permute-start.2 = (bf16[384,768]{1,0:T(8,128)(2,1)S(1)}, bf16[384,768]{1,0:T(8,128)(2,1)S(1)}, u32[]{:S(2)}, u32[]{:S(2)}) collective-permute-start(bf16[384,768]{1,0:T(8,128)(2,1)S(1)} %bitcast.10), channel_id=1, source_target_pairs={{0,1},{1,0},{2,3},{3,2},{4,5},{5,4},{6,7},{7,6},{8,9},{9,8},{10,11... | collective-permute-start | bytes 1769480 | tf_op jit(solution)/shard_map/ppermute | solution.py:266
  42.1 1.3 %collective-permute-done.2.other_ref = bf16[384,768]{1,0:T(8,128)(2,1)S(1)} collective-permute-done((bf16[384,768]{1,0:T(8,128)(2,1)S(1)}, bf16[384,768]{1,0:T(8,128)(2,1)S(1)}, u32[]{:S(2)}, u32[]{:S(2)}) %collective-permute-start.2) | collective-permute-done | bytes 589856 | tf_op jit(solution)/shard_map/ppermute | solution.py:266
  43.5 2.5 %all-to-all-done.1 = bf16[4,96,768]{2,1,0:T(8,128)(2,1)S(1)} async-done(((bf16[4,96,768]{2,1,0:T(8,128)(2,1)}), bf16[4,96,768]{2,1,0:T(8,128)(2,1)S(1)}, u32[]{:S(2)}, u32[]{:S(2)}) %all-to-all-start.1) | async-done | bytes 589856 | tf_op jit(solution)/shard_map/all_to_all | solution.py:262
  45.9 1.6 %shard_map.62 = f32[16,8,128]{2,1,0:T(8,128)} custom-call(f32[1]{0:T(128)S(6)} %copy.6.factor_ref, bf16[384,768]{1,0:T(8,128)(2,1)S(1)} %bitcast.14, bf16[384,768]{1,0:T(8,128)(2,1)S(1)} %bitcast.11, bf16[384,768]{1,0:T(8,128)(2,1)S(1)} %collective-permute-done.2.other_ref, f32[8,128]{1,0:T(8,128)S(1)} %get-tuple-element.27.diagonal_ref), custom_call_target="tpu_custom_call" | custom-call | flops 452984832 | bytes 1839108 | tf_op jit(solution)/shard_map/pallas_call | solution.py:41
  47.5 7.7 %all-to-all-start.2 = ((f32[16,8,128]{2,1,0:T(8,128)}), f32[16,8,128]{2,1,0:T(8,128)S(1)}, u32[]{:S(2)}, u32[]{:S(2)}) async-start(f32[16,8,128]{2,1,0:T(8,128)} %shard_map.62), calls=%async_computation.2 | async-start | bytes 131072 | tf_op jit(solution)/shard_map/all_to_all | solution.py:262
  55.3 0.9 shard_map.63.mine_ref
  56.2 1.9 %collective-permute-start.3 = (f32[8,128]{1,0:T(8,128)S(1)}, f32[8,128]{1,0:T(8,128)S(1)}, u32[]{:S(2)}, u32[]{:S(2)}) collective-permute-start(f32[8,128]{1,0:T(8,128)S(1)} %shard_map.63.mine_ref), channel_id=1, source_target_pairs={{0,1},{1,0},{2,3},{3,2},{4,5},{5,4},{6,7},{7,6},{8,9},{9,8},{10,11... | collective-permute-start | bytes 12296 | tf_op jit(solution)/shard_map/ppermute | solution.py:266
  58.1 1.1 collective-permute-done.3.theirs_ref
  59.2 3.6 %all-to-all-done.2.row_ref = f32[16,8,128]{2,1,0:T(8,128)S(1)} async-done(((f32[16,8,128]{2,1,0:T(8,128)}), f32[16,8,128]{2,1,0:T(8,128)S(1)}, u32[]{:S(2)}, u32[]{:S(2)}) %all-to-all-start.2) | async-done | bytes 65568 | tf_op jit(solution)/shard_map/all_to_all | solution.py:262
  62.9 0.2 shard_map.65
  63.0 16.9 %all_to_all.30.pieces_ref = f32[16,8,128]{2,1,0:T(8,128)S(1)} all-to-all(f32[16,8,128]{2,1,0:T(8,128)S(1)} %shard_map.65), channel_id=1, replica_groups=mesh['z0'=2,'y2'=2,'y1'=2,'y0'=2,'x'=4,'zh'=4,'c'=2] {'x','zh'}, dimensions={0} | all-to-all | bytes 131072 | tf_op jit(solution)/shard_map/all_to_all | solution.py:262
  79.9 2.5 %shard_map.66 = (bf16[384,896]{1,0:T(8,128)(2,1)}, bf16[384,384]{1,0:T(8,128)(2,1)S(1)}, bf16[384,384]{1,0:T(8,128)(2,1)S(1)}, f32[8,128]{1,0:T(8,128)S(1)}) custom-call(f32[1]{0:T(128)S(6)} %copy.6.factor_ref, bf16[384,768]{1,0:T(8,128)(2,1)S(1)} %bitcast.16, bf16[384,768]{1,0:T(8,128)(2,1)S(1)} %bitcast.13, ...), custom_call_target="tpu_custom_call" | custom-call | flops 905969664 | bytes 3182596 | tf_op jit(solution)/shard_map/pallas_call | solution.py:41
  82.4 4.5 %all-to-all-start.4 = ((bf16[4,96,896]{2,1,0:T(8,128)(2,1)}), bf16[4,96,896]{2,1,0:T(8,128)(2,1)S(1)}, u32[]{:S(2)}, u32[]{:S(2)}) async-start(bf16[4,96,896]{2,1,0:T(8,128)(2,1)} %bitcast.6), calls=%async_computation.4 | async-start | bytes 1376256 | tf_op jit(solution)/shard_map/all_to_all | solution.py:262
  86.9 0.8 shard_map.67
  87.7 1.9 %collective-permute-start.4 = (bf16[384,896]{1,0:T(8,128)(2,1)S(1)}, bf16[384,896]{1,0:T(8,128)(2,1)S(1)}, u32[]{:S(2)}, u32[]{:S(2)}) collective-permute-start(bf16[384,896]{1,0:T(8,128)(2,1)S(1)} %get-tuple-element.32), channel_id=1, source_target_pairs={{0,1},{1,0},{2,3},{3,2},{4,5},{5,4},{6,7},{7,6},{8,9},{9,8},{10,11... | collective-permute-start | bytes 2064392 | tf_op jit(solution)/shard_map/ppermute | solution.py:266
  89.6 2.1 %collective-permute-done.4.theirs_ref = bf16[384,896]{1,0:T(8,128)(2,1)S(1)} collective-permute-done((bf16[384,896]{1,0:T(8,128)(2,1)S(1)}, bf16[384,896]{1,0:T(8,128)(2,1)S(1)}, u32[]{:S(2)}, u32[]{:S(2)}) %collective-permute-start.4) | collective-permute-done | bytes 688160 | tf_op jit(solution)/shard_map/ppermute | solution.py:266
  91.7 1.0 shard_map.68
  92.8 1.0 all-to-all-done.4
  93.8 3.6 %all-to-all-start.5 = ((bf16[16,24,768]{2,1,0:T(8,128)(2,1)}), bf16[16,24,768]{2,1,0:T(8,128)(2,1)S(1)}, u32[]{:S(2)}, u32[]{:S(2)}) async-start(bf16[16,24,768]{2,1,0:T(8,128)(2,1)} %bitcast.8), calls=%async_computation.5 | async-start | bytes 1179648 | tf_op jit(solution)/shard_map/all_to_all | solution.py:262
  97.4 0.2 shard_map.69
  97.5 3.0 %collective-permute-start.5 = (bf16[48,896]{1,0:T(8,128)(2,1)S(1)}, bf16[48,896]{1,0:T(8,128)(2,1)S(1)}, u32[]{:S(2)}, u32[]{:S(2)}) collective-permute-start(bf16[48,896]{1,0:T(8,128)(2,1)S(1)} %get-tuple-element.38), channel_id=1, source_target_pairs={{0,192},{64,128},{128,64},{192,0},{1,193},{65,129},{129,65},{193,1... | collective-permute-start | bytes 258056 | tf_op jit(solution)/shard_map/ppermute | solution.py:266
  100.6 6.4 %collective-permute-done.5.theirs_ref = bf16[48,896]{1,0:T(8,128)(2,1)S(1)} collective-permute-done((bf16[48,896]{1,0:T(8,128)(2,1)S(1)}, bf16[48,896]{1,0:T(8,128)(2,1)S(1)}, u32[]{:S(2)}, u32[]{:S(2)}) %collective-permute-start.5) | collective-permute-done | bytes 86048 | tf_op jit(solution)/shard_map/ppermute | solution.py:266
  107.0 0.1 shard_map.70
  107.1 2.0 %collective-permute-start.6 = (bf16[24,896]{1,0:T(8,128)(2,1)S(1)}, bf16[24,896]{1,0:T(8,128)(2,1)S(1)}, u32[]{:S(2)}, u32[]{:S(2)}) collective-permute-start(bf16[24,896]{1,0:T(8,128)(2,1)S(1)} %get-tuple-element.41), channel_id=1, source_target_pairs={{0,64},{64,0},{128,192},{192,128},{1,65},{65,1},{129,193},{193,129... | collective-permute-start | bytes 129032 | tf_op jit(solution)/shard_map/ppermute | solution.py:266
  109.1 4.8 %collective-permute-done.6.theirs_ref = bf16[24,896]{1,0:T(8,128)(2,1)S(1)} collective-permute-done((bf16[24,896]{1,0:T(8,128)(2,1)S(1)}, bf16[24,896]{1,0:T(8,128)(2,1)S(1)}, u32[]{:S(2)}, u32[]{:S(2)}) %collective-permute-start.6) | collective-permute-done | bytes 43040 | tf_op jit(solution)/shard_map/ppermute | solution.py:266
  113.9 0.8 shard_map.71
  114.7 3.1 %all-to-all-done.5 = bf16[16,24,768]{2,1,0:T(8,128)(2,1)S(1)} async-done(((bf16[16,24,768]{2,1,0:T(8,128)(2,1)}), bf16[16,24,768]{2,1,0:T(8,128)(2,1)S(1)}, u32[]{:S(2)}, u32[]{:S(2)}) %all-to-all-start.5) | async-done | bytes 589856 | tf_op jit(solution)/shard_map/all_to_all | solution.py:262
  117.8 0.8 shard_map.72
  (2 shorter events, 0.0 us)
Async XLA Ops:
  0.6 0.9 copy-start
  1.5 13.8 %copy-start.1 = (f32[24,768]{1,0:T(8,128)S(1)}, f32[24,768]{1,0:T(8,128)}, u32[]{:S(2)}) copy-start(f32[24,768]{1,0:T(8,128)} %values_ref.7) | copy-start | bytes 221188
  1.5 13.8 %copy-start.2 = (f32[24,768]{1,0:T(8,128)S(1)}, f32[24,768]{1,0:T(8,128)}, u32[]{:S(2)}) copy-start(f32[24,768]{1,0:T(8,128)} %paired_ref.3) | copy-start | bytes 221188
  2.5 30.2 %all-to-all-start = ((bf16[16,24,768]{2,1,0:T(8,128)(2,1)}), bf16[16,24,768]{2,1,0:T(8,128)(2,1)S(1)}, u32[]{:S(2)}, u32[]{:S(2)}) async-start(bf16[16,24,768]{2,1,0:T(8,128)(2,1)} %bitcast.2), calls=%async_computation | async-start | bytes 1179648 | tf_op jit(solution)/shard_map/all_to_all | solution.py:262
  15.6 6.8 %collective-permute-start = (bf16[24,768]{1,0:T(8,128)(2,1)S(1)}, bf16[24,768]{1,0:T(8,128)(2,1)S(1)}, u32[]{:S(2)}, u32[]{:S(2)}) collective-permute-start(bf16[24,768]{1,0:T(8,128)(2,1)S(1)} %get-tuple-element.25.mine_ref), channel_id=1, source_target_pairs={{0,64},{64,0},{128,192},{192,128},{1,65},{65,1},{129,193},{193,129... | collective-permute-start | bytes 110600 | tf_op jit(solution)/shard_map/ppermute | solution.py:266
  22.4 9.1 %collective-permute-start.1 = (bf16[48,768]{1,0:T(8,128)(2,1)S(1)}, bf16[48,768]{1,0:T(8,128)(2,1)S(1)}, u32[]{:S(2)}, u32[]{:S(2)}) collective-permute-start(bf16[48,768]{1,0:T(8,128)(2,1)S(1)} %shard_map.59.mine_ref), channel_id=1, source_target_pairs={{0,192},{64,128},{128,64},{192,0},{1,193},{65,129},{129,65},{193,1... | collective-permute-start | bytes 221192 | tf_op jit(solution)/shard_map/ppermute | solution.py:266
  32.7 13.2 %all-to-all-start.1 = ((bf16[4,96,768]{2,1,0:T(8,128)(2,1)}), bf16[4,96,768]{2,1,0:T(8,128)(2,1)S(1)}, u32[]{:S(2)}, u32[]{:S(2)}) async-start(bf16[4,96,768]{2,1,0:T(8,128)(2,1)} %bitcast.4), calls=%async_computation.1 | async-start | bytes 1179648 | tf_op jit(solution)/shard_map/all_to_all | solution.py:262
  39.6 3.9 %collective-permute-start.2 = (bf16[384,768]{1,0:T(8,128)(2,1)S(1)}, bf16[384,768]{1,0:T(8,128)(2,1)S(1)}, u32[]{:S(2)}, u32[]{:S(2)}) collective-permute-start(bf16[384,768]{1,0:T(8,128)(2,1)S(1)} %bitcast.10), channel_id=1, source_target_pairs={{0,1},{1,0},{2,3},{3,2},{4,5},{5,4},{6,7},{7,6},{8,9},{9,8},{10,11... | collective-permute-start | bytes 1769480 | tf_op jit(solution)/shard_map/ppermute | solution.py:266
  47.5 15.3 %all-to-all-start.2 = ((f32[16,8,128]{2,1,0:T(8,128)}), f32[16,8,128]{2,1,0:T(8,128)S(1)}, u32[]{:S(2)}, u32[]{:S(2)}) async-start(f32[16,8,128]{2,1,0:T(8,128)} %shard_map.62), calls=%async_computation.2 | async-start | bytes 131072 | tf_op jit(solution)/shard_map/all_to_all | solution.py:262
  56.2 3.1 %collective-permute-start.3 = (f32[8,128]{1,0:T(8,128)S(1)}, f32[8,128]{1,0:T(8,128)S(1)}, u32[]{:S(2)}, u32[]{:S(2)}) collective-permute-start(f32[8,128]{1,0:T(8,128)S(1)} %shard_map.63.mine_ref), channel_id=1, source_target_pairs={{0,1},{1,0},{2,3},{3,2},{4,5},{5,4},{6,7},{7,6},{8,9},{9,8},{10,11... | collective-permute-start | bytes 12296 | tf_op jit(solution)/shard_map/ppermute | solution.py:266
  82.4 11.4 %all-to-all-start.4 = ((bf16[4,96,896]{2,1,0:T(8,128)(2,1)}), bf16[4,96,896]{2,1,0:T(8,128)(2,1)S(1)}, u32[]{:S(2)}, u32[]{:S(2)}) async-start(bf16[4,96,896]{2,1,0:T(8,128)(2,1)} %bitcast.6), calls=%async_computation.4 | async-start | bytes 1376256 | tf_op jit(solution)/shard_map/all_to_all | solution.py:262
  87.7 4.0 %collective-permute-start.4 = (bf16[384,896]{1,0:T(8,128)(2,1)S(1)}, bf16[384,896]{1,0:T(8,128)(2,1)S(1)}, u32[]{:S(2)}, u32[]{:S(2)}) collective-permute-start(bf16[384,896]{1,0:T(8,128)(2,1)S(1)} %get-tuple-element.32), channel_id=1, source_target_pairs={{0,1},{1,0},{2,3},{3,2},{4,5},{5,4},{6,7},{7,6},{8,9},{9,8},{10,11... | collective-permute-start | bytes 2064392 | tf_op jit(solution)/shard_map/ppermute | solution.py:266
  93.8 24.0 %all-to-all-start.5 = ((bf16[16,24,768]{2,1,0:T(8,128)(2,1)}), bf16[16,24,768]{2,1,0:T(8,128)(2,1)S(1)}, u32[]{:S(2)}, u32[]{:S(2)}) async-start(bf16[16,24,768]{2,1,0:T(8,128)(2,1)} %bitcast.8), calls=%async_computation.5 | async-start | bytes 1179648 | tf_op jit(solution)/shard_map/all_to_all | solution.py:262
  97.5 9.4 %collective-permute-start.5 = (bf16[48,896]{1,0:T(8,128)(2,1)S(1)}, bf16[48,896]{1,0:T(8,128)(2,1)S(1)}, u32[]{:S(2)}, u32[]{:S(2)}) collective-permute-start(bf16[48,896]{1,0:T(8,128)(2,1)S(1)} %get-tuple-element.38), channel_id=1, source_target_pairs={{0,192},{64,128},{128,64},{192,0},{1,193},{65,129},{129,65},{193,1... | collective-permute-start | bytes 258056 | tf_op jit(solution)/shard_map/ppermute | solution.py:266
  107.1 6.8 %collective-permute-start.6 = (bf16[24,896]{1,0:T(8,128)(2,1)S(1)}, bf16[24,896]{1,0:T(8,128)(2,1)S(1)}, u32[]{:S(2)}, u32[]{:S(2)}) collective-permute-start(bf16[24,896]{1,0:T(8,128)(2,1)S(1)} %get-tuple-element.41), channel_id=1, source_target_pairs={{0,64},{64,0},{128,192},{192,128},{1,65},{65,1},{129,193},{193,129... | collective-permute-start | bytes 129032 | tf_op jit(solution)/shard_map/ppermute | solution.py:266

commit v8 on v7

--- a/solution.py
+++ b/solution.py
@@ -9,9 +9,9 @@
 from jax.sharding import PartitionSpec as P
 
 ALL = ("z0", "y2", "y1", "y0", "x", "zh", "c")
-INNER = ("z0", "y2", "y1", "y0")
-CHIPS = ("x", "zh")
-NEAR = ("z0", "y0")
+INNER = ("y2", "y1", "x")
+CHIPS = ("y0", "zh", "z0")
+NEAR = "x"
 FAR = ("y2", "y1")
 CORE = "c"
 
@@ -135,8 +135,8 @@
     message_ref[...] = eight([*lines(own), *lines(other)])
 
 
-def pair_columns_kernel(mine_ref, theirs_ref, pair_ref):
-    mine, theirs = mine_ref[...], theirs_ref[...]
+def pair_columns_kernel(core_ref, both_ref, pair_ref):
+    mine, theirs = both_ref[core_ref[0]], both_ref[1 - core_ref[0]]
     own = pair_lse(mine[0:3], theirs[3:6])
     other = pair_lse(mine[3:6], theirs[0:3])
     pair_ref[...] = jnp.concatenate([own, other, jnp.zeros((2, 128), jnp.float32)], axis=0)
@@ -285,7 +285,7 @@
     image_rows, text_rows = own_rows * inner, own_rows * chips
     wide = width + EXTRA
     work = 2 * image_rows * text_rows * width
-    high, low = place(FAR[0]), place(FAR[1])
+    high, low, core = place(FAR[0]), place(FAR[1]), place(CORE)
     tile = shape((8, 128), f32)
 
     text_copies = kernel_call(text_units_kernel, shape((text_rows, width), bf16), text_emb)
@@ -308,7 +308,7 @@
     )
     row_pieces = exchanged(row_message, INNER)
     col_part = kernel_call(columns_kernel, tile, *tile_of, flops=2 * work)
-    pair = kernel_call(pair_columns_kernel, tile, col_part, swapped(col_part, CORE))
+    pair = kernel_call(pair_columns_kernel, tile, core, lax.all_gather(col_part, CORE))
     col_message = kernel_call(
         message_kernel, shape((chips, 8, 128), f32), row_pieces, pair
     )

time: 119 us -> 138 us (1.16)
  blocking collectives: 16.9 us -> 42.6 us
  starting transfers between devices: 56.1 us -> 38.1 us
  waiting for transfers between devices: 32.3 us -> 43.5 us
  local copies, waits for them, and re-layouts: 0.88 us -> 2.55 us
  Pallas kernels: 11.1 us -> 9.44 us
    all_to_all x1 -> x2, blocking collectives: 16.9 us -> 40.8 us  [exchanged(): lax.all_to_all(split, axis, split_axis=0, concat_axis=0, tiled=True)]
    all_to_all x5 -> x4, starting transfers between devices: 35.5 us -> 19.5 us  [exchanged(): lax.all_to_all(split, axis, split_axis=0, concat_axis=0, tiled=True)]
    all_to_all x5 -> x4, waiting for transfers between devices: 10.5 us -> 26.3 us  [exchanged(): lax.all_to_all(split, axis, split_axis=0, concat_axis=0, tiled=True)]
    ppermute x7 -> x6, waiting for transfers between devices: 21.8 us -> 17.2 us  [swapped(): lax.ppermute(x, axis, [(k, k ^ offset) for k in range(lax.axis_size(axis))])]
    ppermute x7 -> x6, starting transfers between devices: 20.6 us -> 18.6 us  [swapped(): lax.ppermute(x, axis, [(k, k ^ offset) for k in range(lax.axis_size(axis))])]
    all_gather x0 -> x1, blocking collectives: none -> 1.8 us  [on_device(): lax.all_gather(col_part, CORE)]
    unnamed x6 -> x10, local copies, waits for them, and re-layouts: 0.88 us -> 2.55 us
    pallas_call x15, Pallas kernels: 11.1 us -> 9.44 us  [kernel_call(): pl.pallas_call(body, out_shape=out_shape, in_specs=[spec(a) for a in args...]
  transfers between devices with their start and end apart: 12 -> 10, of which waited for: 12 -> 7; matrix products, arithmetic and copies ran while one was open for 0% -> 0% of each run, Pallas kernels for 4% -> 2%
where the time goes in v8:
time: 138 us
  waiting for transfers between devices  43.5 us (32%)
  blocking collectives  42.6 us (31%)
  starting transfers between devices  38.1 us (28%)
  Pallas kernels  9.44 us (7%)
  local copies, waits for them, and re-layouts  2.55 us (2%)
  between operations  1.46 us (1%)
    all_to_all x2, blocking collectives, exchanged(): lax.all_to_all(split, axis, split_axis=0, concat_axis=0, tiled=True)  40.8 us
    all_to_all x4, waiting for transfers between devices, exchanged(): lax.all_to_all(split, axis, split_axis=0, concat_axis=0, tiled=True)  26.3 us
    all_to_all x4, starting transfers between devices, exchanged(): lax.all_to_all(split, axis, split_axis=0, concat_axis=0, tiled=True)  19.5 us
    ppermute x6, starting transfers between devices, swapped(): lax.ppermute(x, axis, [(k, k ^ offset) for k in range(lax.axis_size(axis))])  18.6 us
    ppermute x6, waiting for transfers between devices, swapped(): lax.ppermute(x, axis, [(k, k ^ offset) for k in range(lax.axis_size(axis))])  17.2 us
    pallas_call x15, Pallas kernels, kernel_call(): pl.pallas_call(body, out_shape=out_shape, in_specs=[spec(a) for a in args...  9.44 us
  transfers between devices with their start and end apart: 10, of which 7 were waited for; matrix products, arithmetic and copies ran while one was open for 0% of the time, Pallas kernels for 2%

profile of v8, /device:TPU:8, one launch (start us, length us, event | category | flops | bytes accessed | tf_op | source)
XLA Modules:
  0.0 137.7 jit_solution(4035522981681811504)
XLA Ops:
  0.6 0.0 copy-start
  0.6 0.9 copy-done
  1.5 0.0 copy-start.1
  1.5 0.0 copy-start.3
  1.5 0.1 shard_map.61
  1.7 30.1 %all_to_all.30 = bf16[16,24,768]{2,1,0:T(8,128)(2,1)S(1)} all-to-all(bf16[16,24,768]{2,1,0:T(8,128)(2,1)S(1)} %bitcast.22), channel_id=1, replica_groups=mesh['z0'=2,'y2'=2,'y1'=2,'y0'=2,'x'=4,'zh'=4,'c'=2] {'y0','zh','z0'}, dimensions={0} | all-to-all | bytes 1179648 | tf_op jit(solution)/shard_map/all_to_all | solution.py:262
  31.8 1.9 %collective-permute-start.2 = (bf16[384,768]{1,0:T(8,128)(2,1)S(1)}, bf16[384,768]{1,0:T(8,128)(2,1)S(1)}, u32[]{:S(2)}, u32[]{:S(2)}) collective-permute-start(bf16[384,768]{1,0:T(8,128)(2,1)S(1)} %bitcast.12), channel_id=1, source_target_pairs={{0,1},{1,0},{2,3},{3,2},{4,5},{5,4},{6,7},{7,6},{8,9},{9,8},{10,11... | collective-permute-start | bytes 1769480 | tf_op jit(solution)/shard_map/ppermute | solution.py:266
  33.7 0.0 copy-done.1
  33.7 0.0 copy-done.3
  33.7 0.2 shard_map.58
  33.9 4.5 %collective-permute-start = (bf16[24,768]{1,0:T(8,128)(2,1)S(1)}, bf16[24,768]{1,0:T(8,128)(2,1)S(1)}, u32[]{:S(2)}, u32[]{:S(2)}) collective-permute-start(bf16[24,768]{1,0:T(8,128)(2,1)S(1)} %get-tuple-element.25.mine_ref), channel_id=1, source_target_pairs={{0,64},{64,0},{128,192},{192,128},{1,65},{65,1},{129,193},{193,129... | collective-permute-start | bytes 110600 | tf_op jit(solution)/shard_map/ppermute | solution.py:266
  38.5 2.2 %collective-permute-done.theirs_ref = bf16[24,768]{1,0:T(8,128)(2,1)S(1)} collective-permute-done((bf16[24,768]{1,0:T(8,128)(2,1)S(1)}, bf16[24,768]{1,0:T(8,128)(2,1)S(1)}, u32[]{:S(2)}, u32[]{:S(2)}) %collective-permute-start) | collective-permute-done | bytes 36896 | tf_op jit(solution)/shard_map/ppermute | solution.py:266
  40.7 5.6 %collective-permute-start.1 = (bf16[48,768]{1,0:T(8,128)(2,1)S(1)}, bf16[48,768]{1,0:T(8,128)(2,1)S(1)}, u32[]{:S(2)}, u32[]{:S(2)}) collective-permute-start(bf16[48,768]{1,0:T(8,128)(2,1)S(1)} %shard_map.59.mine_ref), channel_id=1, source_target_pairs={{0,192},{64,128},{128,64},{192,0},{1,193},{65,129},{129,65},{193,1... | collective-permute-start | bytes 221192 | tf_op jit(solution)/shard_map/ppermute | solution.py:266
  46.3 3.2 %collective-permute-done.1.theirs_ref = bf16[48,768]{1,0:T(8,128)(2,1)S(1)} collective-permute-done((bf16[48,768]{1,0:T(8,128)(2,1)S(1)}, bf16[48,768]{1,0:T(8,128)(2,1)S(1)}, u32[]{:S(2)}, u32[]{:S(2)}) %collective-permute-start.1) | collective-permute-done | bytes 73760 | tf_op jit(solution)/shard_map/ppermute | solution.py:266
  49.5 0.9 shard_map.60
  50.4 4.3 %all-to-all-start.1 = ((bf16[4,96,768]{2,1,0:T(8,128)(2,1)}), bf16[4,96,768]{2,1,0:T(8,128)(2,1)S(1)}, u32[]{:S(2)}, u32[]{:S(2)}) async-start(bf16[4,96,768]{2,1,0:T(8,128)(2,1)} %bitcast.4), calls=%async_computation.1 | async-start | bytes 1179648 | tf_op jit(solution)/shard_map/all_to_all | solution.py:262
  55.3 7.9 %all-to-all-done.1 = bf16[4,96,768]{2,1,0:T(8,128)(2,1)S(1)} async-done(((bf16[4,96,768]{2,1,0:T(8,128)(2,1)}), bf16[4,96,768]{2,1,0:T(8,128)(2,1)S(1)}, u32[]{:S(2)}, u32[]{:S(2)}) %all-to-all-start.1) | async-done | bytes 589856 | tf_op jit(solution)/shard_map/all_to_all | solution.py:262
  63.2 0.0 collective-permute-done.2.other_ref
  63.3 1.6 %shard_map.62 = f32[16,8,128]{2,1,0:T(8,128)} custom-call(f32[1]{0:T(128)S(6)} %copy.6.factor_ref, bf16[384,768]{1,0:T(8,128)(2,1)S(1)} %bitcast.16, bf16[384,768]{1,0:T(8,128)(2,1)S(1)} %bitcast.13, bf16[384,768]{1,0:T(8,128)(2,1)S(1)} %collective-permute-done.2.other_ref, f32[8,128]{1,0:T(8,128)S(1)} %get-tuple-element.27.diagonal_ref), custom_call_target="tpu_custom_call" | custom-call | flops 452984832 | bytes 1839108 | tf_op jit(solution)/shard_map/pallas_call | solution.py:41
  64.9 6.9 %all-to-all-start.2 = ((f32[16,8,128]{2,1,0:T(8,128)}), f32[16,8,128]{2,1,0:T(8,128)S(1)}, u32[]{:S(2)}, u32[]{:S(2)}) async-start(f32[16,8,128]{2,1,0:T(8,128)} %shard_map.62), calls=%async_computation.2 | async-start | bytes 131072 | tf_op jit(solution)/shard_map/all_to_all | solution.py:262
  71.7 0.9 shard_map.63
  72.6 1.8 %all-gather = f32[16,128]{1,0:T(8,128)S(1)} all-gather(f32[8,128]{1,0:T(8,128)S(1)} %shard_map.63), channel_id=2, replica_groups=mesh['z0'=2,'y2'=2,'y1'=2,'y0'=2,'x'=4,'zh'=4,'c'=2] {'c'}, dimensions={0}, use_global_device_ids=true | all-gather | bytes 12288 | tf_op jit(solution)/shard_map/all_gather | solution.py:311
  74.4 7.3 %all-to-all-done.2.row_ref = f32[16,8,128]{2,1,0:T(8,128)S(1)} async-done(((f32[16,8,128]{2,1,0:T(8,128)}), f32[16,8,128]{2,1,0:T(8,128)S(1)}, u32[]{:S(2)}, u32[]{:S(2)}) %all-to-all-start.2) | async-done | bytes 65568 | tf_op jit(solution)/shard_map/all_to_all | solution.py:262
  81.8 0.2 shard_map.65
  81.9 10.7 %all_to_all.31.pieces_ref = f32[16,8,128]{2,1,0:T(8,128)S(1)} all-to-all(f32[16,8,128]{2,1,0:T(8,128)S(1)} %shard_map.65), channel_id=1, replica_groups=mesh['z0'=2,'y2'=2,'y1'=2,'y0'=2,'x'=4,'zh'=4,'c'=2] {'y0','zh','z0'}, dimensions={0} | all-to-all | bytes 131072 | tf_op jit(solution)/shard_map/all_to_all | solution.py:262
  92.7 1.7 %shard_map.66 = (bf16[384,896]{1,0:T(8,128)(2,1)S(1)}, bf16[384,384]{1,0:T(8,128)(2,1)S(1)}, bf16[384,384]{1,0:T(8,128)(2,1)S(1)}, f32[8,128]{1,0:T(8,128)S(1)}) custom-call(f32[1]{0:T(128)S(6)} %copy.6.factor_ref, bf16[384,768]{1,0:T(8,128)(2,1)S(1)} %bitcast.18, bf16[384,768]{1,0:T(8,128)(2,1)S(1)} %bitcast.15, ...), custom_call_target="tpu_custom_call" | custom-call | flops 905969664 | bytes 3182596 | tf_op jit(solution)/shard_map/pallas_call | solution.py:41
  94.3 0.0 copy-start.2
  94.3 0.8 copy-done.2
  95.2 1.6 %shard_map.67 = (f32[384,768]{1,0:T(8,128)S(1)}, bf16[384,896]{1,0:T(8,128)(2,1)}) custom-call(bf16[384,768]{1,0:T(8,128)(2,1)S(1)} %bitcast.19, bf16[384,384]{1,0:T(8,128)(2,1)S(1)} %get-tuple-element.28.own_ref, bf16[384,384]{1,0:T(8,128)(2,1)S(1)} %get-tuple-element.29.other_ref, f32[8,128]{1,0:T(8,128)S(1)} %get-tuple-element.30.share_ref.shared_ref), custom_call_target="tpu_custom_call" | custom-call | flops 452984832 | bytes 3051520 | tf_op jit(solution)/shard_map/pallas_call | solution.py:41
  96.8 1.9 %collective-permute-start.3 = (bf16[384,896]{1,0:T(8,128)(2,1)}, bf16[384,896]{1,0:T(8,128)(2,1)S(1)}, u32[]{:S(2)}, u32[]{:S(2)}) collective-permute-start(bf16[384,896]{1,0:T(8,128)(2,1)} %get-tuple-element.32), channel_id=1, source_target_pairs={{0,1},{1,0},{2,3},{3,2},{4,5},{5,4},{6,7},{7,6},{8,9},{9,8},{10,11... | collective-permute-start | bytes 2064392 | tf_op jit(solution)/shard_map/ppermute | solution.py:266
  98.7 3.5 %all-to-all-start.4 = ((bf16[4,96,896]{2,1,0:T(8,128)(2,1)}), bf16[4,96,896]{2,1,0:T(8,128)(2,1)S(1)}, u32[]{:S(2)}, u32[]{:S(2)}) async-start(bf16[4,96,896]{2,1,0:T(8,128)(2,1)} %bitcast.23), calls=%async_computation.4 | async-start | bytes 1376256 | tf_op jit(solution)/shard_map/all_to_all | solution.py:262
  102.2 0.0 collective-permute-done.3.theirs_ref
  102.2 0.2 shard_map.68
  102.5 0.0 copy-start.4
  102.5 0.8 copy-done.4
  103.3 11.1 %all-to-all-done.4 = bf16[4,96,896]{2,1,0:T(8,128)(2,1)S(1)} async-done(((bf16[4,96,896]{2,1,0:T(8,128)(2,1)}), bf16[4,96,896]{2,1,0:T(8,128)(2,1)S(1)}, u32[]{:S(2)}, u32[]{:S(2)}) %all-to-all-start.4) | async-done | bytes 688160 | tf_op jit(solution)/shard_map/all_to_all | solution.py:262
  114.4 4.8 %all-to-all-start.5 = ((bf16[16,24,768]{2,1,0:T(8,128)(2,1)}), bf16[16,24,768]{2,1,0:T(8,128)(2,1)S(1)}, u32[]{:S(2)}, u32[]{:S(2)}) async-start(bf16[16,24,768]{2,1,0:T(8,128)(2,1)} %bitcast.24), calls=%async_computation.5 | async-start | bytes 1179648 | tf_op jit(solution)/shard_map/all_to_all | solution.py:262
  119.2 0.2 shard_map.69
  119.4 2.6 %collective-permute-start.4 = (bf16[48,896]{1,0:T(8,128)(2,1)S(1)}, bf16[48,896]{1,0:T(8,128)(2,1)S(1)}, u32[]{:S(2)}, u32[]{:S(2)}) collective-permute-start(bf16[48,896]{1,0:T(8,128)(2,1)S(1)} %get-tuple-element.38), channel_id=1, source_target_pairs={{0,192},{64,128},{128,64},{192,0},{1,193},{65,129},{129,65},{193,1... | collective-permute-start | bytes 258056 | tf_op jit(solution)/shard_map/ppermute | solution.py:266
  122.0 7.1 %collective-permute-done.4.theirs_ref = bf16[48,896]{1,0:T(8,128)(2,1)S(1)} collective-permute-done((bf16[48,896]{1,0:T(8,128)(2,1)S(1)}, bf16[48,896]{1,0:T(8,128)(2,1)S(1)}, u32[]{:S(2)}, u32[]{:S(2)}) %collective-permute-start.4) | collective-permute-done | bytes 86048 | tf_op jit(solution)/shard_map/ppermute | solution.py:266
  129.1 0.1 shard_map.70
  129.2 2.2 %collective-permute-start.5 = (bf16[24,896]{1,0:T(8,128)(2,1)S(1)}, bf16[24,896]{1,0:T(8,128)(2,1)S(1)}, u32[]{:S(2)}, u32[]{:S(2)}) collective-permute-start(bf16[24,896]{1,0:T(8,128)(2,1)S(1)} %get-tuple-element.41), channel_id=1, source_target_pairs={{0,64},{64,0},{128,192},{192,128},{1,65},{65,1},{129,193},{193,129... | collective-permute-start | bytes 129032 | tf_op jit(solution)/shard_map/ppermute | solution.py:266
  131.4 4.6 %collective-permute-done.5.theirs_ref = bf16[24,896]{1,0:T(8,128)(2,1)S(1)} collective-permute-done((bf16[24,896]{1,0:T(8,128)(2,1)S(1)}, bf16[24,896]{1,0:T(8,128)(2,1)S(1)}, u32[]{:S(2)}, u32[]{:S(2)}) %collective-permute-start.5) | collective-permute-done | bytes 43040 | tf_op jit(solution)/shard_map/ppermute | solution.py:266
  136.0 0.8 shard_map.71
  136.9 0.0 all-to-all-done.5
  136.9 0.8 shard_map.72
  (2 shorter events, 0.0 us)
Async XLA Ops:
  0.6 0.9 copy-start
  1.5 32.2 %copy-start.1 = (f32[24,768]{1,0:T(8,128)S(1)}, f32[24,768]{1,0:T(8,128)}, u32[]{:S(2)}) copy-start(f32[24,768]{1,0:T(8,128)} %values_ref.7) | copy-start | bytes 221188
  1.5 32.2 %copy-start.3 = (f32[24,768]{1,0:T(8,128)S(1)}, f32[24,768]{1,0:T(8,128)}, u32[]{:S(2)}) copy-start(f32[24,768]{1,0:T(8,128)} %paired_ref.3) | copy-start | bytes 221188
  31.8 31.5 %collective-permute-start.2 = (bf16[384,768]{1,0:T(8,128)(2,1)S(1)}, bf16[384,768]{1,0:T(8,128)(2,1)S(1)}, u32[]{:S(2)}, u32[]{:S(2)}) collective-permute-start(bf16[384,768]{1,0:T(8,128)(2,1)S(1)} %bitcast.12), channel_id=1, source_target_pairs={{0,1},{1,0},{2,3},{3,2},{4,5},{5,4},{6,7},{7,6},{8,9},{9,8},{10,11... | collective-permute-start | bytes 1769480 | tf_op jit(solution)/shard_map/ppermute | solution.py:266
  33.9 6.8 %collective-permute-start = (bf16[24,768]{1,0:T(8,128)(2,1)S(1)}, bf16[24,768]{1,0:T(8,128)(2,1)S(1)}, u32[]{:S(2)}, u32[]{:S(2)}) collective-permute-start(bf16[24,768]{1,0:T(8,128)(2,1)S(1)} %get-tuple-element.25.mine_ref), channel_id=1, source_target_pairs={{0,64},{64,0},{128,192},{192,128},{1,65},{65,1},{129,193},{193,129... | collective-permute-start | bytes 110600 | tf_op jit(solution)/shard_map/ppermute | solution.py:266
  40.7 8.7 %collective-permute-start.1 = (bf16[48,768]{1,0:T(8,128)(2,1)S(1)}, bf16[48,768]{1,0:T(8,128)(2,1)S(1)}, u32[]{:S(2)}, u32[]{:S(2)}) collective-permute-start(bf16[48,768]{1,0:T(8,128)(2,1)S(1)} %shard_map.59.mine_ref), channel_id=1, source_target_pairs={{0,192},{64,128},{128,64},{192,0},{1,193},{65,129},{129,65},{193,1... | collective-permute-start | bytes 221192 | tf_op jit(solution)/shard_map/ppermute | solution.py:266
  50.4 12.9 %all-to-all-start.1 = ((bf16[4,96,768]{2,1,0:T(8,128)(2,1)}), bf16[4,96,768]{2,1,0:T(8,128)(2,1)S(1)}, u32[]{:S(2)}, u32[]{:S(2)}) async-start(bf16[4,96,768]{2,1,0:T(8,128)(2,1)} %bitcast.4), calls=%async_computation.1 | async-start | bytes 1179648 | tf_op jit(solution)/shard_map/all_to_all | solution.py:262
  64.9 16.9 %all-to-all-start.2 = ((f32[16,8,128]{2,1,0:T(8,128)}), f32[16,8,128]{2,1,0:T(8,128)S(1)}, u32[]{:S(2)}, u32[]{:S(2)}) async-start(f32[16,8,128]{2,1,0:T(8,128)} %shard_map.62), calls=%async_computation.2 | async-start | bytes 131072 | tf_op jit(solution)/shard_map/all_to_all | solution.py:262
  94.3 0.9 copy-start.2
  96.8 5.4 %collective-permute-start.3 = (bf16[384,896]{1,0:T(8,128)(2,1)}, bf16[384,896]{1,0:T(8,128)(2,1)S(1)}, u32[]{:S(2)}, u32[]{:S(2)}) collective-permute-start(bf16[384,896]{1,0:T(8,128)(2,1)} %get-tuple-element.32), channel_id=1, source_target_pairs={{0,1},{1,0},{2,3},{3,2},{4,5},{5,4},{6,7},{7,6},{8,9},{9,8},{10,11... | collective-permute-start | bytes 2064392 | tf_op jit(solution)/shard_map/ppermute | solution.py:266
  98.7 15.6 %all-to-all-start.4 = ((bf16[4,96,896]{2,1,0:T(8,128)(2,1)}), bf16[4,96,896]{2,1,0:T(8,128)(2,1)S(1)}, u32[]{:S(2)}, u32[]{:S(2)}) async-start(bf16[4,96,896]{2,1,0:T(8,128)(2,1)} %bitcast.23), calls=%async_computation.4 | async-start | bytes 1376256 | tf_op jit(solution)/shard_map/all_to_all | solution.py:262
  102.5 0.8 copy-start.4
  114.4 22.5 %all-to-all-start.5 = ((bf16[16,24,768]{2,1,0:T(8,128)(2,1)}), bf16[16,24,768]{2,1,0:T(8,128)(2,1)S(1)}, u32[]{:S(2)}, u32[]{:S(2)}) async-start(bf16[16,24,768]{2,1,0:T(8,128)(2,1)} %bitcast.24), calls=%async_computation.5 | async-start | bytes 1179648 | tf_op jit(solution)/shard_map/all_to_all | solution.py:262
  119.4 9.7 %collective-permute-start.4 = (bf16[48,896]{1,0:T(8,128)(2,1)S(1)}, bf16[48,896]{1,0:T(8,128)(2,1)S(1)}, u32[]{:S(2)}, u32[]{:S(2)}) collective-permute-start(bf16[48,896]{1,0:T(8,128)(2,1)S(1)} %get-tuple-element.38), channel_id=1, source_target_pairs={{0,192},{64,128},{128,64},{192,0},{1,193},{65,129},{129,65},{193,1... | collective-permute-start | bytes 258056 | tf_op jit(solution)/shard_map/ppermute | solution.py:266
  129.2 6.8 %collective-permute-start.5 = (bf16[24,896]{1,0:T(8,128)(2,1)S(1)}, bf16[24,896]{1,0:T(8,128)(2,1)S(1)}, u32[]{:S(2)}, u32[]{:S(2)}) collective-permute-start(bf16[24,896]{1,0:T(8,128)(2,1)S(1)} %get-tuple-element.41), channel_id=1, source_target_pairs={{0,64},{64,0},{128,192},{192,128},{1,65},{65,1},{129,193},{193,129... | collective-permute-start | bytes 129032 | tf_op jit(solution)/shard_map/ppermute | solution.py:266

commit v9 on v7

--- a/solution.py
+++ b/solution.py
@@ -8,11 +8,11 @@
 from jax.sharding import Mesh
 from jax.sharding import PartitionSpec as P
 
-ALL = ("z0", "y2", "y1", "y0", "x", "zh", "c")
-INNER = ("z0", "y2", "y1", "y0")
-CHIPS = ("x", "zh")
+ALL = ("z0", "y2", "y1", "y0", "x", "z2", "z1", "c")
+INNER = ("z2", "z1", "z0", "y0")
+CHIPS = ("x", "y2", "y1")
 NEAR = ("z0", "y0")
-FAR = ("y2", "y1")
+FAR = ("z2", "z1")
 CORE = "c"
 
 EPSILON = 1e-06
@@ -358,7 +358,7 @@
 
 
 def solution(mesh):
-    split = Mesh(mesh.devices.reshape(2, 2, 2, 2, 4, 4, 2), ALL)
+    split = Mesh(mesh.devices.reshape(2, 2, 2, 2, 4, 2, 2, 2), ALL)
     in_specs = (P(ALL, None), P(ALL, None), P())
     out_specs = (P(), P(ALL, None), P(ALL, None))
     return jax.shard_map(

time: 119 us -> 119 us (level)
  the two profiles are of different devices: /device:TPU:8 before, /device:TPU:64 now
where the time goes in v9:
time: 119 us; the launch traced here: 118 us
  starting transfers between devices  57.7 us (48%)
  waiting for transfers between devices  30.8 us (26%)
  blocking collectives  15.9 us (13%)
  Pallas kernels  11.1 us (9%)
  between operations  1.44 us (1%)
    all_to_all x5, starting transfers between devices, exchanged(): lax.all_to_all(split, axis, split_axis=0, concat_axis=0, tiled=True)  32 us
    ppermute x7, starting transfers between devices, swapped(): lax.ppermute(x, axis, [(k, k ^ offset) for k in range(lax.axis_size(axis))])  25.7 us
    ppermute x7, waiting for transfers between devices, swapped(): lax.ppermute(x, axis, [(k, k ^ offset) for k in range(lax.axis_size(axis))])  20.7 us
    all_to_all x1, blocking collectives, exchanged(): lax.all_to_all(split, axis, split_axis=0, concat_axis=0, tiled=True)  15.9 us
    pallas_call x15, Pallas kernels, kernel_call(): pl.pallas_call(body, out_shape=out_shape, in_specs=[spec(a) for a in args...  11.1 us
    all_to_all x5, waiting for transfers between devices, exchanged(): lax.all_to_all(split, axis, split_axis=0, concat_axis=0, tiled=True)  10.1 us
  transfers between devices with their start and end apart: 12, of which 11 were waited for; matrix products, arithmetic and copies ran while one was open for 0% of the time, Pallas kernels for 4%

profile of v9, /device:TPU:64, one launch (start us, length us, event | category | flops | bytes accessed | tf_op | source)
XLA Modules:
  0.0 117.9 jit_solution(15135187346913240842)
XLA Ops:
  0.6 0.0 copy-start
  0.6 0.9 copy-done
  1.5 0.0 copy-start.1
  1.5 0.0 copy-start.2
  1.5 1.0 shard_map.61
  2.5 9.7 %all-to-all-start = ((bf16[16,24,768]{2,1,0:T(8,128)(2,1)}), bf16[16,24,768]{2,1,0:T(8,128)(2,1)S(1)}, u32[]{:S(2)}, u32[]{:S(2)}) async-start(bf16[16,24,768]{2,1,0:T(8,128)(2,1)} %bitcast.2), calls=%async_computation | async-start | bytes 1179648 | tf_op jit(solution)/shard_map/all_to_all | solution.py:262
  12.1 0.0 copy-done.1
  12.2 0.0 copy-done.2
  12.2 0.2 shard_map.58
  12.4 6.1 %collective-permute-start = (bf16[24,768]{1,0:T(8,128)(2,1)S(1)}, bf16[24,768]{1,0:T(8,128)(2,1)S(1)}, u32[]{:S(2)}, u32[]{:S(2)}) collective-permute-start(bf16[24,768]{1,0:T(8,128)(2,1)S(1)} %get-tuple-element.25.mine_ref), channel_id=1, source_target_pairs={{0,2},{2,0},{4,6},{6,4},{1,3},{3,1},{5,7},{7,5},{8,10},{10,8},{12,... | collective-permute-start | bytes 110600 | tf_op jit(solution)/shard_map/ppermute | solution.py:266
  18.5 1.9 %collective-permute-done.theirs_ref = bf16[24,768]{1,0:T(8,128)(2,1)S(1)} collective-permute-done((bf16[24,768]{1,0:T(8,128)(2,1)S(1)}, bf16[24,768]{1,0:T(8,128)(2,1)S(1)}, u32[]{:S(2)}, u32[]{:S(2)}) %collective-permute-start) | collective-permute-done | bytes 36896 | tf_op jit(solution)/shard_map/ppermute | solution.py:266
  20.5 9.2 %collective-permute-start.1 = (bf16[48,768]{1,0:T(8,128)(2,1)S(1)}, bf16[48,768]{1,0:T(8,128)(2,1)S(1)}, u32[]{:S(2)}, u32[]{:S(2)}) collective-permute-start(bf16[48,768]{1,0:T(8,128)(2,1)S(1)} %shard_map.59.mine_ref), channel_id=1, source_target_pairs={{0,6},{2,4},{4,2},{6,0},{1,7},{3,5},{5,3},{7,1},{8,14},{10,12},{12... | collective-permute-start | bytes 221192 | tf_op jit(solution)/shard_map/ppermute | solution.py:266
  29.6 2.7 %collective-permute-done.1.theirs_ref = bf16[48,768]{1,0:T(8,128)(2,1)S(1)} collective-permute-done((bf16[48,768]{1,0:T(8,128)(2,1)S(1)}, bf16[48,768]{1,0:T(8,128)(2,1)S(1)}, u32[]{:S(2)}, u32[]{:S(2)}) %collective-permute-start.1) | collective-permute-done | bytes 73760 | tf_op jit(solution)/shard_map/ppermute | solution.py:266
  32.4 0.9 shard_map.60
  33.3 0.0 all-to-all-done
  33.3 3.5 %all-to-all-start.1 = ((bf16[4,96,768]{2,1,0:T(8,128)(2,1)}), bf16[4,96,768]{2,1,0:T(8,128)(2,1)S(1)}, u32[]{:S(2)}, u32[]{:S(2)}) async-start(bf16[4,96,768]{2,1,0:T(8,128)(2,1)} %bitcast.4), calls=%async_computation.1 | async-start | bytes 1179648 | tf_op jit(solution)/shard_map/all_to_all | solution.py:262
  36.7 1.9 %collective-permute-start.2 = (bf16[384,768]{1,0:T(8,128)(2,1)S(1)}, bf16[384,768]{1,0:T(8,128)(2,1)S(1)}, u32[]{:S(2)}, u32[]{:S(2)}) collective-permute-start(bf16[384,768]{1,0:T(8,128)(2,1)S(1)} %bitcast.10), channel_id=1, source_target_pairs={{0,1},{1,0},{2,3},{3,2},{4,5},{5,4},{6,7},{7,6},{8,9},{9,8},{10,11... | collective-permute-start | bytes 1769480 | tf_op jit(solution)/shard_map/ppermute | solution.py:266
  39.3 1.3 %collective-permute-done.2.other_ref = bf16[384,768]{1,0:T(8,128)(2,1)S(1)} collective-permute-done((bf16[384,768]{1,0:T(8,128)(2,1)S(1)}, bf16[384,768]{1,0:T(8,128)(2,1)S(1)}, u32[]{:S(2)}, u32[]{:S(2)}) %collective-permute-start.2) | collective-permute-done | bytes 589856 | tf_op jit(solution)/shard_map/ppermute | solution.py:266
  40.6 2.6 %all-to-all-done.1 = bf16[4,96,768]{2,1,0:T(8,128)(2,1)S(1)} async-done(((bf16[4,96,768]{2,1,0:T(8,128)(2,1)}), bf16[4,96,768]{2,1,0:T(8,128)(2,1)S(1)}, u32[]{:S(2)}, u32[]{:S(2)}) %all-to-all-start.1) | async-done | bytes 589856 | tf_op jit(solution)/shard_map/all_to_all | solution.py:262
  43.2 1.6 %shard_map.62 = f32[16,8,128]{2,1,0:T(8,128)} custom-call(f32[1]{0:T(128)S(6)} %copy.6.factor_ref, bf16[384,768]{1,0:T(8,128)(2,1)S(1)} %bitcast.14, bf16[384,768]{1,0:T(8,128)(2,1)S(1)} %bitcast.11, bf16[384,768]{1,0:T(8,128)(2,1)S(1)} %collective-permute-done.2.other_ref, f32[8,128]{1,0:T(8,128)S(1)} %get-tuple-element.27.diagonal_ref), custom_call_target="tpu_custom_call" | custom-call | flops 452984832 | bytes 1839108 | tf_op jit(solution)/shard_map/pallas_call | solution.py:41
  44.8 10.3 %all-to-all-start.2 = ((f32[16,8,128]{2,1,0:T(8,128)}), f32[16,8,128]{2,1,0:T(8,128)S(1)}, u32[]{:S(2)}, u32[]{:S(2)}) async-start(f32[16,8,128]{2,1,0:T(8,128)} %shard_map.62), calls=%async_computation.2 | async-start | bytes 131072 | tf_op jit(solution)/shard_map/all_to_all | solution.py:262
  55.2 0.9 shard_map.63.mine_ref
  56.1 1.9 %collective-permute-start.3 = (f32[8,128]{1,0:T(8,128)S(1)}, f32[8,128]{1,0:T(8,128)S(1)}, u32[]{:S(2)}, u32[]{:S(2)}) collective-permute-start(f32[8,128]{1,0:T(8,128)S(1)} %shard_map.63.mine_ref), channel_id=1, source_target_pairs={{0,1},{1,0},{2,3},{3,2},{4,5},{5,4},{6,7},{7,6},{8,9},{9,8},{10,11... | collective-permute-start | bytes 12296 | tf_op jit(solution)/shard_map/ppermute | solution.py:266
  58.0 1.1 collective-permute-done.3.theirs_ref
  59.1 3.4 %all-to-all-done.2.row_ref = f32[16,8,128]{2,1,0:T(8,128)S(1)} async-done(((f32[16,8,128]{2,1,0:T(8,128)}), f32[16,8,128]{2,1,0:T(8,128)S(1)}, u32[]{:S(2)}, u32[]{:S(2)}) %all-to-all-start.2) | async-done | bytes 65568 | tf_op jit(solution)/shard_map/all_to_all | solution.py:262
  62.6 0.2 shard_map.65
  62.8 15.9 %all_to_all.30.pieces_ref = f32[16,8,128]{2,1,0:T(8,128)S(1)} all-to-all(f32[16,8,128]{2,1,0:T(8,128)S(1)} %shard_map.65), channel_id=1, replica_groups=mesh['z0'=2,'y2'=2,'y1'=2,'y0'=2,'x'=4,'z2'=2,'z1'=2,'c'=2] {'x','y2','y1'}, dimensions={0} | all-to-all | bytes 131072 | tf_op jit(solution)/shard_map/all_to_all | solution.py:262
  78.7 2.5 %shard_map.66 = (bf16[384,896]{1,0:T(8,128)(2,1)}, bf16[384,384]{1,0:T(8,128)(2,1)S(1)}, bf16[384,384]{1,0:T(8,128)(2,1)S(1)}, f32[8,128]{1,0:T(8,128)S(1)}) custom-call(f32[1]{0:T(128)S(6)} %copy.6.factor_ref, bf16[384,768]{1,0:T(8,128)(2,1)S(1)} %bitcast.16, bf16[384,768]{1,0:T(8,128)(2,1)S(1)} %bitcast.13, ...), custom_call_target="tpu_custom_call" | custom-call | flops 905969664 | bytes 3182596 | tf_op jit(solution)/shard_map/pallas_call | solution.py:41
  81.2 4.9 %all-to-all-start.4 = ((bf16[4,96,896]{2,1,0:T(8,128)(2,1)}), bf16[4,96,896]{2,1,0:T(8,128)(2,1)S(1)}, u32[]{:S(2)}, u32[]{:S(2)}) async-start(bf16[4,96,896]{2,1,0:T(8,128)(2,1)} %bitcast.6), calls=%async_computation.4 | async-start | bytes 1376256 | tf_op jit(solution)/shard_map/all_to_all | solution.py:262
  86.1 0.8 shard_map.67
  86.9 1.9 %collective-permute-start.4 = (bf16[384,896]{1,0:T(8,128)(2,1)S(1)}, bf16[384,896]{1,0:T(8,128)(2,1)S(1)}, u32[]{:S(2)}, u32[]{:S(2)}) collective-permute-start(bf16[384,896]{1,0:T(8,128)(2,1)S(1)} %get-tuple-element.32), channel_id=1, source_target_pairs={{0,1},{1,0},{2,3},{3,2},{4,5},{5,4},{6,7},{7,6},{8,9},{9,8},{10,11... | collective-permute-start | bytes 2064392 | tf_op jit(solution)/shard_map/ppermute | solution.py:266
  88.8 2.1 %collective-permute-done.4.theirs_ref = bf16[384,896]{1,0:T(8,128)(2,1)S(1)} collective-permute-done((bf16[384,896]{1,0:T(8,128)(2,1)S(1)}, bf16[384,896]{1,0:T(8,128)(2,1)S(1)}, u32[]{:S(2)}, u32[]{:S(2)}) %collective-permute-start.4) | collective-permute-done | bytes 688160 | tf_op jit(solution)/shard_map/ppermute | solution.py:266
  91.0 1.0 shard_map.68
  92.0 1.0 all-to-all-done.4
  93.1 3.6 %all-to-all-start.5 = ((bf16[16,24,768]{2,1,0:T(8,128)(2,1)}), bf16[16,24,768]{2,1,0:T(8,128)(2,1)S(1)}, u32[]{:S(2)}, u32[]{:S(2)}) async-start(bf16[16,24,768]{2,1,0:T(8,128)(2,1)} %bitcast.8), calls=%async_computation.5 | async-start | bytes 1179648 | tf_op jit(solution)/shard_map/all_to_all | solution.py:262
  96.6 0.2 shard_map.69
  96.8 2.8 %collective-permute-start.5 = (bf16[48,896]{1,0:T(8,128)(2,1)S(1)}, bf16[48,896]{1,0:T(8,128)(2,1)S(1)}, u32[]{:S(2)}, u32[]{:S(2)}) collective-permute-start(bf16[48,896]{1,0:T(8,128)(2,1)S(1)} %get-tuple-element.38), channel_id=1, source_target_pairs={{0,6},{2,4},{4,2},{6,0},{1,7},{3,5},{5,3},{7,1},{8,14},{10,12},{12... | collective-permute-start | bytes 258056 | tf_op jit(solution)/shard_map/ppermute | solution.py:266
  99.6 6.6 %collective-permute-done.5.theirs_ref = bf16[48,896]{1,0:T(8,128)(2,1)S(1)} collective-permute-done((bf16[48,896]{1,0:T(8,128)(2,1)S(1)}, bf16[48,896]{1,0:T(8,128)(2,1)S(1)}, u32[]{:S(2)}, u32[]{:S(2)}) %collective-permute-start.5) | collective-permute-done | bytes 86048 | tf_op jit(solution)/shard_map/ppermute | solution.py:266
  106.2 0.1 shard_map.70
  106.4 1.9 %collective-permute-start.6 = (bf16[24,896]{1,0:T(8,128)(2,1)S(1)}, bf16[24,896]{1,0:T(8,128)(2,1)S(1)}, u32[]{:S(2)}, u32[]{:S(2)}) collective-permute-start(bf16[24,896]{1,0:T(8,128)(2,1)S(1)} %get-tuple-element.41), channel_id=1, source_target_pairs={{0,2},{2,0},{4,6},{6,4},{1,3},{3,1},{5,7},{7,5},{8,10},{10,8},{12,... | collective-permute-start | bytes 129032 | tf_op jit(solution)/shard_map/ppermute | solution.py:266
  108.3 4.9 %collective-permute-done.6.theirs_ref = bf16[24,896]{1,0:T(8,128)(2,1)S(1)} collective-permute-done((bf16[24,896]{1,0:T(8,128)(2,1)S(1)}, bf16[24,896]{1,0:T(8,128)(2,1)S(1)}, u32[]{:S(2)}, u32[]{:S(2)}) %collective-permute-start.6) | collective-permute-done | bytes 43040 | tf_op jit(solution)/shard_map/ppermute | solution.py:266
  113.2 0.8 shard_map.71
  114.0 3.1 %all-to-all-done.5 = bf16[16,24,768]{2,1,0:T(8,128)(2,1)S(1)} async-done(((bf16[16,24,768]{2,1,0:T(8,128)(2,1)}), bf16[16,24,768]{2,1,0:T(8,128)(2,1)S(1)}, u32[]{:S(2)}, u32[]{:S(2)}) %all-to-all-start.5) | async-done | bytes 589856 | tf_op jit(solution)/shard_map/all_to_all | solution.py:262
  117.1 0.8 shard_map.72
  (2 shorter events, 0.0 us)
Async XLA Ops:
  0.6 0.9 copy-start
  1.5 10.6 %copy-start.1 = (f32[24,768]{1,0:T(8,128)S(1)}, f32[24,768]{1,0:T(8,128)}, u32[]{:S(2)}) copy-start(f32[24,768]{1,0:T(8,128)} %values_ref.7) | copy-start | bytes 221188
  1.5 10.6 %copy-start.2 = (f32[24,768]{1,0:T(8,128)S(1)}, f32[24,768]{1,0:T(8,128)}, u32[]{:S(2)}) copy-start(f32[24,768]{1,0:T(8,128)} %paired_ref.3) | copy-start | bytes 221188
  2.5 30.8 %all-to-all-start = ((bf16[16,24,768]{2,1,0:T(8,128)(2,1)}), bf16[16,24,768]{2,1,0:T(8,128)(2,1)S(1)}, u32[]{:S(2)}, u32[]{:S(2)}) async-start(bf16[16,24,768]{2,1,0:T(8,128)(2,1)} %bitcast.2), calls=%async_computation | async-start | bytes 1179648 | tf_op jit(solution)/shard_map/all_to_all | solution.py:262
  12.4 8.0 %collective-permute-start = (bf16[24,768]{1,0:T(8,128)(2,1)S(1)}, bf16[24,768]{1,0:T(8,128)(2,1)S(1)}, u32[]{:S(2)}, u32[]{:S(2)}) collective-permute-start(bf16[24,768]{1,0:T(8,128)(2,1)S(1)} %get-tuple-element.25.mine_ref), channel_id=1, source_target_pairs={{0,2},{2,0},{4,6},{6,4},{1,3},{3,1},{5,7},{7,5},{8,10},{10,8},{12,... | collective-permute-start | bytes 110600 | tf_op jit(solution)/shard_map/ppermute | solution.py:266
  20.5 11.9 %collective-permute-start.1 = (bf16[48,768]{1,0:T(8,128)(2,1)S(1)}, bf16[48,768]{1,0:T(8,128)(2,1)S(1)}, u32[]{:S(2)}, u32[]{:S(2)}) collective-permute-start(bf16[48,768]{1,0:T(8,128)(2,1)S(1)} %shard_map.59.mine_ref), channel_id=1, source_target_pairs={{0,6},{2,4},{4,2},{6,0},{1,7},{3,5},{5,3},{7,1},{8,14},{10,12},{12... | collective-permute-start | bytes 221192 | tf_op jit(solution)/shard_map/ppermute | solution.py:266
  33.3 10.0 %all-to-all-start.1 = ((bf16[4,96,768]{2,1,0:T(8,128)(2,1)}), bf16[4,96,768]{2,1,0:T(8,128)(2,1)S(1)}, u32[]{:S(2)}, u32[]{:S(2)}) async-start(bf16[4,96,768]{2,1,0:T(8,128)(2,1)} %bitcast.4), calls=%async_computation.1 | async-start | bytes 1179648 | tf_op jit(solution)/shard_map/all_to_all | solution.py:262
  36.7 3.9 %collective-permute-start.2 = (bf16[384,768]{1,0:T(8,128)(2,1)S(1)}, bf16[384,768]{1,0:T(8,128)(2,1)S(1)}, u32[]{:S(2)}, u32[]{:S(2)}) collective-permute-start(bf16[384,768]{1,0:T(8,128)(2,1)S(1)} %bitcast.10), channel_id=1, source_target_pairs={{0,1},{1,0},{2,3},{3,2},{4,5},{5,4},{6,7},{7,6},{8,9},{9,8},{10,11... | collective-permute-start | bytes 1769480 | tf_op jit(solution)/shard_map/ppermute | solution.py:266
  44.8 17.7 %all-to-all-start.2 = ((f32[16,8,128]{2,1,0:T(8,128)}), f32[16,8,128]{2,1,0:T(8,128)S(1)}, u32[]{:S(2)}, u32[]{:S(2)}) async-start(f32[16,8,128]{2,1,0:T(8,128)} %shard_map.62), calls=%async_computation.2 | async-start | bytes 131072 | tf_op jit(solution)/shard_map/all_to_all | solution.py:262
  56.1 3.1 %collective-permute-start.3 = (f32[8,128]{1,0:T(8,128)S(1)}, f32[8,128]{1,0:T(8,128)S(1)}, u32[]{:S(2)}, u32[]{:S(2)}) collective-permute-start(f32[8,128]{1,0:T(8,128)S(1)} %shard_map.63.mine_ref), channel_id=1, source_target_pairs={{0,1},{1,0},{2,3},{3,2},{4,5},{5,4},{6,7},{7,6},{8,9},{9,8},{10,11... | collective-permute-start | bytes 12296 | tf_op jit(solution)/shard_map/ppermute | solution.py:266
  81.2 11.9 %all-to-all-start.4 = ((bf16[4,96,896]{2,1,0:T(8,128)(2,1)}), bf16[4,96,896]{2,1,0:T(8,128)(2,1)S(1)}, u32[]{:S(2)}, u32[]{:S(2)}) async-start(bf16[4,96,896]{2,1,0:T(8,128)(2,1)} %bitcast.6), calls=%async_computation.4 | async-start | bytes 1376256 | tf_op jit(solution)/shard_map/all_to_all | solution.py:262
  86.9 4.0 %collective-permute-start.4 = (bf16[384,896]{1,0:T(8,128)(2,1)S(1)}, bf16[384,896]{1,0:T(8,128)(2,1)S(1)}, u32[]{:S(2)}, u32[]{:S(2)}) collective-permute-start(bf16[384,896]{1,0:T(8,128)(2,1)S(1)} %get-tuple-element.32), channel_id=1, source_target_pairs={{0,1},{1,0},{2,3},{3,2},{4,5},{5,4},{6,7},{7,6},{8,9},{9,8},{10,11... | collective-permute-start | bytes 2064392 | tf_op jit(solution)/shard_map/ppermute | solution.py:266
  93.1 24.0 %all-to-all-start.5 = ((bf16[16,24,768]{2,1,0:T(8,128)(2,1)}), bf16[16,24,768]{2,1,0:T(8,128)(2,1)S(1)}, u32[]{:S(2)}, u32[]{:S(2)}) async-start(bf16[16,24,768]{2,1,0:T(8,128)(2,1)} %bitcast.8), calls=%async_computation.5 | async-start | bytes 1179648 | tf_op jit(solution)/shard_map/all_to_all | solution.py:262
  96.8 9.4 %collective-permute-start.5 = (bf16[48,896]{1,0:T(8,128)(2,1)S(1)}, bf16[48,896]{1,0:T(8,128)(2,1)S(1)}, u32[]{:S(2)}, u32[]{:S(2)}) collective-permute-start(bf16[48,896]{1,0:T(8,128)(2,1)S(1)} %get-tuple-element.38), channel_id=1, source_target_pairs={{0,6},{2,4},{4,2},{6,0},{1,7},{3,5},{5,3},{7,1},{8,14},{10,12},{12... | collective-permute-start | bytes 258056 | tf_op jit(solution)/shard_map/ppermute | solution.py:266
  106.4 6.8 %collective-permute-start.6 = (bf16[24,896]{1,0:T(8,128)(2,1)S(1)}, bf16[24,896]{1,0:T(8,128)(2,1)S(1)}, u32[]{:S(2)}, u32[]{:S(2)}) collective-permute-start(bf16[24,896]{1,0:T(8,128)(2,1)S(1)} %get-tuple-element.41), channel_id=1, source_target_pairs={{0,2},{2,0},{4,6},{6,4},{1,3},{3,1},{5,7},{7,5},{8,10},{10,8},{12,... | collective-permute-start | bytes 129032 | tf_op jit(solution)/shard_map/ppermute | solution.py:266

commit v10 on v9

--- a/solution.py
+++ b/solution.py
@@ -102,10 +102,9 @@
     return jnp.concatenate([*rows, *[zero] * (8 - len(rows))], axis=0)
 
 
-def lse_of(parts):
-    peak = functools.reduce(jnp.maximum, [jnp.max(p, axis=0, keepdims=True) for p in parts])
-    total = sum(jnp.sum(jnp.exp2(p - peak), axis=0, keepdims=True) for p in parts)
-    return peak + jnp.log2(total)
+def lse_of(logits):
+    peak = jnp.max(logits, axis=0, keepdims=True)
+    return peak + jnp.log2(jnp.sum(jnp.exp2(logits - peak), axis=0, keepdims=True))
 
 
 def pieces_lse(pieces):
@@ -121,8 +120,10 @@
 def rows_kernel(factor_ref, image_ref, own_ref, other_ref, diagonal_ref, message_ref):
     factor = factor_ref[0] * LOG2_E
     image = image_ref[...]
-    lse = lse_of([factor * f32_dot(text[...], image, LAST) for text in (own_ref, other_ref)])
-    message = eight([*lines(lse), factor * diagonal_ref[0:1, :]])
+    own, other = (
+        lse_of(factor * f32_dot(text[...], image, LAST)) for text in (own_ref, other_ref)
+    )
+    message = eight([*lines(pair_lse(own, other)), factor * diagonal_ref[0:1, :]])
     message_ref[...] = jnp.broadcast_to(message[None], message_ref.shape)
 
 
@@ -130,7 +131,7 @@
     factor = factor_ref[0] * LOG2_E
     image = image_ref[...]
     own, other = (
-        lse_of([factor * f32_dot(image, text[...], LAST)]) for text in (own_ref, other_ref)
+        lse_of(factor * f32_dot(image, text[...], LAST)) for text in (own_ref, other_ref)
     )
     message_ref[...] = eight([*lines(own), *lines(other)])
 
@@ -182,12 +183,15 @@
     image_out[:, width:] = packed(col_share, image_out.shape[0])
 
 
-def text_sums_kernel(image_ref, own_ref, other_ref, share_ref, own_out, other_out):
+def other_sums_kernel(image_ref, weights_ref, share_ref, sums_ref):
     image = image_ref[...]
     width = image.shape[1]
-    other_out[:, :width] = f32_dot(other_ref[...], image, FIRST).astype(jnp.bfloat16)
-    other_out[:, width:] = packed(jnp.max(share_ref[...]), other_out.shape[0])
-    own_out[...] = f32_dot(own_ref[...], image, FIRST)
+    sums_ref[:, :width] = f32_dot(weights_ref[...], image, FIRST).astype(jnp.bfloat16)
+    sums_ref[:, width:] = packed(jnp.max(share_ref[...]), sums_ref.shape[0])
+
+
+def own_sums_kernel(image_ref, weights_ref, sums_ref):
+    sums_ref[...] = f32_dot(weights_ref[...], image_ref[...], FIRST)
 
 
 def pair_sums_kernel(own_ref, theirs_ref, shared_ref, sums_ref, share_ref):
@@ -315,17 +319,19 @@
     col_pieces = exchanged(col_message, CHIPS)
 
     half_tile = shape((image_rows, text_rows), bf16)
-    image_part, *weights, row_share = kernel_call(
+    image_part, own_weights, other_weights, row_share = kernel_call(
         weights_kernel,
         (shape((image_rows, wide), bf16), half_tile, half_tile, tile),
         *tile_of, row_pieces, col_pieces,
         flops=4 * work,
     )
-    own_part, other_part = kernel_call(
-        text_sums_kernel,
-        (shape((text_rows, width), f32), shape((text_rows, wide), bf16)),
-        image_group, *weights, row_share,
-        flops=2 * work,
+    other_part = kernel_call(
+        other_sums_kernel, shape((text_rows, wide), bf16),
+        image_group, other_weights, row_share,
+        flops=work,
+    )
+    own_part = kernel_call(
+        own_sums_kernel, shape((text_rows, width), f32), image_group, own_weights, flops=work
     )
     image_pieces = exchanged(image_part, NEAR)
     text_part, row_share = kernel_call(

time: 119 us -> 118 us (level)
  the two profiles are of different devices: /device:TPU:64 before, /device:TPU:8 now
where the time goes in v10:
time: 118 us; the launch traced here: 117 us
  starting transfers between devices  59.6 us (51%)
  waiting for transfers between devices  27.8 us (24%)
  blocking collectives  15.9 us (13%)
  Pallas kernels  11.2 us (9%)
  between operations  1.44 us (1%)
    all_to_all x5, starting transfers between devices, exchanged(): lax.all_to_all(split, axis, split_axis=0, concat_axis=0, tiled=True)  31.9 us
    ppermute x7, starting transfers between devices, swapped(): lax.ppermute(x, axis, [(k, k ^ offset) for k in range(lax.axis_size(axis))])  27.7 us
    ppermute x7, waiting for transfers between devices, swapped(): lax.ppermute(x, axis, [(k, k ^ offset) for k in range(lax.axis_size(axis))])  18 us
    all_to_all x1, blocking collectives, exchanged(): lax.all_to_all(split, axis, split_axis=0, concat_axis=0, tiled=True)  15.9 us
    pallas_call x16, Pallas kernels, kernel_call(): pl.pallas_call(body, out_shape=out_shape, in_specs=[spec(a) for a in args...  11.2 us
    all_to_all x5, waiting for transfers between devices, exchanged(): lax.all_to_all(split, axis, split_axis=0, concat_axis=0, tiled=True)  9.79 us
  transfers between devices with their start and end apart: 12, of which 11 were waited for; matrix products, arithmetic and copies ran while one was open for 0% of the time, Pallas kernels for 4%

profile of v10, /device:TPU:8, one launch (start us, length us, event | category | flops | bytes accessed | tf_op | source)
XLA Modules:
  0.0 116.9 jit_solution(1514418011638494331)
XLA Ops:
  0.6 0.0 copy-start
  0.6 0.9 copy-done
  1.5 0.0 copy-start.1
  1.5 0.0 copy-start.2
  1.5 1.0 shard_map.61
  2.5 8.8 %all-to-all-start = ((bf16[16,24,768]{2,1,0:T(8,128)(2,1)}), bf16[16,24,768]{2,1,0:T(8,128)(2,1)S(1)}, u32[]{:S(2)}, u32[]{:S(2)}) async-start(bf16[16,24,768]{2,1,0:T(8,128)(2,1)} %bitcast.2), calls=%async_computation | async-start | bytes 1179648 | tf_op jit(solution)/shard_map/all_to_all | solution.py:266
  11.2 0.0 copy-done.1
  11.3 0.0 copy-done.2
  11.3 0.2 shard_map.58
  11.5 6.1 %collective-permute-start = (bf16[24,768]{1,0:T(8,128)(2,1)S(1)}, bf16[24,768]{1,0:T(8,128)(2,1)S(1)}, u32[]{:S(2)}, u32[]{:S(2)}) collective-permute-start(bf16[24,768]{1,0:T(8,128)(2,1)S(1)} %get-tuple-element.23.mine_ref), channel_id=1, source_target_pairs={{0,2},{2,0},{4,6},{6,4},{1,3},{3,1},{5,7},{7,5},{8,10},{10,8},{12,... | collective-permute-start | bytes 110600 | tf_op jit(solution)/shard_map/ppermute | solution.py:270
  17.6 1.9 %collective-permute-done.theirs_ref = bf16[24,768]{1,0:T(8,128)(2,1)S(1)} collective-permute-done((bf16[24,768]{1,0:T(8,128)(2,1)S(1)}, bf16[24,768]{1,0:T(8,128)(2,1)S(1)}, u32[]{:S(2)}, u32[]{:S(2)}) %collective-permute-start) | collective-permute-done | bytes 36896 | tf_op jit(solution)/shard_map/ppermute | solution.py:270
  19.5 9.7 %collective-permute-start.1 = (bf16[48,768]{1,0:T(8,128)(2,1)S(1)}, bf16[48,768]{1,0:T(8,128)(2,1)S(1)}, u32[]{:S(2)}, u32[]{:S(2)}) collective-permute-start(bf16[48,768]{1,0:T(8,128)(2,1)S(1)} %shard_map.59.mine_ref), channel_id=1, source_target_pairs={{0,6},{2,4},{4,2},{6,0},{1,7},{3,5},{5,3},{7,1},{8,14},{10,12},{12... | collective-permute-start | bytes 221192 | tf_op jit(solution)/shard_map/ppermute | solution.py:270
  29.3 2.4 %collective-permute-done.1.theirs_ref = bf16[48,768]{1,0:T(8,128)(2,1)S(1)} collective-permute-done((bf16[48,768]{1,0:T(8,128)(2,1)S(1)}, bf16[48,768]{1,0:T(8,128)(2,1)S(1)}, u32[]{:S(2)}, u32[]{:S(2)}) %collective-permute-start.1) | collective-permute-done | bytes 73760 | tf_op jit(solution)/shard_map/ppermute | solution.py:270
  31.6 0.9 shard_map.60
  32.5 0.0 all-to-all-done
  32.5 4.9 %all-to-all-start.1 = ((bf16[4,96,768]{2,1,0:T(8,128)(2,1)}), bf16[4,96,768]{2,1,0:T(8,128)(2,1)S(1)}, u32[]{:S(2)}, u32[]{:S(2)}) async-start(bf16[4,96,768]{2,1,0:T(8,128)(2,1)} %bitcast.4), calls=%async_computation.1 | async-start | bytes 1179648 | tf_op jit(solution)/shard_map/all_to_all | solution.py:266
  37.5 1.9 %collective-permute-start.2 = (bf16[384,768]{1,0:T(8,128)(2,1)S(1)}, bf16[384,768]{1,0:T(8,128)(2,1)S(1)}, u32[]{:S(2)}, u32[]{:S(2)}) collective-permute-start(bf16[384,768]{1,0:T(8,128)(2,1)S(1)} %bitcast.15), channel_id=1, source_target_pairs={{0,1},{1,0},{2,3},{3,2},{4,5},{5,4},{6,7},{7,6},{8,9},{9,8},{10,11... | collective-permute-start | bytes 1769480 | tf_op jit(solution)/shard_map/ppermute | solution.py:270
  40.0 1.3 %collective-permute-done.2.other_ref = bf16[384,768]{1,0:T(8,128)(2,1)S(1)} collective-permute-done((bf16[384,768]{1,0:T(8,128)(2,1)S(1)}, bf16[384,768]{1,0:T(8,128)(2,1)S(1)}, u32[]{:S(2)}, u32[]{:S(2)}) %collective-permute-start.2) | collective-permute-done | bytes 589856 | tf_op jit(solution)/shard_map/ppermute | solution.py:270
  41.4 3.1 %all-to-all-done.1 = bf16[4,96,768]{2,1,0:T(8,128)(2,1)S(1)} async-done(((bf16[4,96,768]{2,1,0:T(8,128)(2,1)}), bf16[4,96,768]{2,1,0:T(8,128)(2,1)S(1)}, u32[]{:S(2)}, u32[]{:S(2)}) %all-to-all-start.1) | async-done | bytes 589856 | tf_op jit(solution)/shard_map/all_to_all | solution.py:266
  44.4 1.6 %shard_map.62 = f32[16,8,128]{2,1,0:T(8,128)} custom-call(f32[1]{0:T(128)S(6)} %copy.6.factor_ref, bf16[384,768]{1,0:T(8,128)(2,1)S(1)} %bitcast.10, bf16[384,768]{1,0:T(8,128)(2,1)S(1)} %bitcast.16, bf16[384,768]{1,0:T(8,128)(2,1)S(1)} %collective-permute-done.2.other_ref, f32[8,128]{1,0:T(8,128)S(1)} %get-tuple-element.25.diagonal_ref), custom_call_target="tpu_custom_call" | custom-call | flops 452984832 | bytes 1839108 | tf_op jit(solution)/shard_map/pallas_call | solution.py:41
  46.0 9.9 %all-to-all-start.2 = ((f32[16,8,128]{2,1,0:T(8,128)}), f32[16,8,128]{2,1,0:T(8,128)S(1)}, u32[]{:S(2)}, u32[]{:S(2)}) async-start(f32[16,8,128]{2,1,0:T(8,128)} %shard_map.62), calls=%async_computation.2 | async-start | bytes 131072 | tf_op jit(solution)/shard_map/all_to_all | solution.py:266
  55.9 0.9 shard_map.63.mine_ref
  56.8 1.9 %collective-permute-start.3 = (f32[8,128]{1,0:T(8,128)S(1)}, f32[8,128]{1,0:T(8,128)S(1)}, u32[]{:S(2)}, u32[]{:S(2)}) collective-permute-start(f32[8,128]{1,0:T(8,128)S(1)} %shard_map.63.mine_ref), channel_id=1, source_target_pairs={{0,1},{1,0},{2,3},{3,2},{4,5},{5,4},{6,7},{7,6},{8,9},{9,8},{10,11... | collective-permute-start | bytes 12296 | tf_op jit(solution)/shard_map/ppermute | solution.py:270
  58.7 1.1 collective-permute-done.3.theirs_ref
  59.9 3.6 %all-to-all-done.2.row_ref = f32[16,8,128]{2,1,0:T(8,128)S(1)} async-done(((f32[16,8,128]{2,1,0:T(8,128)}), f32[16,8,128]{2,1,0:T(8,128)S(1)}, u32[]{:S(2)}, u32[]{:S(2)}) %all-to-all-start.2) | async-done | bytes 65568 | tf_op jit(solution)/shard_map/all_to_all | solution.py:266
  63.5 0.2 shard_map.65
  63.7 15.9 %all_to_all.30.pieces_ref = f32[16,8,128]{2,1,0:T(8,128)S(1)} all-to-all(f32[16,8,128]{2,1,0:T(8,128)S(1)} %shard_map.65), channel_id=1, replica_groups=mesh['z0'=2,'y2'=2,'y1'=2,'y0'=2,'x'=4,'z2'=2,'z1'=2,'c'=2] {'x','y2','y1'}, dimensions={0} | all-to-all | bytes 131072 | tf_op jit(solution)/shard_map/all_to_all | solution.py:266
  79.6 2.5 %shard_map.66 = (bf16[384,896]{1,0:T(8,128)(2,1)}, bf16[384,384]{1,0:T(8,128)(2,1)S(1)}, bf16[384,384]{1,0:T(8,128)(2,1)S(1)}, f32[8,128]{1,0:T(8,128)S(1)}) custom-call(f32[1]{0:T(128)S(6)} %copy.6.factor_ref, bf16[384,768]{1,0:T(8,128)(2,1)S(1)} %bitcast.12, bf16[384,768]{1,0:T(8,128)(2,1)S(1)} %bitcast.18, ...), custom_call_target="tpu_custom_call" | custom-call | flops 905969664 | bytes 3182596 | tf_op jit(solution)/shard_map/pallas_call | solution.py:41
  82.1 4.7 %all-to-all-start.4 = ((bf16[4,96,896]{2,1,0:T(8,128)(2,1)}), bf16[4,96,896]{2,1,0:T(8,128)(2,1)S(1)}, u32[]{:S(2)}, u32[]{:S(2)}) async-start(bf16[4,96,896]{2,1,0:T(8,128)(2,1)} %bitcast.6), calls=%async_computation.4 | async-start | bytes 1376256 | tf_op jit(solution)/shard_map/all_to_all | solution.py:266
  86.8 0.5 shard_map.68
  87.4 1.9 %collective-permute-start.4 = (bf16[384,896]{1,0:T(8,128)(2,1)S(1)}, bf16[384,896]{1,0:T(8,128)(2,1)S(1)}, u32[]{:S(2)}, u32[]{:S(2)}) collective-permute-start(bf16[384,896]{1,0:T(8,128)(2,1)S(1)} %shard_map.68), channel_id=1, source_target_pairs={{0,1},{1,0},{2,3},{3,2},{4,5},{5,4},{6,7},{7,6},{8,9},{9,8},{10,11... | collective-permute-start | bytes 2064392 | tf_op jit(solution)/shard_map/ppermute | solution.py:270
  89.3 0.5 shard_map.67.own_ref
  89.8 1.6 %collective-permute-done.4.theirs_ref = bf16[384,896]{1,0:T(8,128)(2,1)S(1)} collective-permute-done((bf16[384,896]{1,0:T(8,128)(2,1)S(1)}, bf16[384,896]{1,0:T(8,128)(2,1)S(1)}, u32[]{:S(2)}, u32[]{:S(2)}) %collective-permute-start.4) | collective-permute-done | bytes 688160 | tf_op jit(solution)/shard_map/ppermute | solution.py:270
  91.4 1.0 shard_map.69
  92.4 1.3 %all-to-all-done.4 = bf16[4,96,896]{2,1,0:T(8,128)(2,1)S(1)} async-done(((bf16[4,96,896]{2,1,0:T(8,128)(2,1)}), bf16[4,96,896]{2,1,0:T(8,128)(2,1)S(1)}, u32[]{:S(2)}, u32[]{:S(2)}) %all-to-all-start.4) | async-done | bytes 688160 | tf_op jit(solution)/shard_map/all_to_all | solution.py:266
  93.8 3.6 %all-to-all-start.5 = ((bf16[16,24,768]{2,1,0:T(8,128)(2,1)}), bf16[16,24,768]{2,1,0:T(8,128)(2,1)S(1)}, u32[]{:S(2)}, u32[]{:S(2)}) async-start(bf16[16,24,768]{2,1,0:T(8,128)(2,1)} %bitcast.8), calls=%async_computation.5 | async-start | bytes 1179648 | tf_op jit(solution)/shard_map/all_to_all | solution.py:266
  97.3 0.2 shard_map.70
  97.5 2.8 %collective-permute-start.5 = (bf16[48,896]{1,0:T(8,128)(2,1)S(1)}, bf16[48,896]{1,0:T(8,128)(2,1)S(1)}, u32[]{:S(2)}, u32[]{:S(2)}) collective-permute-start(bf16[48,896]{1,0:T(8,128)(2,1)S(1)} %get-tuple-element.34), channel_id=1, source_target_pairs={{0,6},{2,4},{4,2},{6,0},{1,7},{3,5},{5,3},{7,1},{8,14},{10,12},{12... | collective-permute-start | bytes 258056 | tf_op jit(solution)/shard_map/ppermute | solution.py:270
  100.3 5.8 %collective-permute-done.5.theirs_ref = bf16[48,896]{1,0:T(8,128)(2,1)S(1)} collective-permute-done((bf16[48,896]{1,0:T(8,128)(2,1)S(1)}, bf16[48,896]{1,0:T(8,128)(2,1)S(1)}, u32[]{:S(2)}, u32[]{:S(2)}) %collective-permute-start.5) | collective-permute-done | bytes 86048 | tf_op jit(solution)/shard_map/ppermute | solution.py:270
  106.1 0.1 shard_map.71
  106.2 3.4 %collective-permute-start.6 = (bf16[24,896]{1,0:T(8,128)(2,1)S(1)}, bf16[24,896]{1,0:T(8,128)(2,1)S(1)}, u32[]{:S(2)}, u32[]{:S(2)}) collective-permute-start(bf16[24,896]{1,0:T(8,128)(2,1)S(1)} %get-tuple-element.37), channel_id=1, source_target_pairs={{0,2},{2,0},{4,6},{6,4},{1,3},{3,1},{5,7},{7,5},{8,10},{10,8},{12,... | collective-permute-start | bytes 129032 | tf_op jit(solution)/shard_map/ppermute | solution.py:270
  109.6 3.9 %collective-permute-done.6.theirs_ref = bf16[24,896]{1,0:T(8,128)(2,1)S(1)} collective-permute-done((bf16[24,896]{1,0:T(8,128)(2,1)S(1)}, bf16[24,896]{1,0:T(8,128)(2,1)S(1)}, u32[]{:S(2)}, u32[]{:S(2)}) %collective-permute-start.6) | collective-permute-done | bytes 43040 | tf_op jit(solution)/shard_map/ppermute | solution.py:270
  113.5 0.8 shard_map.72
  114.3 1.8 %all-to-all-done.5 = bf16[16,24,768]{2,1,0:T(8,128)(2,1)S(1)} async-done(((bf16[16,24,768]{2,1,0:T(8,128)(2,1)}), bf16[16,24,768]{2,1,0:T(8,128)(2,1)S(1)}, u32[]{:S(2)}, u32[]{:S(2)}) %all-to-all-start.5) | async-done | bytes 589856 | tf_op jit(solution)/shard_map/all_to_all | solution.py:266
  116.1 0.8 shard_map.73
  (2 shorter events, 0.0 us)
Async XLA Ops:
  0.6 0.9 copy-start
  1.5 9.7 %copy-start.1 = (f32[24,768]{1,0:T(8,128)S(1)}, f32[24,768]{1,0:T(8,128)}, u32[]{:S(2)}) copy-start(f32[24,768]{1,0:T(8,128)} %values_ref.7) | copy-start | bytes 221188
  1.5 9.7 %copy-start.2 = (f32[24,768]{1,0:T(8,128)S(1)}, f32[24,768]{1,0:T(8,128)}, u32[]{:S(2)}) copy-start(f32[24,768]{1,0:T(8,128)} %paired_ref.3) | copy-start | bytes 221188
  2.5 30.1 %all-to-all-start = ((bf16[16,24,768]{2,1,0:T(8,128)(2,1)}), bf16[16,24,768]{2,1,0:T(8,128)(2,1)S(1)}, u32[]{:S(2)}, u32[]{:S(2)}) async-start(bf16[16,24,768]{2,1,0:T(8,128)(2,1)} %bitcast.2), calls=%async_computation | async-start | bytes 1179648 | tf_op jit(solution)/shard_map/all_to_all | solution.py:266
  11.5 8.0 %collective-permute-start = (bf16[24,768]{1,0:T(8,128)(2,1)S(1)}, bf16[24,768]{1,0:T(8,128)(2,1)S(1)}, u32[]{:S(2)}, u32[]{:S(2)}) collective-permute-start(bf16[24,768]{1,0:T(8,128)(2,1)S(1)} %get-tuple-element.23.mine_ref), channel_id=1, source_target_pairs={{0,2},{2,0},{4,6},{6,4},{1,3},{3,1},{5,7},{7,5},{8,10},{10,8},{12,... | collective-permute-start | bytes 110600 | tf_op jit(solution)/shard_map/ppermute | solution.py:270
  19.5 12.1 %collective-permute-start.1 = (bf16[48,768]{1,0:T(8,128)(2,1)S(1)}, bf16[48,768]{1,0:T(8,128)(2,1)S(1)}, u32[]{:S(2)}, u32[]{:S(2)}) collective-permute-start(bf16[48,768]{1,0:T(8,128)(2,1)S(1)} %shard_map.59.mine_ref), channel_id=1, source_target_pairs={{0,6},{2,4},{4,2},{6,0},{1,7},{3,5},{5,3},{7,1},{8,14},{10,12},{12... | collective-permute-start | bytes 221192 | tf_op jit(solution)/shard_map/ppermute | solution.py:270
  32.5 11.9 %all-to-all-start.1 = ((bf16[4,96,768]{2,1,0:T(8,128)(2,1)}), bf16[4,96,768]{2,1,0:T(8,128)(2,1)S(1)}, u32[]{:S(2)}, u32[]{:S(2)}) async-start(bf16[4,96,768]{2,1,0:T(8,128)(2,1)} %bitcast.4), calls=%async_computation.1 | async-start | bytes 1179648 | tf_op jit(solution)/shard_map/all_to_all | solution.py:266
  37.5 3.9 %collective-permute-start.2 = (bf16[384,768]{1,0:T(8,128)(2,1)S(1)}, bf16[384,768]{1,0:T(8,128)(2,1)S(1)}, u32[]{:S(2)}, u32[]{:S(2)}) collective-permute-start(bf16[384,768]{1,0:T(8,128)(2,1)S(1)} %bitcast.15), channel_id=1, source_target_pairs={{0,1},{1,0},{2,3},{3,2},{4,5},{5,4},{6,7},{7,6},{8,9},{9,8},{10,11... | collective-permute-start | bytes 1769480 | tf_op jit(solution)/shard_map/ppermute | solution.py:270
  46.0 17.5 %all-to-all-start.2 = ((f32[16,8,128]{2,1,0:T(8,128)}), f32[16,8,128]{2,1,0:T(8,128)S(1)}, u32[]{:S(2)}, u32[]{:S(2)}) async-start(f32[16,8,128]{2,1,0:T(8,128)} %shard_map.62), calls=%async_computation.2 | async-start | bytes 131072 | tf_op jit(solution)/shard_map/all_to_all | solution.py:266
  56.8 3.1 %collective-permute-start.3 = (f32[8,128]{1,0:T(8,128)S(1)}, f32[8,128]{1,0:T(8,128)S(1)}, u32[]{:S(2)}, u32[]{:S(2)}) collective-permute-start(f32[8,128]{1,0:T(8,128)S(1)} %shard_map.63.mine_ref), channel_id=1, source_target_pairs={{0,1},{1,0},{2,3},{3,2},{4,5},{5,4},{6,7},{7,6},{8,9},{9,8},{10,11... | collective-permute-start | bytes 12296 | tf_op jit(solution)/shard_map/ppermute | solution.py:270
  82.1 11.6 %all-to-all-start.4 = ((bf16[4,96,896]{2,1,0:T(8,128)(2,1)}), bf16[4,96,896]{2,1,0:T(8,128)(2,1)S(1)}, u32[]{:S(2)}, u32[]{:S(2)}) async-start(bf16[4,96,896]{2,1,0:T(8,128)(2,1)} %bitcast.6), calls=%async_computation.4 | async-start | bytes 1376256 | tf_op jit(solution)/shard_map/all_to_all | solution.py:266
  87.4 4.0 %collective-permute-start.4 = (bf16[384,896]{1,0:T(8,128)(2,1)S(1)}, bf16[384,896]{1,0:T(8,128)(2,1)S(1)}, u32[]{:S(2)}, u32[]{:S(2)}) collective-permute-start(bf16[384,896]{1,0:T(8,128)(2,1)S(1)} %shard_map.68), channel_id=1, source_target_pairs={{0,1},{1,0},{2,3},{3,2},{4,5},{5,4},{6,7},{7,6},{8,9},{9,8},{10,11... | collective-permute-start | bytes 2064392 | tf_op jit(solution)/shard_map/ppermute | solution.py:270
  93.8 22.3 %all-to-all-start.5 = ((bf16[16,24,768]{2,1,0:T(8,128)(2,1)}), bf16[16,24,768]{2,1,0:T(8,128)(2,1)S(1)}, u32[]{:S(2)}, u32[]{:S(2)}) async-start(bf16[16,24,768]{2,1,0:T(8,128)(2,1)} %bitcast.8), calls=%async_computation.5 | async-start | bytes 1179648 | tf_op jit(solution)/shard_map/all_to_all | solution.py:266
  97.5 8.6 %collective-permute-start.5 = (bf16[48,896]{1,0:T(8,128)(2,1)S(1)}, bf16[48,896]{1,0:T(8,128)(2,1)S(1)}, u32[]{:S(2)}, u32[]{:S(2)}) collective-permute-start(bf16[48,896]{1,0:T(8,128)(2,1)S(1)} %get-tuple-element.34), channel_id=1, source_target_pairs={{0,6},{2,4},{4,2},{6,0},{1,7},{3,5},{5,3},{7,1},{8,14},{10,12},{12... | collective-permute-start | bytes 258056 | tf_op jit(solution)/shard_map/ppermute | solution.py:270
  106.2 7.3 %collective-permute-start.6 = (bf16[24,896]{1,0:T(8,128)(2,1)S(1)}, bf16[24,896]{1,0:T(8,128)(2,1)S(1)}, u32[]{:S(2)}, u32[]{:S(2)}) collective-permute-start(bf16[24,896]{1,0:T(8,128)(2,1)S(1)} %get-tuple-element.37), channel_id=1, source_target_pairs={{0,2},{2,0},{4,6},{6,4},{1,3},{3,1},{5,7},{7,5},{8,10},{10,8},{12,... | collective-permute-start | bytes 129032 | tf_op jit(solution)/shard_map/ppermute | solution.py:270

commit v11 on v10

--- a/solution.py
+++ b/solution.py
@@ -14,6 +14,7 @@
 NEAR = ("z0", "y0")
 FAR = ("z2", "z1")
 CORE = "c"
+BLOCK = (*CHIPS, CORE)
 
 EPSILON = 1e-06
 LAST = (((1,), (1,)), ((), ()))
@@ -127,40 +128,38 @@
     message_ref[...] = jnp.broadcast_to(message[None], message_ref.shape)
 
 
-def columns_kernel(factor_ref, image_ref, own_ref, other_ref, message_ref):
+def columns_kernel(factor_ref, image_ref, own_ref, other_ref, core_ref, message_ref):
     factor = factor_ref[0] * LOG2_E
     image = image_ref[...]
     own, other = (
         lse_of(factor * f32_dot(image, text[...], LAST)) for text in (own_ref, other_ref)
     )
-    message_ref[...] = eight([*lines(own), *lines(other)])
-
-
-def pair_columns_kernel(mine_ref, theirs_ref, pair_ref):
-    mine, theirs = mine_ref[...], theirs_ref[...]
-    own = pair_lse(mine[0:3], theirs[3:6])
-    other = pair_lse(mine[3:6], theirs[0:3])
-    pair_ref[...] = jnp.concatenate([own, other, jnp.zeros((2, 128), jnp.float32)], axis=0)
-
-
-def message_kernel(row_ref, pair_ref, message_ref):
+    first = core_ref[0] == 0
+    message_ref[...] = eight(
+        [*lines(jnp.where(first, own, other)), *lines(jnp.where(first, other, own))]
+    )
+
+
+def message_kernel(row_ref, columns_ref, message_ref):
     pieces = row_ref[...]
     share = jnp.sum(pieces_lse(pieces)[0:3]) - 2.0 * jnp.max(jnp.sum(pieces, axis=0)[3:4])
     number = lax.broadcasted_iota(jnp.int32, (8, 128), 0)
-    message = jnp.where(number == 6, share, pair_ref[...])
+    message = jnp.where(number == 6, share, columns_ref[...])
     message_ref[...] = jnp.broadcast_to(message[None], message_ref.shape)
 
 
 def weights_kernel(
-    factor_ref, image_ref, own_ref, other_ref, row_ref, pieces_ref,
+    factor_ref, image_ref, own_ref, other_ref, core_ref, row_ref, pieces_ref,
     image_out, own_out, other_out, share_ref,
 ):
     factor = factor_ref[0]
     width = own_ref.shape[1]
     pieces = pieces_ref[...]
     cols = pieces_lse(pieces)
-    own_lse, other_lse = line(cols[0:3]), line(cols[3:6])
-    col_share = jnp.sum(own_lse) + jnp.sum(other_lse)
+    low_lse, high_lse = line(cols[0:3]), line(cols[3:6])
+    first = core_ref[0] == 0
+    own_lse, other_lse = jnp.where(first, low_lse, high_lse), jnp.where(first, high_lse, low_lse)
+    col_share = jnp.sum(low_lse) + jnp.sum(high_lse)
     rows = pieces_lse(row_ref[...])[0:3]
     row_share = jnp.max(jnp.sum(pieces, axis=0)[6:7])
     share_ref[...] = jnp.broadcast_to(row_share, share_ref.shape)
@@ -183,23 +182,16 @@
     image_out[:, width:] = packed(col_share, image_out.shape[0])
 
 
-def other_sums_kernel(image_ref, weights_ref, share_ref, sums_ref):
-    image = image_ref[...]
-    width = image.shape[1]
-    sums_ref[:, :width] = f32_dot(weights_ref[...], image, FIRST).astype(jnp.bfloat16)
-    sums_ref[:, width:] = packed(jnp.max(share_ref[...]), sums_ref.shape[0])
+def other_sums_kernel(image_ref, weights_ref, sums_ref):
+    sums_ref[...] = f32_dot(weights_ref[...], image_ref[...], FIRST).astype(jnp.bfloat16)
 
 
 def own_sums_kernel(image_ref, weights_ref, sums_ref):
     sums_ref[...] = f32_dot(weights_ref[...], image_ref[...], FIRST)
 
 
-def pair_sums_kernel(own_ref, theirs_ref, shared_ref, sums_ref, share_ref):
-    width = own_ref.shape[1]
-    theirs = theirs_ref[...].astype(jnp.float32)
-    sums_ref[...] = (own_ref[...] + theirs[:, :width]).astype(jnp.bfloat16)
-    share = jnp.max(shared_ref[...]) + unpacked(theirs, width)
-    share_ref[...] = jnp.broadcast_to(share, share_ref.shape)
+def pair_sums_kernel(own_ref, theirs_ref, sums_ref):
+    sums_ref[...] = (own_ref[...] + theirs_ref[...].astype(jnp.float32)).astype(jnp.bfloat16)
 
 
 def slabs_sum(pieces_ref, rows):
@@ -289,7 +281,7 @@
     image_rows, text_rows = own_rows * inner, own_rows * chips
     wide = width + EXTRA
     work = 2 * image_rows * text_rows * width
-    high, low = place(FAR[0]), place(FAR[1])
+    high, low, core = place(FAR[0]), place(FAR[1]), place(CORE)
     tile = shape((8, 128), f32)
 
     text_copies = kernel_call(text_units_kernel, shape((text_rows, width), bf16), text_emb)
@@ -311,32 +303,29 @@
         rows_kernel, shape((inner, 8, 128), f32), *tile_of, diagonal, flops=2 * work
     )
     row_pieces = exchanged(row_message, INNER)
-    col_part = kernel_call(columns_kernel, tile, *tile_of, flops=2 * work)
-    pair = kernel_call(pair_columns_kernel, tile, col_part, swapped(col_part, CORE))
+    col_part = kernel_call(columns_kernel, tile, *tile_of, core, flops=2 * work)
     col_message = kernel_call(
-        message_kernel, shape((chips, 8, 128), f32), row_pieces, pair
-    )
-    col_pieces = exchanged(col_message, CHIPS)
+        message_kernel, shape((lax.axis_size(BLOCK), 8, 128), f32), row_pieces, col_part
+    )
+    col_pieces = exchanged(col_message, BLOCK)
 
     half_tile = shape((image_rows, text_rows), bf16)
     image_part, own_weights, other_weights, row_share = kernel_call(
         weights_kernel,
         (shape((image_rows, wide), bf16), half_tile, half_tile, tile),
-        *tile_of, row_pieces, col_pieces,
+        *tile_of, core, row_pieces, col_pieces,
         flops=4 * work,
     )
     other_part = kernel_call(
-        other_sums_kernel, shape((text_rows, wide), bf16),
-        image_group, other_weights, row_share,
+        other_sums_kernel, shape((text_rows, width), bf16), image_group, other_weights,
         flops=work,
     )
     own_part = kernel_call(
         own_sums_kernel, shape((text_rows, width), f32), image_group, own_weights, flops=work
     )
     image_pieces = exchanged(image_part, NEAR)
-    text_part, row_share = kernel_call(
-        pair_sums_kernel, (shape((text_rows, width), bf16), tile),
-        own_part, swapped(other_part, CORE), row_share,
+    text_part = kernel_call(
+        pair_sums_kernel, shape((text_rows, width), bf16), own_part, swapped(other_part, CORE)
     )
     text_pieces = exchanged(after(text_part, image_pieces), CHIPS)
 

time: 118 us -> 123 us (1.042)
  waiting for transfers between devices: 27.8 us -> 33.7 us
  starting transfers between devices: 59.6 us -> 57.8 us
    all_to_all x5, waiting for transfers between devices: 9.79 us -> 18 us  [exchanged(): lax.all_to_all(split, axis, split_axis=0, concat_axis=0, tiled=True)]
    ppermute x7 -> x6, waiting for transfers between devices: 18 us -> 15.7 us  [swapped(): lax.ppermute(x, axis, [(k, k ^ offset) for k in range(lax.axis_size(axis))])]
    ppermute x7 -> x6, starting transfers between devices: 27.7 us -> 26.2 us  [swapped(): lax.ppermute(x, axis, [(k, k ^ offset) for k in range(lax.axis_size(axis))])]
    pallas_call x16 -> x15, Pallas kernels: 11.2 us -> 11.1 us  [kernel_call(): pl.pallas_call(body, out_shape=out_shape, in_specs=[spec(a) for a in args...]
  transfers between devices with their start and end apart: 12 -> 11, of which waited for: 11 -> 10; matrix products, arithmetic and copies ran while one was open for 0% -> 0% of each run, Pallas kernels for 4% -> 4%
where the time goes in v11:
time: 123 us; the launch traced here: 122 us
  starting transfers between devices  57.8 us (47%)
  waiting for transfers between devices  33.7 us (27%)
  blocking collectives  17.1 us (14%)
  Pallas kernels  11.1 us (9%)
  between operations  1.43 us (1%)
    all_to_all x5, starting transfers between devices, exchanged(): lax.all_to_all(split, axis, split_axis=0, concat_axis=0, tiled=True)  31.6 us
    ppermute x6, starting transfers between devices, swapped(): lax.ppermute(x, axis, [(k, k ^ offset) for k in range(lax.axis_size(axis))])  26.2 us
    all_to_all x5, waiting for transfers between devices, exchanged(): lax.all_to_all(split, axis, split_axis=0, concat_axis=0, tiled=True)  18 us
    all_to_all x1, blocking collectives, exchanged(): lax.all_to_all(split, axis, split_axis=0, concat_axis=0, tiled=True)  17.1 us
    ppermute x6, waiting for transfers between devices, swapped(): lax.ppermute(x, axis, [(k, k ^ offset) for k in range(lax.axis_size(axis))])  15.7 us
    pallas_call x15, Pallas kernels, kernel_call(): pl.pallas_call(body, out_shape=out_shape, in_specs=[spec(a) for a in args...  11.1 us
  transfers between devices with their start and end apart: 11, of which 10 were waited for; matrix products, arithmetic and copies ran while one was open for 0% of the time, Pallas kernels for 4%

profile of v11, /device:TPU:8, one launch (start us, length us, event | category | flops | bytes accessed | tf_op | source)
XLA Modules:
  0.0 122.1 jit_solution(14897214320946928840)
XLA Ops:
  0.6 0.0 copy-start
  0.6 0.9 copy-done
  1.5 0.0 copy-start.1
  1.5 0.0 copy-start.2
  1.5 1.0 shard_map.61
  2.5 8.8 %all-to-all-start = ((bf16[16,24,768]{2,1,0:T(8,128)(2,1)}), bf16[16,24,768]{2,1,0:T(8,128)(2,1)S(1)}, u32[]{:S(2)}, u32[]{:S(2)}) async-start(bf16[16,24,768]{2,1,0:T(8,128)(2,1)} %bitcast.2), calls=%async_computation | async-start | bytes 1179648 | tf_op jit(solution)/shard_map/all_to_all | solution.py:258
  11.3 0.0 copy-done.1
  11.3 0.0 copy-done.2
  11.3 0.2 shard_map.58
  11.5 6.1 %collective-permute-start = (bf16[24,768]{1,0:T(8,128)(2,1)S(1)}, bf16[24,768]{1,0:T(8,128)(2,1)S(1)}, u32[]{:S(2)}, u32[]{:S(2)}) collective-permute-start(bf16[24,768]{1,0:T(8,128)(2,1)S(1)} %get-tuple-element.21.mine_ref), channel_id=1, source_target_pairs={{0,2},{2,0},{4,6},{6,4},{1,3},{3,1},{5,7},{7,5},{8,10},{10,8},{12,... | collective-permute-start | bytes 110600 | tf_op jit(solution)/shard_map/ppermute | solution.py:262
  17.6 1.9 %collective-permute-done.theirs_ref = bf16[24,768]{1,0:T(8,128)(2,1)S(1)} collective-permute-done((bf16[24,768]{1,0:T(8,128)(2,1)S(1)}, bf16[24,768]{1,0:T(8,128)(2,1)S(1)}, u32[]{:S(2)}, u32[]{:S(2)}) %collective-permute-start) | collective-permute-done | bytes 36896 | tf_op jit(solution)/shard_map/ppermute | solution.py:262
  19.6 9.7 %collective-permute-start.1 = (bf16[48,768]{1,0:T(8,128)(2,1)S(1)}, bf16[48,768]{1,0:T(8,128)(2,1)S(1)}, u32[]{:S(2)}, u32[]{:S(2)}) collective-permute-start(bf16[48,768]{1,0:T(8,128)(2,1)S(1)} %shard_map.59.mine_ref), channel_id=1, source_target_pairs={{0,6},{2,4},{4,2},{6,0},{1,7},{3,5},{5,3},{7,1},{8,14},{10,12},{12... | collective-permute-start | bytes 221192 | tf_op jit(solution)/shard_map/ppermute | solution.py:262
  29.3 2.4 %collective-permute-done.1.theirs_ref = bf16[48,768]{1,0:T(8,128)(2,1)S(1)} collective-permute-done((bf16[48,768]{1,0:T(8,128)(2,1)S(1)}, bf16[48,768]{1,0:T(8,128)(2,1)S(1)}, u32[]{:S(2)}, u32[]{:S(2)}) %collective-permute-start.1) | collective-permute-done | bytes 73760 | tf_op jit(solution)/shard_map/ppermute | solution.py:262
  31.6 0.9 shard_map.60
  32.5 0.0 all-to-all-done
  32.5 4.9 %all-to-all-start.1 = ((bf16[4,96,768]{2,1,0:T(8,128)(2,1)}), bf16[4,96,768]{2,1,0:T(8,128)(2,1)S(1)}, u32[]{:S(2)}, u32[]{:S(2)}) async-start(bf16[4,96,768]{2,1,0:T(8,128)(2,1)} %bitcast.4), calls=%async_computation.1 | async-start | bytes 1179648 | tf_op jit(solution)/shard_map/all_to_all | solution.py:258
  37.4 1.9 %collective-permute-start.2 = (bf16[384,768]{1,0:T(8,128)(2,1)S(1)}, bf16[384,768]{1,0:T(8,128)(2,1)S(1)}, u32[]{:S(2)}, u32[]{:S(2)}) collective-permute-start(bf16[384,768]{1,0:T(8,128)(2,1)S(1)} %bitcast.16), channel_id=1, source_target_pairs={{0,1},{1,0},{2,3},{3,2},{4,5},{5,4},{6,7},{7,6},{8,9},{9,8},{10,11... | collective-permute-start | bytes 1769480 | tf_op jit(solution)/shard_map/ppermute | solution.py:262
  40.0 1.3 %collective-permute-done.2.other_ref = bf16[384,768]{1,0:T(8,128)(2,1)S(1)} collective-permute-done((bf16[384,768]{1,0:T(8,128)(2,1)S(1)}, bf16[384,768]{1,0:T(8,128)(2,1)S(1)}, u32[]{:S(2)}, u32[]{:S(2)}) %collective-permute-start.2) | collective-permute-done | bytes 589856 | tf_op jit(solution)/shard_map/ppermute | solution.py:262
  41.3 3.1 %all-to-all-done.1 = bf16[4,96,768]{2,1,0:T(8,128)(2,1)S(1)} async-done(((bf16[4,96,768]{2,1,0:T(8,128)(2,1)}), bf16[4,96,768]{2,1,0:T(8,128)(2,1)S(1)}, u32[]{:S(2)}, u32[]{:S(2)}) %all-to-all-start.1) | async-done | bytes 589856 | tf_op jit(solution)/shard_map/all_to_all | solution.py:258
  44.4 1.6 %shard_map.62 = f32[16,8,128]{2,1,0:T(8,128)} custom-call(f32[1]{0:T(128)S(6)} %copy.6.factor_ref, bf16[384,768]{1,0:T(8,128)(2,1)S(1)} %bitcast.11, bf16[384,768]{1,0:T(8,128)(2,1)S(1)} %bitcast.17, bf16[384,768]{1,0:T(8,128)(2,1)S(1)} %collective-permute-done.2.other_ref, f32[8,128]{1,0:T(8,128)S(1)} %get-tuple-element.23.diagonal_ref), custom_call_target="tpu_custom_call" | custom-call | flops 452984832 | bytes 1839108 | tf_op jit(solution)/shard_map/pallas_call | solution.py:42
  46.0 9.9 %all-to-all-start.2 = ((f32[16,8,128]{2,1,0:T(8,128)}), f32[16,8,128]{2,1,0:T(8,128)S(1)}, u32[]{:S(2)}, u32[]{:S(2)}) async-start(f32[16,8,128]{2,1,0:T(8,128)} %shard_map.62), calls=%async_computation.2 | async-start | bytes 131072 | tf_op jit(solution)/shard_map/all_to_all | solution.py:258
  55.9 0.9 shard_map.63.columns_ref
  56.8 6.7 %all-to-all-done.2.row_ref = f32[16,8,128]{2,1,0:T(8,128)S(1)} async-done(((f32[16,8,128]{2,1,0:T(8,128)}), f32[16,8,128]{2,1,0:T(8,128)S(1)}, u32[]{:S(2)}, u32[]{:S(2)}) %all-to-all-start.2) | async-done | bytes 65568 | tf_op jit(solution)/shard_map/all_to_all | solution.py:258
  63.5 0.2 shard_map.64
  63.7 17.1 %all_to_all.30.pieces_ref = f32[32,8,128]{2,1,0:T(8,128)S(1)} all-to-all(f32[32,8,128]{2,1,0:T(8,128)S(1)} %shard_map.64), channel_id=1, replica_groups=mesh['z0'=2,'y2'=2,'y1'=2,'y0'=2,'x'=4,'z2'=2,'z1'=2,'c'=2] {'x','y2','y..., dimensions={0} | all-to-all | bytes 262144 | tf_op jit(solution)/shard_map/all_to_all | solution.py:258
  80.8 2.5 %shard_map.65 = (bf16[384,896]{1,0:T(8,128)(2,1)}, bf16[384,384]{1,0:T(8,128)(2,1)S(1)}, bf16[384,384]{1,0:T(8,128)(2,1)S(1)}, f32[8,128]{1,0:T(8,128)S(1)}) custom-call(f32[1]{0:T(128)S(6)} %copy.6.factor_ref, bf16[384,768]{1,0:T(8,128)(2,1)S(1)} %bitcast.13, bf16[384,768]{1,0:T(8,128)(2,1)S(1)} %bitcast.19, ...), custom_call_target="tpu_custom_call" | custom-call | flops 905969664 | bytes 3248136 | tf_op jit(solution)/shard_map/pallas_call | solution.py:42
  83.3 4.4 %all-to-all-start.4 = ((bf16[4,96,896]{2,1,0:T(8,128)(2,1)}), bf16[4,96,896]{2,1,0:T(8,128)(2,1)S(1)}, u32[]{:S(2)}, u32[]{:S(2)}) async-start(bf16[4,96,896]{2,1,0:T(8,128)(2,1)} %bitcast.7), calls=%async_computation.4 | async-start | bytes 1376256 | tf_op jit(solution)/shard_map/all_to_all | solution.py:258
  87.7 0.5 shard_map.67
  88.2 2.0 %collective-permute-start.3 = (bf16[384,768]{1,0:T(8,128)(2,1)S(1)}, bf16[384,768]{1,0:T(8,128)(2,1)S(1)}, u32[]{:S(2)}, u32[]{:S(2)}) collective-permute-start(bf16[384,768]{1,0:T(8,128)(2,1)S(1)} %shard_map.67), channel_id=1, source_target_pairs={{0,1},{1,0},{2,3},{3,2},{4,5},{5,4},{6,7},{7,6},{8,9},{9,8},{10,11... | collective-permute-start | bytes 1769480 | tf_op jit(solution)/shard_map/ppermute | solution.py:262
  90.2 0.5 shard_map.66.own_ref
  90.7 1.4 %collective-permute-done.3.theirs_ref = bf16[384,768]{1,0:T(8,128)(2,1)S(1)} collective-permute-done((bf16[384,768]{1,0:T(8,128)(2,1)S(1)}, bf16[384,768]{1,0:T(8,128)(2,1)S(1)}, u32[]{:S(2)}, u32[]{:S(2)}) %collective-permute-start.3) | collective-permute-done | bytes 589856 | tf_op jit(solution)/shard_map/ppermute | solution.py:262
  92.1 0.9 shard_map.68
  93.0 4.6 %all-to-all-done.4 = bf16[4,96,896]{2,1,0:T(8,128)(2,1)S(1)} async-done(((bf16[4,96,896]{2,1,0:T(8,128)(2,1)}), bf16[4,96,896]{2,1,0:T(8,128)(2,1)S(1)}, u32[]{:S(2)}, u32[]{:S(2)}) %all-to-all-start.4) | async-done | bytes 688160 | tf_op jit(solution)/shard_map/all_to_all | solution.py:258
  97.7 3.6 %all-to-all-start.5 = ((bf16[16,24,768]{2,1,0:T(8,128)(2,1)}), bf16[16,24,768]{2,1,0:T(8,128)(2,1)S(1)}, u32[]{:S(2)}, u32[]{:S(2)}) async-start(bf16[16,24,768]{2,1,0:T(8,128)(2,1)} %bitcast.9), calls=%async_computation.5 | async-start | bytes 1179648 | tf_op jit(solution)/shard_map/all_to_all | solution.py:258
  101.2 0.2 shard_map.69
  101.4 2.7 %collective-permute-start.4 = (bf16[48,896]{1,0:T(8,128)(2,1)S(1)}, bf16[48,896]{1,0:T(8,128)(2,1)S(1)}, u32[]{:S(2)}, u32[]{:S(2)}) collective-permute-start(bf16[48,896]{1,0:T(8,128)(2,1)S(1)} %get-tuple-element.30), channel_id=1, source_target_pairs={{0,6},{2,4},{4,2},{6,0},{1,7},{3,5},{5,3},{7,1},{8,14},{10,12},{12... | collective-permute-start | bytes 258056 | tf_op jit(solution)/shard_map/ppermute | solution.py:262
  104.1 5.8 %collective-permute-done.4.theirs_ref = bf16[48,896]{1,0:T(8,128)(2,1)S(1)} collective-permute-done((bf16[48,896]{1,0:T(8,128)(2,1)S(1)}, bf16[48,896]{1,0:T(8,128)(2,1)S(1)}, u32[]{:S(2)}, u32[]{:S(2)}) %collective-permute-start.4) | collective-permute-done | bytes 86048 | tf_op jit(solution)/shard_map/ppermute | solution.py:262
  109.9 0.1 shard_map.70
  110.0 3.9 %collective-permute-start.5 = (bf16[24,896]{1,0:T(8,128)(2,1)S(1)}, bf16[24,896]{1,0:T(8,128)(2,1)S(1)}, u32[]{:S(2)}, u32[]{:S(2)}) collective-permute-start(bf16[24,896]{1,0:T(8,128)(2,1)S(1)} %get-tuple-element.33), channel_id=1, source_target_pairs={{0,2},{2,0},{4,6},{6,4},{1,3},{3,1},{5,7},{7,5},{8,10},{10,8},{12,... | collective-permute-start | bytes 129032 | tf_op jit(solution)/shard_map/ppermute | solution.py:262
  114.0 2.9 %collective-permute-done.5.theirs_ref = bf16[24,896]{1,0:T(8,128)(2,1)S(1)} collective-permute-done((bf16[24,896]{1,0:T(8,128)(2,1)S(1)}, bf16[24,896]{1,0:T(8,128)(2,1)S(1)}, u32[]{:S(2)}, u32[]{:S(2)}) %collective-permute-start.5) | collective-permute-done | bytes 43040 | tf_op jit(solution)/shard_map/ppermute | solution.py:262
  116.8 0.8 shard_map.71
  117.7 3.6 %all-to-all-done.5 = bf16[16,24,768]{2,1,0:T(8,128)(2,1)S(1)} async-done(((bf16[16,24,768]{2,1,0:T(8,128)(2,1)}), bf16[16,24,768]{2,1,0:T(8,128)(2,1)S(1)}, u32[]{:S(2)}, u32[]{:S(2)}) %all-to-all-start.5) | async-done | bytes 589856 | tf_op jit(solution)/shard_map/all_to_all | solution.py:258
  121.3 0.8 shard_map.72
  (1 shorter events, 0.0 us)
Async XLA Ops:
  0.6 0.9 copy-start
  1.5 9.7 %copy-start.1 = (f32[24,768]{1,0:T(8,128)S(1)}, f32[24,768]{1,0:T(8,128)}, u32[]{:S(2)}) copy-start(f32[24,768]{1,0:T(8,128)} %values_ref.7) | copy-start | bytes 221188
  1.5 9.8 %copy-start.2 = (f32[24,768]{1,0:T(8,128)S(1)}, f32[24,768]{1,0:T(8,128)}, u32[]{:S(2)}) copy-start(f32[24,768]{1,0:T(8,128)} %paired_ref.3) | copy-start | bytes 221188
  2.5 30.0 %all-to-all-start = ((bf16[16,24,768]{2,1,0:T(8,128)(2,1)}), bf16[16,24,768]{2,1,0:T(8,128)(2,1)S(1)}, u32[]{:S(2)}, u32[]{:S(2)}) async-start(bf16[16,24,768]{2,1,0:T(8,128)(2,1)} %bitcast.2), calls=%async_computation | async-start | bytes 1179648 | tf_op jit(solution)/shard_map/all_to_all | solution.py:258
  11.5 8.0 %collective-permute-start = (bf16[24,768]{1,0:T(8,128)(2,1)S(1)}, bf16[24,768]{1,0:T(8,128)(2,1)S(1)}, u32[]{:S(2)}, u32[]{:S(2)}) collective-permute-start(bf16[24,768]{1,0:T(8,128)(2,1)S(1)} %get-tuple-element.21.mine_ref), channel_id=1, source_target_pairs={{0,2},{2,0},{4,6},{6,4},{1,3},{3,1},{5,7},{7,5},{8,10},{10,8},{12,... | collective-permute-start | bytes 110600 | tf_op jit(solution)/shard_map/ppermute | solution.py:262
  19.6 12.1 %collective-permute-start.1 = (bf16[48,768]{1,0:T(8,128)(2,1)S(1)}, bf16[48,768]{1,0:T(8,128)(2,1)S(1)}, u32[]{:S(2)}, u32[]{:S(2)}) collective-permute-start(bf16[48,768]{1,0:T(8,128)(2,1)S(1)} %shard_map.59.mine_ref), channel_id=1, source_target_pairs={{0,6},{2,4},{4,2},{6,0},{1,7},{3,5},{5,3},{7,1},{8,14},{10,12},{12... | collective-permute-start | bytes 221192 | tf_op jit(solution)/shard_map/ppermute | solution.py:262
  32.5 11.9 %all-to-all-start.1 = ((bf16[4,96,768]{2,1,0:T(8,128)(2,1)}), bf16[4,96,768]{2,1,0:T(8,128)(2,1)S(1)}, u32[]{:S(2)}, u32[]{:S(2)}) async-start(bf16[4,96,768]{2,1,0:T(8,128)(2,1)} %bitcast.4), calls=%async_computation.1 | async-start | bytes 1179648 | tf_op jit(solution)/shard_map/all_to_all | solution.py:258
  37.4 3.9 %collective-permute-start.2 = (bf16[384,768]{1,0:T(8,128)(2,1)S(1)}, bf16[384,768]{1,0:T(8,128)(2,1)S(1)}, u32[]{:S(2)}, u32[]{:S(2)}) collective-permute-start(bf16[384,768]{1,0:T(8,128)(2,1)S(1)} %bitcast.16), channel_id=1, source_target_pairs={{0,1},{1,0},{2,3},{3,2},{4,5},{5,4},{6,7},{7,6},{8,9},{9,8},{10,11... | collective-permute-start | bytes 1769480 | tf_op jit(solution)/shard_map/ppermute | solution.py:262
  46.0 17.5 %all-to-all-start.2 = ((f32[16,8,128]{2,1,0:T(8,128)}), f32[16,8,128]{2,1,0:T(8,128)S(1)}, u32[]{:S(2)}, u32[]{:S(2)}) async-start(f32[16,8,128]{2,1,0:T(8,128)} %shard_map.62), calls=%async_computation.2 | async-start | bytes 131072 | tf_op jit(solution)/shard_map/all_to_all | solution.py:258
  83.3 14.3 %all-to-all-start.4 = ((bf16[4,96,896]{2,1,0:T(8,128)(2,1)}), bf16[4,96,896]{2,1,0:T(8,128)(2,1)S(1)}, u32[]{:S(2)}, u32[]{:S(2)}) async-start(bf16[4,96,896]{2,1,0:T(8,128)(2,1)} %bitcast.7), calls=%async_computation.4 | async-start | bytes 1376256 | tf_op jit(solution)/shard_map/all_to_all | solution.py:258
  88.2 3.9 %collective-permute-start.3 = (bf16[384,768]{1,0:T(8,128)(2,1)S(1)}, bf16[384,768]{1,0:T(8,128)(2,1)S(1)}, u32[]{:S(2)}, u32[]{:S(2)}) collective-permute-start(bf16[384,768]{1,0:T(8,128)(2,1)S(1)} %shard_map.67), channel_id=1, source_target_pairs={{0,1},{1,0},{2,3},{3,2},{4,5},{5,4},{6,7},{7,6},{8,9},{9,8},{10,11... | collective-permute-start | bytes 1769480 | tf_op jit(solution)/shard_map/ppermute | solution.py:262
  97.7 23.6 %all-to-all-start.5 = ((bf16[16,24,768]{2,1,0:T(8,128)(2,1)}), bf16[16,24,768]{2,1,0:T(8,128)(2,1)S(1)}, u32[]{:S(2)}, u32[]{:S(2)}) async-start(bf16[16,24,768]{2,1,0:T(8,128)(2,1)} %bitcast.9), calls=%async_computation.5 | async-start | bytes 1179648 | tf_op jit(solution)/shard_map/all_to_all | solution.py:258
  101.4 8.5 %collective-permute-start.4 = (bf16[48,896]{1,0:T(8,128)(2,1)S(1)}, bf16[48,896]{1,0:T(8,128)(2,1)S(1)}, u32[]{:S(2)}, u32[]{:S(2)}) collective-permute-start(bf16[48,896]{1,0:T(8,128)(2,1)S(1)} %get-tuple-element.30), channel_id=1, source_target_pairs={{0,6},{2,4},{4,2},{6,0},{1,7},{3,5},{5,3},{7,1},{8,14},{10,12},{12... | collective-permute-start | bytes 258056 | tf_op jit(solution)/shard_map/ppermute | solution.py:262
  110.0 6.8 %collective-permute-start.5 = (bf16[24,896]{1,0:T(8,128)(2,1)S(1)}, bf16[24,896]{1,0:T(8,128)(2,1)S(1)}, u32[]{:S(2)}, u32[]{:S(2)}) collective-permute-start(bf16[24,896]{1,0:T(8,128)(2,1)S(1)} %get-tuple-element.33), channel_id=1, source_target_pairs={{0,2},{2,0},{4,6},{6,4},{1,3},{3,1},{5,7},{7,5},{8,10},{10,8},{12,... | collective-permute-start | bytes 129032 | tf_op jit(solution)/shard_map/ppermute | solution.py:262

commit v12 on v10

--- a/solution.py
+++ b/solution.py
@@ -10,7 +10,7 @@
 
 ALL = ("z0", "y2", "y1", "y0", "x", "z2", "z1", "c")
 INNER = ("z2", "z1", "z0", "y0")
-CHIPS = ("x", "y2", "y1")
+CHIPS = ("y2", "y1", "x")
 NEAR = ("z0", "y0")
 FAR = ("z2", "z1")
 CORE = "c"

time: 118 us -> 118 us (level)
  no operation moved by 1% of the time
where the time goes in v12:
time: 118 us; the launch traced here: 117 us
  starting transfers between devices  59.1 us (50%)
  waiting for transfers between devices  28 us (24%)
  blocking collectives  16.3 us (14%)
  Pallas kernels  11.2 us (9%)
  between operations  1.44 us (1%)
    all_to_all x5, starting transfers between devices, exchanged(): lax.all_to_all(split, axis, split_axis=0, concat_axis=0, tiled=True)  31.5 us
    ppermute x7, starting transfers between devices, swapped(): lax.ppermute(x, axis, [(k, k ^ offset) for k in range(lax.axis_size(axis))])  27.5 us
    ppermute x7, waiting for transfers between devices, swapped(): lax.ppermute(x, axis, [(k, k ^ offset) for k in range(lax.axis_size(axis))])  18.2 us
    all_to_all x1, blocking collectives, exchanged(): lax.all_to_all(split, axis, split_axis=0, concat_axis=0, tiled=True)  16.3 us
    pallas_call x16, Pallas kernels, kernel_call(): pl.pallas_call(body, out_shape=out_shape, in_specs=[spec(a) for a in args...  11.2 us
    all_to_all x5, waiting for transfers between devices, exchanged(): lax.all_to_all(split, axis, split_axis=0, concat_axis=0, tiled=True)  9.83 us
  transfers between devices with their start and end apart: 12, of which 11 were waited for; matrix products, arithmetic and copies ran while one was open for 0% of the time, Pallas kernels for 4%

profile of v12, /device:TPU:8, one launch (start us, length us, event | category | flops | bytes accessed | tf_op | source)
XLA Modules:
  0.0 116.9 jit_solution(7948371237792528918)
XLA Ops:
  0.6 0.0 copy-start
  0.6 0.9 copy-done
  1.5 0.0 copy-start.1
  1.5 0.0 copy-start.2
  1.5 1.0 shard_map.61
  2.5 8.8 %all-to-all-start = ((bf16[16,24,768]{2,1,0:T(8,128)(2,1)}), bf16[16,24,768]{2,1,0:T(8,128)(2,1)S(1)}, u32[]{:S(2)}, u32[]{:S(2)}) async-start(bf16[16,24,768]{2,1,0:T(8,128)(2,1)} %bitcast.2), calls=%async_computation | async-start | bytes 1179648 | tf_op jit(solution)/shard_map/all_to_all | solution.py:266
  11.2 0.0 copy-done.1
  11.3 0.0 copy-done.2
  11.3 0.2 shard_map.58
  11.5 6.1 %collective-permute-start = (bf16[24,768]{1,0:T(8,128)(2,1)S(1)}, bf16[24,768]{1,0:T(8,128)(2,1)S(1)}, u32[]{:S(2)}, u32[]{:S(2)}) collective-permute-start(bf16[24,768]{1,0:T(8,128)(2,1)S(1)} %get-tuple-element.23.mine_ref), channel_id=1, source_target_pairs={{0,2},{2,0},{4,6},{6,4},{1,3},{3,1},{5,7},{7,5},{8,10},{10,8},{12,... | collective-permute-start | bytes 110600 | tf_op jit(solution)/shard_map/ppermute | solution.py:270
  17.6 1.9 %collective-permute-done.theirs_ref = bf16[24,768]{1,0:T(8,128)(2,1)S(1)} collective-permute-done((bf16[24,768]{1,0:T(8,128)(2,1)S(1)}, bf16[24,768]{1,0:T(8,128)(2,1)S(1)}, u32[]{:S(2)}, u32[]{:S(2)}) %collective-permute-start) | collective-permute-done | bytes 36896 | tf_op jit(solution)/shard_map/ppermute | solution.py:270
  19.5 9.7 %collective-permute-start.1 = (bf16[48,768]{1,0:T(8,128)(2,1)S(1)}, bf16[48,768]{1,0:T(8,128)(2,1)S(1)}, u32[]{:S(2)}, u32[]{:S(2)}) collective-permute-start(bf16[48,768]{1,0:T(8,128)(2,1)S(1)} %shard_map.59.mine_ref), channel_id=1, source_target_pairs={{0,6},{2,4},{4,2},{6,0},{1,7},{3,5},{5,3},{7,1},{8,14},{10,12},{12... | collective-permute-start | bytes 221192 | tf_op jit(solution)/shard_map/ppermute | solution.py:270
  29.3 2.4 %collective-permute-done.1.theirs_ref = bf16[48,768]{1,0:T(8,128)(2,1)S(1)} collective-permute-done((bf16[48,768]{1,0:T(8,128)(2,1)S(1)}, bf16[48,768]{1,0:T(8,128)(2,1)S(1)}, u32[]{:S(2)}, u32[]{:S(2)}) %collective-permute-start.1) | collective-permute-done | bytes 73760 | tf_op jit(solution)/shard_map/ppermute | solution.py:270
  31.6 0.9 shard_map.60
  32.5 0.0 all-to-all-done
  32.5 4.9 %all-to-all-start.1 = ((bf16[4,96,768]{2,1,0:T(8,128)(2,1)}), bf16[4,96,768]{2,1,0:T(8,128)(2,1)S(1)}, u32[]{:S(2)}, u32[]{:S(2)}) async-start(bf16[4,96,768]{2,1,0:T(8,128)(2,1)} %bitcast.4), calls=%async_computation.1 | async-start | bytes 1179648 | tf_op jit(solution)/shard_map/all_to_all | solution.py:266
  37.5 1.9 %collective-permute-start.2 = (bf16[384,768]{1,0:T(8,128)(2,1)S(1)}, bf16[384,768]{1,0:T(8,128)(2,1)S(1)}, u32[]{:S(2)}, u32[]{:S(2)}) collective-permute-start(bf16[384,768]{1,0:T(8,128)(2,1)S(1)} %bitcast.15), channel_id=1, source_target_pairs={{0,1},{1,0},{2,3},{3,2},{4,5},{5,4},{6,7},{7,6},{8,9},{9,8},{10,11... | collective-permute-start | bytes 1769480 | tf_op jit(solution)/shard_map/ppermute | solution.py:270
  40.0 1.3 %collective-permute-done.2.other_ref = bf16[384,768]{1,0:T(8,128)(2,1)S(1)} collective-permute-done((bf16[384,768]{1,0:T(8,128)(2,1)S(1)}, bf16[384,768]{1,0:T(8,128)(2,1)S(1)}, u32[]{:S(2)}, u32[]{:S(2)}) %collective-permute-start.2) | collective-permute-done | bytes 589856 | tf_op jit(solution)/shard_map/ppermute | solution.py:270
  41.4 3.1 %all-to-all-done.1 = bf16[4,96,768]{2,1,0:T(8,128)(2,1)S(1)} async-done(((bf16[4,96,768]{2,1,0:T(8,128)(2,1)}), bf16[4,96,768]{2,1,0:T(8,128)(2,1)S(1)}, u32[]{:S(2)}, u32[]{:S(2)}) %all-to-all-start.1) | async-done | bytes 589856 | tf_op jit(solution)/shard_map/all_to_all | solution.py:266
  44.4 1.6 %shard_map.62 = f32[16,8,128]{2,1,0:T(8,128)} custom-call(f32[1]{0:T(128)S(6)} %copy.6.factor_ref, bf16[384,768]{1,0:T(8,128)(2,1)S(1)} %bitcast.10, bf16[384,768]{1,0:T(8,128)(2,1)S(1)} %bitcast.16, bf16[384,768]{1,0:T(8,128)(2,1)S(1)} %collective-permute-done.2.other_ref, f32[8,128]{1,0:T(8,128)S(1)} %get-tuple-element.25.diagonal_ref), custom_call_target="tpu_custom_call" | custom-call | flops 452984832 | bytes 1839108 | tf_op jit(solution)/shard_map/pallas_call | solution.py:41
  46.0 9.5 %all-to-all-start.2 = ((f32[16,8,128]{2,1,0:T(8,128)}), f32[16,8,128]{2,1,0:T(8,128)S(1)}, u32[]{:S(2)}, u32[]{:S(2)}) async-start(f32[16,8,128]{2,1,0:T(8,128)} %shard_map.62), calls=%async_computation.2 | async-start | bytes 131072 | tf_op jit(solution)/shard_map/all_to_all | solution.py:266
  55.4 0.9 shard_map.63.mine_ref
  56.3 1.9 %collective-permute-start.3 = (f32[8,128]{1,0:T(8,128)S(1)}, f32[8,128]{1,0:T(8,128)S(1)}, u32[]{:S(2)}, u32[]{:S(2)}) collective-permute-start(f32[8,128]{1,0:T(8,128)S(1)} %shard_map.63.mine_ref), channel_id=1, source_target_pairs={{0,1},{1,0},{2,3},{3,2},{4,5},{5,4},{6,7},{7,6},{8,9},{9,8},{10,11... | collective-permute-start | bytes 12296 | tf_op jit(solution)/shard_map/ppermute | solution.py:270
  58.3 1.1 collective-permute-done.3.theirs_ref
  59.4 3.6 %all-to-all-done.2.row_ref = f32[16,8,128]{2,1,0:T(8,128)S(1)} async-done(((f32[16,8,128]{2,1,0:T(8,128)}), f32[16,8,128]{2,1,0:T(8,128)S(1)}, u32[]{:S(2)}, u32[]{:S(2)}) %all-to-all-start.2) | async-done | bytes 65568 | tf_op jit(solution)/shard_map/all_to_all | solution.py:266
  63.1 0.2 shard_map.65
  63.2 16.3 %all_to_all.30.pieces_ref = f32[16,8,128]{2,1,0:T(8,128)S(1)} all-to-all(f32[16,8,128]{2,1,0:T(8,128)S(1)} %shard_map.65), channel_id=1, replica_groups=mesh['z0'=2,'y2'=2,'y1'=2,'y0'=2,'x'=4,'z2'=2,'z1'=2,'c'=2] {'y2','y1','x'}, dimensions={0} | all-to-all | bytes 131072 | tf_op jit(solution)/shard_map/all_to_all | solution.py:266
  79.5 2.5 %shard_map.66 = (bf16[384,896]{1,0:T(8,128)(2,1)}, bf16[384,384]{1,0:T(8,128)(2,1)S(1)}, bf16[384,384]{1,0:T(8,128)(2,1)S(1)}, f32[8,128]{1,0:T(8,128)S(1)}) custom-call(f32[1]{0:T(128)S(6)} %copy.6.factor_ref, bf16[384,768]{1,0:T(8,128)(2,1)S(1)} %bitcast.12, bf16[384,768]{1,0:T(8,128)(2,1)S(1)} %bitcast.18, ...), custom_call_target="tpu_custom_call" | custom-call | flops 905969664 | bytes 3182596 | tf_op jit(solution)/shard_map/pallas_call | solution.py:41
  82.0 4.8 %all-to-all-start.4 = ((bf16[4,96,896]{2,1,0:T(8,128)(2,1)}), bf16[4,96,896]{2,1,0:T(8,128)(2,1)S(1)}, u32[]{:S(2)}, u32[]{:S(2)}) async-start(bf16[4,96,896]{2,1,0:T(8,128)(2,1)} %bitcast.6), calls=%async_computation.4 | async-start | bytes 1376256 | tf_op jit(solution)/shard_map/all_to_all | solution.py:266
  86.8 0.5 shard_map.68
  87.3 1.9 %collective-permute-start.4 = (bf16[384,896]{1,0:T(8,128)(2,1)S(1)}, bf16[384,896]{1,0:T(8,128)(2,1)S(1)}, u32[]{:S(2)}, u32[]{:S(2)}) collective-permute-start(bf16[384,896]{1,0:T(8,128)(2,1)S(1)} %shard_map.68), channel_id=1, source_target_pairs={{0,1},{1,0},{2,3},{3,2},{4,5},{5,4},{6,7},{7,6},{8,9},{9,8},{10,11... | collective-permute-start | bytes 2064392 | tf_op jit(solution)/shard_map/ppermute | solution.py:270
  89.2 0.5 shard_map.67.own_ref
  89.7 1.6 %collective-permute-done.4.theirs_ref = bf16[384,896]{1,0:T(8,128)(2,1)S(1)} collective-permute-done((bf16[384,896]{1,0:T(8,128)(2,1)S(1)}, bf16[384,896]{1,0:T(8,128)(2,1)S(1)}, u32[]{:S(2)}, u32[]{:S(2)}) %collective-permute-start.4) | collective-permute-done | bytes 688160 | tf_op jit(solution)/shard_map/ppermute | solution.py:270
  91.3 1.0 shard_map.69
  92.4 1.3 %all-to-all-done.4 = bf16[4,96,896]{2,1,0:T(8,128)(2,1)S(1)} async-done(((bf16[4,96,896]{2,1,0:T(8,128)(2,1)}), bf16[4,96,896]{2,1,0:T(8,128)(2,1)S(1)}, u32[]{:S(2)}, u32[]{:S(2)}) %all-to-all-start.4) | async-done | bytes 688160 | tf_op jit(solution)/shard_map/all_to_all | solution.py:266
  93.7 3.6 %all-to-all-start.5 = ((bf16[16,24,768]{2,1,0:T(8,128)(2,1)}), bf16[16,24,768]{2,1,0:T(8,128)(2,1)S(1)}, u32[]{:S(2)}, u32[]{:S(2)}) async-start(bf16[16,24,768]{2,1,0:T(8,128)(2,1)} %bitcast.8), calls=%async_computation.5 | async-start | bytes 1179648 | tf_op jit(solution)/shard_map/all_to_all | solution.py:266
  97.3 0.2 shard_map.70
  97.4 2.6 %collective-permute-start.5 = (bf16[48,896]{1,0:T(8,128)(2,1)S(1)}, bf16[48,896]{1,0:T(8,128)(2,1)S(1)}, u32[]{:S(2)}, u32[]{:S(2)}) collective-permute-start(bf16[48,896]{1,0:T(8,128)(2,1)S(1)} %get-tuple-element.34), channel_id=1, source_target_pairs={{0,6},{2,4},{4,2},{6,0},{1,7},{3,5},{5,3},{7,1},{8,14},{10,12},{12... | collective-permute-start | bytes 258056 | tf_op jit(solution)/shard_map/ppermute | solution.py:270
  100.1 6.0 %collective-permute-done.5.theirs_ref = bf16[48,896]{1,0:T(8,128)(2,1)S(1)} collective-permute-done((bf16[48,896]{1,0:T(8,128)(2,1)S(1)}, bf16[48,896]{1,0:T(8,128)(2,1)S(1)}, u32[]{:S(2)}, u32[]{:S(2)}) %collective-permute-start.5) | collective-permute-done | bytes 86048 | tf_op jit(solution)/shard_map/ppermute | solution.py:270
  106.0 0.1 shard_map.71
  106.1 3.4 %collective-permute-start.6 = (bf16[24,896]{1,0:T(8,128)(2,1)S(1)}, bf16[24,896]{1,0:T(8,128)(2,1)S(1)}, u32[]{:S(2)}, u32[]{:S(2)}) collective-permute-start(bf16[24,896]{1,0:T(8,128)(2,1)S(1)} %get-tuple-element.37), channel_id=1, source_target_pairs={{0,2},{2,0},{4,6},{6,4},{1,3},{3,1},{5,7},{7,5},{8,10},{10,8},{12,... | collective-permute-start | bytes 129032 | tf_op jit(solution)/shard_map/ppermute | solution.py:270
  109.5 3.9 %collective-permute-done.6.theirs_ref = bf16[24,896]{1,0:T(8,128)(2,1)S(1)} collective-permute-done((bf16[24,896]{1,0:T(8,128)(2,1)S(1)}, bf16[24,896]{1,0:T(8,128)(2,1)S(1)}, u32[]{:S(2)}, u32[]{:S(2)}) %collective-permute-start.6) | collective-permute-done | bytes 43040 | tf_op jit(solution)/shard_map/ppermute | solution.py:270
  113.4 0.8 shard_map.72
  114.2 1.8 %all-to-all-done.5 = bf16[16,24,768]{2,1,0:T(8,128)(2,1)S(1)} async-done(((bf16[16,24,768]{2,1,0:T(8,128)(2,1)}), bf16[16,24,768]{2,1,0:T(8,128)(2,1)S(1)}, u32[]{:S(2)}, u32[]{:S(2)}) %all-to-all-start.5) | async-done | bytes 589856 | tf_op jit(solution)/shard_map/all_to_all | solution.py:266
  116.0 0.8 shard_map.73
  (2 shorter events, 0.0 us)
Async XLA Ops:
  0.6 0.9 copy-start
  1.5 9.7 %copy-start.1 = (f32[24,768]{1,0:T(8,128)S(1)}, f32[24,768]{1,0:T(8,128)}, u32[]{:S(2)}) copy-start(f32[24,768]{1,0:T(8,128)} %values_ref.7) | copy-start | bytes 221188
  1.5 9.7 %copy-start.2 = (f32[24,768]{1,0:T(8,128)S(1)}, f32[24,768]{1,0:T(8,128)}, u32[]{:S(2)}) copy-start(f32[24,768]{1,0:T(8,128)} %paired_ref.3) | copy-start | bytes 221188
  2.5 30.1 %all-to-all-start = ((bf16[16,24,768]{2,1,0:T(8,128)(2,1)}), bf16[16,24,768]{2,1,0:T(8,128)(2,1)S(1)}, u32[]{:S(2)}, u32[]{:S(2)}) async-start(bf16[16,24,768]{2,1,0:T(8,128)(2,1)} %bitcast.2), calls=%async_computation | async-start | bytes 1179648 | tf_op jit(solution)/shard_map/all_to_all | solution.py:266
  11.5 8.0 %collective-permute-start = (bf16[24,768]{1,0:T(8,128)(2,1)S(1)}, bf16[24,768]{1,0:T(8,128)(2,1)S(1)}, u32[]{:S(2)}, u32[]{:S(2)}) collective-permute-start(bf16[24,768]{1,0:T(8,128)(2,1)S(1)} %get-tuple-element.23.mine_ref), channel_id=1, source_target_pairs={{0,2},{2,0},{4,6},{6,4},{1,3},{3,1},{5,7},{7,5},{8,10},{10,8},{12,... | collective-permute-start | bytes 110600 | tf_op jit(solution)/shard_map/ppermute | solution.py:270
  19.5 12.1 %collective-permute-start.1 = (bf16[48,768]{1,0:T(8,128)(2,1)S(1)}, bf16[48,768]{1,0:T(8,128)(2,1)S(1)}, u32[]{:S(2)}, u32[]{:S(2)}) collective-permute-start(bf16[48,768]{1,0:T(8,128)(2,1)S(1)} %shard_map.59.mine_ref), channel_id=1, source_target_pairs={{0,6},{2,4},{4,2},{6,0},{1,7},{3,5},{5,3},{7,1},{8,14},{10,12},{12... | collective-permute-start | bytes 221192 | tf_op jit(solution)/shard_map/ppermute | solution.py:270
  32.5 11.9 %all-to-all-start.1 = ((bf16[4,96,768]{2,1,0:T(8,128)(2,1)}), bf16[4,96,768]{2,1,0:T(8,128)(2,1)S(1)}, u32[]{:S(2)}, u32[]{:S(2)}) async-start(bf16[4,96,768]{2,1,0:T(8,128)(2,1)} %bitcast.4), calls=%async_computation.1 | async-start | bytes 1179648 | tf_op jit(solution)/shard_map/all_to_all | solution.py:266
  37.5 3.9 %collective-permute-start.2 = (bf16[384,768]{1,0:T(8,128)(2,1)S(1)}, bf16[384,768]{1,0:T(8,128)(2,1)S(1)}, u32[]{:S(2)}, u32[]{:S(2)}) collective-permute-start(bf16[384,768]{1,0:T(8,128)(2,1)S(1)} %bitcast.15), channel_id=1, source_target_pairs={{0,1},{1,0},{2,3},{3,2},{4,5},{5,4},{6,7},{7,6},{8,9},{9,8},{10,11... | collective-permute-start | bytes 1769480 | tf_op jit(solution)/shard_map/ppermute | solution.py:270
  46.0 17.1 %all-to-all-start.2 = ((f32[16,8,128]{2,1,0:T(8,128)}), f32[16,8,128]{2,1,0:T(8,128)S(1)}, u32[]{:S(2)}, u32[]{:S(2)}) async-start(f32[16,8,128]{2,1,0:T(8,128)} %shard_map.62), calls=%async_computation.2 | async-start | bytes 131072 | tf_op jit(solution)/shard_map/all_to_all | solution.py:266
  56.3 3.1 %collective-permute-start.3 = (f32[8,128]{1,0:T(8,128)S(1)}, f32[8,128]{1,0:T(8,128)S(1)}, u32[]{:S(2)}, u32[]{:S(2)}) collective-permute-start(f32[8,128]{1,0:T(8,128)S(1)} %shard_map.63.mine_ref), channel_id=1, source_target_pairs={{0,1},{1,0},{2,3},{3,2},{4,5},{5,4},{6,7},{7,6},{8,9},{9,8},{10,11... | collective-permute-start | bytes 12296 | tf_op jit(solution)/shard_map/ppermute | solution.py:270
  82.0 11.7 %all-to-all-start.4 = ((bf16[4,96,896]{2,1,0:T(8,128)(2,1)}), bf16[4,96,896]{2,1,0:T(8,128)(2,1)S(1)}, u32[]{:S(2)}, u32[]{:S(2)}) async-start(bf16[4,96,896]{2,1,0:T(8,128)(2,1)} %bitcast.6), calls=%async_computation.4 | async-start | bytes 1376256 | tf_op jit(solution)/shard_map/all_to_all | solution.py:266
  87.3 4.0 %collective-permute-start.4 = (bf16[384,896]{1,0:T(8,128)(2,1)S(1)}, bf16[384,896]{1,0:T(8,128)(2,1)S(1)}, u32[]{:S(2)}, u32[]{:S(2)}) collective-permute-start(bf16[384,896]{1,0:T(8,128)(2,1)S(1)} %shard_map.68), channel_id=1, source_target_pairs={{0,1},{1,0},{2,3},{3,2},{4,5},{5,4},{6,7},{7,6},{8,9},{9,8},{10,11... | collective-permute-start | bytes 2064392 | tf_op jit(solution)/shard_map/ppermute | solution.py:270
  93.7 22.4 %all-to-all-start.5 = ((bf16[16,24,768]{2,1,0:T(8,128)(2,1)}), bf16[16,24,768]{2,1,0:T(8,128)(2,1)S(1)}, u32[]{:S(2)}, u32[]{:S(2)}) async-start(bf16[16,24,768]{2,1,0:T(8,128)(2,1)} %bitcast.8), calls=%async_computation.5 | async-start | bytes 1179648 | tf_op jit(solution)/shard_map/all_to_all | solution.py:266
  97.4 8.6 %collective-permute-start.5 = (bf16[48,896]{1,0:T(8,128)(2,1)S(1)}, bf16[48,896]{1,0:T(8,128)(2,1)S(1)}, u32[]{:S(2)}, u32[]{:S(2)}) collective-permute-start(bf16[48,896]{1,0:T(8,128)(2,1)S(1)} %get-tuple-element.34), channel_id=1, source_target_pairs={{0,6},{2,4},{4,2},{6,0},{1,7},{3,5},{5,3},{7,1},{8,14},{10,12},{12... | collective-permute-start | bytes 258056 | tf_op jit(solution)/shard_map/ppermute | solution.py:270
  106.1 7.3 %collective-permute-start.6 = (bf16[24,896]{1,0:T(8,128)(2,1)S(1)}, bf16[24,896]{1,0:T(8,128)(2,1)S(1)}, u32[]{:S(2)}, u32[]{:S(2)}) collective-permute-start(bf16[24,896]{1,0:T(8,128)(2,1)S(1)} %get-tuple-element.37), channel_id=1, source_target_pairs={{0,2},{2,0},{4,6},{6,4},{1,3},{3,1},{5,7},{7,5},{8,10},{10,8},{12,... | collective-permute-start | bytes 129032 | tf_op jit(solution)/shard_map/ppermute | solution.py:270
